TPU v7x, 32 devices: a whole 2x2x4 slice. The times are simulated.
32 devices in a mesh: dp: 4 (over z), ctx: 2 (over x), expert: 4 (over y, core).
Axes of the slice: x: 2, y: 2, z: 4, core: 2. Of those that a mesh axis runs over, the one named last changes fastest.
Arguments:
- layer_input: bfloat16 [16384, 1024], P(('dp', 'ctx', 'expert')), may hold values from -6 to 6
- attn_gain: float32 [1024], replicated, may hold values from 0.5 to 1.5
- qkv_weight: bfloat16 [1024, 3072], replicated, may hold values from -0.1875 to 0.1875
- out_weight: bfloat16 [1024, 1024], replicated, may hold values from -1.5 to 1.5
- bias_table: float32 [32, 16], P(None, 'expert'), may hold values from -4 to 4
- moe_gain: float32 [1024], replicated, may hold values from 0.5 to 1.5
- router_weight: bfloat16 [1024, 4], replicated, may hold values from -0.125 to 0.125
- expert_in: bfloat16 [4, 1024, 5632], P('expert'), may hold values from -0.1875 to 0.1875
- expert_down: bfloat16 [4, 2816, 1024], P('expert'), may hold values from -0.625 to 0.625
- expert_ids: int32 [16384, 2], P(('dp', 'ctx', 'expert')), may hold values from 0 to 3, all different within a row
- fill_order: int32 [32, 1024], P(('dp', 'ctx', 'expert')), may hold values from 0 to 1023, each once within a row
- block_ids: int32 [4, 4096], P('dp'), may hold values from 0 to 15, never falling along the last dimension, each value on 1 to 512 neighbouring positions
- bucket_ids: int32 [8191], replicated, may hold values from 0 to 31
- cotangent: bfloat16 [16384, 1024], P(('dp', 'ctx', 'expert')), may hold values from -6 to 6
Outputs:
- layer_output: bfloat16 [16384, 1024], P(('dp', 'ctx', 'expert'))
- input_grad: float32 [16384, 1024], P(('dp', 'ctx', 'expert'))
- attn_gain_grad: float32 [1024], P(('dp', 'ctx', 'expert'))
- qkv_grad: float32 [1024, 3072], P(('dp', 'ctx', 'expert'))
- out_grad: float32 [1024, 1024], P(('dp', 'ctx', 'expert'))
- bias_grad: float32 [32, 16], P(('dp', 'ctx'), 'expert')
- moe_gain_grad: float32 [1024], P(('dp', 'ctx', 'expert'))
- router_grad: float32 [1024, 4], P(('dp', 'ctx', 'expert'))
- expert_in_grad: float32 [4, 1024, 5632], P('expert', ('dp', 'ctx'))
- expert_down_grad: float32 [4, 2816, 1024], P('expert', None, ('dp', 'ctx'))
Inputs may be any that keep to these rules, and one draw needn't show every extreme that they name: `expert_ids`: each token's 2 expert ids differ. `fill_order`: each row is a permutation of the numbers 0 to 1023. `block_ids`: along each sequence the block number never falls and each block holds 1 to 512 positions, one exactly 512.
All inputs are finite; a program needn't handle non-finite values.
Results may differ from a plain program's by a relative error of at most 0.029.
Values may be sent and summed in bfloat16 or wider, within the bound.
A program may use at most 640 MiB of HBM per device.

v0:
```python
import functools

import jax
import jax.numpy as jnp
from jax import lax
from jax.experimental import pallas as pl
from jax.experimental.pallas import tpu as pltpu
from jax.sharding import PartitionSpec as P


HEAD_DIM = 64
TOP = 2
LOG2E = 1.4426950408889634
SCALE = 0.125 * LOG2E
HIDE = -(2.0**100)
f32 = jnp.float32
bf16 = jnp.bfloat16
highest = lax.Precision.HIGHEST
NN = (((1,), (0,)), ((), ()))
NT = (((1,), (1,)), ((), ()))
TN = (((0,), (0,)), ((), ()))


def mm(left, right, dims):
    return lax.dot_general(left, right, dims, preferred_element_type=f32)


def cost(flops, bytes_accessed, transcendentals=0):
    return pl.CostEstimate(
        flops=int(flops), bytes_accessed=int(bytes_accessed), transcendentals=int(transcendentals)
    )


def fill_table(tab_ref, buck_ref, tb_ref, width, mul):
    buck = buck_ref[...]
    row = jnp.zeros(buck.shape, f32)
    for b in range(tab_ref.shape[0]):
        row = jnp.where(buck == b, tab_ref[b] * mul, row)
    for m in range(16):
        rolled = pltpu.roll(row, 8 * m, 1, stride=1, stride_axis=0)
        for c in range(width // 128 - 1):
            lo = width - 128 - 128 * c
            tb_ref[16 * c + m] = rolled[:, lo : lo + 128]


def bias_tile(tb_ref, start, rows, cols):
    parts = [
        tb_ref[pl.ds(start - 16 * c, rows // 8)].reshape(rows, 128) for c in range(cols // 128)
    ]
    return jnp.concatenate(parts, axis=1)


def attention_fwd_kernel(
    bk, order, nch_ref, tab_ref, buck_ref, kmask_ref, qmask_ref, q_ref, k_ref, v_ref,
    o_ref, lse_ref, kaug, vaug, tb,
):
    qi = pl.program_id(0)
    blocks, _, _, tok = k_ref.shape
    length = blocks * tok

    @pl.when(qi == 0)
    def _():
        fill_table(tab_ref, buck_ref, tb, 2 * length, LOG2E)
        first = lax.broadcasted_iota(jnp.int32, (16, length), 0) == 0
        vaug[HEAD_DIM:, :] = first.astype(f32).astype(bf16)
        for p in range(blocks):
            rows = slice(p * tok, (p + 1) * tok)
            kaug[rows, :] = jnp.concatenate([k_ref[order(p), 0].T, kmask_ref[rows, :]], axis=1)
            vaug[0:HEAD_DIM, rows] = v_ref[order(p), 0]

    qaug = jnp.concatenate([q_ref[0, 0], qmask_ref[...]], axis=0)
    base = (length - 128) // 8 - qi * (tok // 8)

    def step(j, carry):
        peak, acc = carry
        ks = pl.ds(pl.multiple_of(j * bk, bk), bk)
        scores = mm(kaug[ks, :], qaug, NN) * SCALE + bias_tile(tb, base + j * (bk // 8), bk, tok)
        now = jnp.maximum(peak, jnp.max(scores, axis=0, keepdims=True))
        weights = jnp.exp2(scores - now).astype(bf16)
        return now, acc * jnp.exp2(peak - now) + mm(vaug[:, ks], weights, NN)

    start = (jnp.full((1, tok), -1e37, f32), jnp.zeros((HEAD_DIM + 16, tok), f32))
    peak, acc = lax.fori_loop(0, nch_ref[qi], step, start)
    total = acc[HEAD_DIM : HEAD_DIM + 1]
    o_ref[0] = (acc[0:HEAD_DIM] / total).astype(bf16)
    lse_ref[0] = peak + jnp.log2(total)


def attention_fwd(order, chunks, table, buck, kmask, qmask, qkv, bk):
    blocks, _, dim, tok = qkv.shape
    length = blocks * tok
    return pl.pallas_call(
        functools.partial(attention_fwd_kernel, bk, order),
        grid_spec=pltpu.PrefetchScalarGridSpec(
            num_scalar_prefetch=2,
            grid=(blocks,),
            in_specs=[
                pl.BlockSpec((8, 2 * length), lambda i, *_: (0, 0)),
                pl.BlockSpec((length, 64), lambda i, *_: (0, 0)),
                pl.BlockSpec((64, tok), lambda i, *_: (0, i)),
                pl.BlockSpec((1, 1, dim, tok), lambda i, *_: (order(i), 0, 0, 0)),
                pl.BlockSpec((blocks, 1, dim, tok), lambda i, *_: (0, 1, 0, 0)),
                pl.BlockSpec((blocks, 1, dim, tok), lambda i, *_: (0, 2, 0, 0)),
            ],
            out_specs=[
                pl.BlockSpec((1, dim, tok), lambda i, *_: (order(i), 0, 0)),
                pl.BlockSpec((1, 1, tok), lambda i, *_: (i, 0, 0)),
            ],
            scratch_shapes=[
                pltpu.VMEM((length, 128), bf16),
                pltpu.VMEM((dim + 16, length), bf16),
                pltpu.VMEM((2 * length // 8 - 16, 8, 128), f32),
            ],
        ),
        out_shape=[
            jax.ShapeDtypeStruct((blocks, dim, tok), bf16),
            jax.ShapeDtypeStruct((blocks, 1, tok), f32),
        ],
        compiler_params=pltpu.CompilerParams(vmem_limit_bytes=48 << 20),
        cost_estimate=cost(2000 * length * length // 2, 4 * length * 2 * dim, length * length // 2),
        name="attention_fwd",
    )(chunks, table, buck, kmask, qmask, qkv, qkv, qkv)


def three_rows(values, rows):
    high = values.astype(bf16).astype(f32)
    mid = (values - high).astype(bf16).astype(f32)
    row = lax.broadcasted_iota(jnp.int32, (rows, values.shape[1]), 0)
    out = jnp.where(row == 0, high, jnp.where(row == 1, mid, jnp.where(row == 2, values - high - mid, 0.0)))
    return out.astype(bf16)


def attention_bwd_kernel(
    bk, order, nch_ref, tab_ref, buck_ref, kmask_ref, qmask_ref, q_ref, k_ref, v_ref, o_ref,
    do_ref, lse_ref, out_ref, off_ref, knat, kaug, vaug, tb, gb, dkacc, dvacc,
):
    qi = pl.program_id(0)
    blocks, _, _, tok = k_ref.shape
    length = blocks * tok

    @pl.when(qi == 0)
    def _():
        fill_table(tab_ref, buck_ref, tb, 2 * length, LOG2E)
        gb[...] = jnp.zeros_like(gb)
        dkacc[...] = jnp.zeros_like(dkacc)
        dvacc[...] = jnp.zeros_like(dvacc)
        three = lax.broadcasted_iota(jnp.int32, (64, length), 0) < 3
        vaug[64:128, :] = three.astype(f32).astype(bf16)
        kaug[64:128, :] = kmask_ref[...]
        for p in range(blocks):
            rows = slice(p * tok, (p + 1) * tok)
            knat[rows, :] = k_ref[order(p), 0].T
            kaug[0:64, rows] = k_ref[order(p), 0]
            vaug[0:64, rows] = v_ref[order(p), 0]

    q_t = q_ref[0, 0]
    do_t = do_ref[0]
    delta = jnp.sum(do_t.astype(f32) * o_ref[0].astype(f32), axis=0, keepdims=True)
    lse = lse_ref[0] * (1.0 / SCALE)
    blank = jnp.zeros((32, tok), bf16)
    qaug = jnp.concatenate([q_t, qmask_ref[...], three_rows(-lse, 16), blank], axis=0).T
    doaug = jnp.concatenate([do_t, three_rows(-delta, 32), blank], axis=0).T
    base = (length - 128) // 8 + qi * (tok // 8)

    def step(j, dq):
        ks = pl.ds(pl.multiple_of(j * bk, bk), bk)
        start = base - j * (bk // 8)
        probs = jnp.exp2(mm(qaug, kaug[:, ks], NN) * SCALE + bias_tile(tb, start, tok, bk))
        ds = probs * mm(doaug, vaug[:, ks], NN)
        for c in range(bk // 128):
            at = pl.ds(start - 16 * c, tok // 8)
            gb[at] += ds[:, 128 * c : 128 * c + 128].reshape(tok // 8, 8, 128)
        low = ds.astype(bf16)
        dvacc[:, ks] += mm(do_t, probs.astype(bf16), NN)
        dkacc[:, ks] += mm(q_t, low, NN)
        return dq + mm(low, knat[ks, :], NN)

    dq = lax.fori_loop(0, nch_ref[qi], step, jnp.zeros((tok, 64), f32))
    out_ref[order(qi), 0] = (dq * 0.125).T.astype(bf16)

    @pl.when(qi == blocks - 1)
    def _():
        for p in range(blocks):
            rows = slice(p * tok, (p + 1) * tok)
            out_ref[order(p), 1] = (dkacc[:, rows] * 0.125).astype(bf16)
            out_ref[order(p), 2] = dvacc[:, rows].astype(bf16)
        width = 2 * length
        total = jnp.zeros((8, width), f32)
        for m in range(16):
            tiles = [gb[16 * c + m] for c in range(width // 128 - 2, -1, -1)]
            skewed = jnp.concatenate([jnp.zeros((8, 128), f32)] + tiles, axis=1)
            total = total + (pltpu.roll(skewed, width - 8 * m, 1) if m else skewed)
        row = total[0:1]
        for s in range(1, 8):
            row = row + pltpu.roll(total[s : s + 1], width - s, 1)
        buck = buck_ref[0:1, :]
        for b in range(off_ref.shape[0]):
            mine = jnp.where(buck == b, row, 0.0)
            parts = [mine[:, 128 * c : 128 * c + 128] for c in range(width // 128)]
            while len(parts) > 1:
                parts = [x + y for x, y in zip(parts[::2], parts[1::2])]
            off_ref[b : b + 1, :] = parts[0]


def attention_bwd(order, chunks, table, buck, kmask, qmask, qkv, mixed, mixed_grad, lse, bk):
    blocks, _, dim, tok = qkv.shape
    length = blocks * tok
    one = pl.BlockSpec((1, dim, tok), lambda i, *_: (order(i), 0, 0))
    return pl.pallas_call(
        functools.partial(attention_bwd_kernel, bk, order),
        grid_spec=pltpu.PrefetchScalarGridSpec(
            num_scalar_prefetch=2,
            grid=(blocks,),
            in_specs=[
                pl.BlockSpec((8, 2 * length), lambda i, *_: (0, 0)),
                pl.BlockSpec((64, length), lambda i, *_: (0, 0)),
                pl.BlockSpec((16, tok), lambda i, *_: (0, i)),
                pl.BlockSpec((1, 1, dim, tok), lambda i, *_: (order(i), 0, 0, 0)),
                pl.BlockSpec((blocks, 1, dim, tok), lambda i, *_: (0, 1, 0, 0)),
                pl.BlockSpec((blocks, 1, dim, tok), lambda i, *_: (0, 2, 0, 0)),
                one,
                one,
                pl.BlockSpec((1, 1, tok), lambda i, *_: (i, 0, 0)),
            ],
            out_specs=[
                pl.BlockSpec((blocks, 3, dim, tok), lambda i, *_: (0, 0, 0, 0)),
                pl.BlockSpec((table.shape[0], 128), lambda i, *_: (0, 0)),
            ],
            scratch_shapes=[
                pltpu.VMEM((length, dim), bf16),
                pltpu.VMEM((128, length), bf16),
                pltpu.VMEM((128, length), bf16),
                pltpu.VMEM((2 * length // 8 - 16, 8, 128), f32),
                pltpu.VMEM((2 * length // 8 - 16, 8, 128), f32),
                pltpu.VMEM((dim, length), f32),
                pltpu.VMEM((dim, length), f32),
            ],
        ),
        out_shape=[
            jax.ShapeDtypeStruct((blocks, 3, dim, tok), bf16),
            jax.ShapeDtypeStruct((table.shape[0], 128), f32),
        ],
        compiler_params=pltpu.CompilerParams(vmem_limit_bytes=48 << 20),
        cost_estimate=cost(5000 * length * length // 2, 8 * length * 2 * dim, length * length // 2),
        name="attention_bwd",
    )(chunks, table, buck, kmask, qmask, qkv, qkv, qkv, mixed, mixed_grad, lse)


def write_groups(acc, refs):
    rows = refs[0].shape[0]
    for d, ref in enumerate(refs):
        ref[...] = acc[d * rows : (d + 1) * rows, :].astype(bf16)


def expert_fwd_kernel(
    steps, x_ref, wg_ref, wu_ref, wd_ref, h_ref, act_ref, slope_ref, *refs
):
    outs, acc = refs[:-1], refs[-1]
    f = pl.program_id(0)

    @pl.when(f == 0)
    def _():
        acc[...] = jnp.zeros_like(acc)

    x = x_ref[...]
    gate = mm(x, wg_ref[0], NN)
    up = mm(x, wu_ref[0], NN)
    square = gate * gate
    t = jnp.tanh(gate * (0.7978845608028654 + 0.035677408136300125 * square))
    half = 0.5 + 0.5 * t
    act = gate * half
    slope = half + (gate * (0.5 - 0.5 * t * t)) * (
        0.7978845608028654 + 0.10703222440890037 * square
    )
    hidden = (act * up).astype(bf16)
    h_ref[...] = hidden
    act_ref[...] = act.astype(bf16)
    slope_ref[...] = (slope * up).astype(bf16)
    acc[...] += mm(hidden, wd_ref[0], NN)

    @pl.when(f == steps - 1)
    def _():
        write_groups(acc, outs)


def expert_fwd(x, w_in, w_down, groups, tile=256):
    rows, width = x.shape
    ff = w_down.shape[1]
    steps = ff // tile
    whole = pl.BlockSpec((rows, width), lambda f: (0, 0))
    part = pl.BlockSpec((rows, tile), lambda f: (0, f))
    inner = jax.ShapeDtypeStruct((rows, ff), bf16)
    one = pl.BlockSpec((rows // groups, width), lambda f: (0, 0))
    return pl.pallas_call(
        functools.partial(expert_fwd_kernel, steps),
        grid=(steps,),
        in_specs=[
            whole,
            pl.BlockSpec((1, width, tile), lambda f: (0, 0, f)),
            pl.BlockSpec((1, width, tile), lambda f: (0, 0, f + steps)),
            pl.BlockSpec((1, tile, width), lambda f: (0, f, 0)),
        ],
        out_specs=[part, part, part] + [one] * groups,
        out_shape=[inner, inner, inner]
        + [jax.ShapeDtypeStruct((rows // groups, width), bf16)] * groups,
        scratch_shapes=[pltpu.VMEM((rows, width), f32)],
        compiler_params=pltpu.CompilerParams(vmem_limit_bytes=48 << 20),
        cost_estimate=cost(
            10 * rows * width * ff, 6 * width * ff + rows * (4 * width + 6 * ff), rows * ff
        ),
        name="expert_fwd",
    )(x, w_in, w_in, w_down)


def expert_bwd_kernel(
    steps, g_ref, gate_ref, act_ref, slope_ref, wg_ref, wu_ref, wd_ref,
    grads_ref, *refs,
):
    outs, pg, acc = refs[:-2], refs[-2], refs[-1]
    f = pl.program_id(0)

    @pl.when(f == 0)
    def _():
        pg[...] = (g_ref[...].astype(f32) * gate_ref[...]).astype(bf16)
        acc[...] = jnp.zeros_like(acc)

    hidden_grad = mm(pg[...], wd_ref[0], NT)
    dg = (slope_ref[...].astype(f32) * hidden_grad).astype(bf16)
    du = (act_ref[...].astype(f32) * hidden_grad).astype(bf16)
    grads_ref[0] = dg
    grads_ref[1] = du
    acc[...] += mm(dg, wg_ref[0], NT) + mm(du, wu_ref[0], NT)

    @pl.when(f == steps - 1)
    def _():
        write_groups(acc, outs)


def expert_bwd(g, gate, act, slope, w_in, w_down, groups, tile=256):
    rows, width = g.shape
    ff = w_down.shape[1]
    steps = ff // tile
    whole = pl.BlockSpec((rows, width), lambda f: (0, 0))
    part = pl.BlockSpec((rows, tile), lambda f: (0, f))
    one = pl.BlockSpec((rows // groups, width), lambda f: (0, 0))
    return pl.pallas_call(
        functools.partial(expert_bwd_kernel, steps),
        grid=(steps,),
        in_specs=[
            whole,
            pl.BlockSpec((rows, 1), lambda f: (0, 0)),
            part,
            part,
            pl.BlockSpec((1, width, tile), lambda f: (0, 0, f)),
            pl.BlockSpec((1, width, tile), lambda f: (0, 0, f + steps)),
            pl.BlockSpec((1, tile, width), lambda f: (0, f, 0)),
        ],
        out_specs=[pl.BlockSpec((2, rows, tile), lambda f: (0, 0, f))] + [one] * groups,
        out_shape=[jax.ShapeDtypeStruct((2, rows, ff), bf16)]
        + [jax.ShapeDtypeStruct((rows // groups, width), bf16)] * groups,
        scratch_shapes=[pltpu.VMEM((rows, width), bf16), pltpu.VMEM((rows, width), f32)],
        compiler_params=pltpu.CompilerParams(vmem_limit_bytes=48 << 20),
        cost_estimate=cost(
            10 * rows * width * ff, 6 * width * ff + rows * (4 * width + 8 * ff)
        ),
        name="expert_bwd",
    )(g, gate, act, slope, w_in, w_in, w_down)


def column_block(ref, copies, ctx, flip, a):
    blk = ref.shape[1] // copies
    low = ref[:, 2 * a * blk : (2 * a + 1) * blk]
    high = ref[:, (2 * a + 1) * blk : (2 * a + 2) * blk]
    return jnp.where(lax.rem(ctx + flip, 2) == 0, low, high)


def in_grad_kernel(copies, ctx_ref, *refs):
    n = (len(refs) - 3) // 2
    xs, gs = refs[:n], refs[n : 2 * n]
    own_ref, other_ref, xt = refs[2 * n :]
    width = xs[0].shape[1]
    blk = width // copies

    @pl.when(pl.program_id(0) == 0)
    def _():
        at = 0
        for x_ref in xs:
            rows = x_ref.shape[0]
            for flip in range(2):
                for a in range(copies // 2):
                    to = (flip * (copies // 2) + a) * blk
                    xt[to : to + blk, at : at + rows] = column_block(
                        x_ref, copies, ctx_ref[0], flip, a
                    ).T
            at += rows

    grads = jnp.concatenate([g[0] for g in gs], axis=0)
    grad = mm(xt[...], grads, NN).astype(bf16)
    own_ref[...] = grad[: width // 2]
    other_ref[...] = grad[width // 2 :]


def in_grad(ctx, xs, grads, copies, first, count, tile=256):
    width = xs[0].shape[1]
    steps = grads[0].shape[2] // tile
    total = sum(x.shape[0] for x in xs)
    half = jax.ShapeDtypeStruct((width // 2, count * tile), bf16)
    out = pl.BlockSpec((width // 2, tile), lambda f, c: (0, f))

    def at(f, c):
        return ((f + first) // steps, 0, (f + first) % steps)

    return pl.pallas_call(
        functools.partial(in_grad_kernel, copies),
        grid_spec=pltpu.PrefetchScalarGridSpec(
            num_scalar_prefetch=1,
            grid=(count,),
            in_specs=[pl.BlockSpec(x.shape, lambda f, c: (0, 0)) for x in xs]
            + [pl.BlockSpec((1, g.shape[1], tile), at) for g in grads],
            out_specs=[out, out],
            scratch_shapes=[pltpu.VMEM((width, total), bf16)],
        ),
        out_shape=[half, half],
        compiler_params=pltpu.CompilerParams(vmem_limit_bytes=48 << 20),
        cost_estimate=cost(
            4 * total * width * count * tile, 2 * (total + width) * count * tile + 2 * total * width
        ),
        name="in_grad",
    )(ctx, *xs, *grads)


def down_grad_kernel(copies, ctx_ref, *refs):
    n = (len(refs) - 3) // 3
    hs, ps, gates = refs[:n], refs[n : 2 * n], refs[2 * n : 3 * n]
    own_ref, other_ref, pg = refs[3 * n :]
    blk = ps[0].shape[1] // copies

    @pl.when(pl.program_id(0) == 0)
    def _():
        at = 0
        for p_ref, gate_ref in zip(ps, gates):
            rows = p_ref.shape[0]
            for flip in range(2):
                for a in range(copies // 2):
                    to = (flip * (copies // 2) + a) * blk
                    block = column_block(p_ref, copies, ctx_ref[0], flip, a).astype(f32)
                    pg[at : at + rows, to : to + blk] = (block * gate_ref[...]).astype(bf16)
            at += rows

    grad = mm(jnp.concatenate([h[...] for h in hs], axis=0), pg[...], TN).astype(bf16)
    for a in range(copies // 2):
        own_ref[a] = grad[:, a * blk : (a + 1) * blk]
        to = (copies // 2 + a) * blk
        other_ref[a] = grad[:, to : to + blk]


def down_grad(ctx, hs, ps, gates, copies, first, count, tile=256):
    ff = count * tile
    width = ps[0].shape[1]
    total = sum(h.shape[0] for h in hs)
    blk = width // copies
    half = jax.ShapeDtypeStruct((copies // 2, ff, blk), bf16)
    out = pl.BlockSpec((copies // 2, tile, blk), lambda f, c: (0, f, 0))
    return pl.pallas_call(
        functools.partial(down_grad_kernel, copies),
        grid_spec=pltpu.PrefetchScalarGridSpec(
            num_scalar_prefetch=1,
            grid=(count,),
            in_specs=[pl.BlockSpec((h.shape[0], tile), lambda f, c: (0, f + first)) for h in hs]
            + [pl.BlockSpec(p.shape, lambda f, c: (0, 0)) for p in ps]
            + [pl.BlockSpec(g.shape, lambda f, c: (0, 0)) for g in gates],
            out_specs=[out, out],
            scratch_shapes=[pltpu.VMEM((total, width), bf16)],
        ),
        out_shape=[half, half],
        compiler_params=pltpu.CompilerParams(vmem_limit_bytes=48 << 20),
        cost_estimate=cost(4 * total * width * ff, 2 * (total * (width + ff) + width * ff)),
        name="down_grad",
    )(ctx, *hs, *ps, *gates)


def project_kernel(x_ref, gain_ref, w_ref, normed_ref, *refs):
    outs, normed_t = refs[:-1], refs[-1]
    heads = len(outs)

    @pl.when((pl.program_id(0) == 0) & (pl.program_id(1) == 0))
    def _():
        x = x_ref[...].astype(f32)
        scale = lax.rsqrt(jnp.mean(x * x, axis=1, keepdims=True) + 1e-06)
        normed = (x * scale * gain_ref[...]).astype(bf16)
        normed_ref[...] = normed
        normed_t[...] = normed.T

    cols = w_ref.shape[1]
    tok = normed_t.shape[1]
    rows = mm(w_ref[...], normed_t[...], TN).astype(bf16)
    rows = rows.reshape(cols // (heads * HEAD_DIM), heads, HEAD_DIM, tok)
    for h in range(heads):
        outs[h][:, 0] = rows[:, h]


def project(x, gain, weight, groups, heads, cols=512):
    tok, width = x.shape
    per = cols // (heads * HEAD_DIM)
    blocks = width // cols
    return pl.pallas_call(
        project_kernel,
        grid=(3, blocks),
        in_specs=[
            pl.BlockSpec((tok, width), lambda p, j: (0, 0)),
            pl.BlockSpec((1, width), lambda p, j: (0, 0)),
            pl.BlockSpec((width, cols), lambda p, j: (0, p * blocks + j)),
        ],
        out_specs=[pl.BlockSpec((tok, width), lambda p, j: (0, 0))]
        + [pl.BlockSpec((per, 1, HEAD_DIM, tok), lambda p, j: (j, p, 0, 0))] * heads,
        out_shape=[jax.ShapeDtypeStruct((tok, width), bf16)]
        + [jax.ShapeDtypeStruct((groups, 3, HEAD_DIM, tok), bf16)] * heads,
        scratch_shapes=[pltpu.VMEM((width, tok), bf16)],
        compiler_params=pltpu.CompilerParams(vmem_limit_bytes=48 << 20),
        cost_estimate=cost(6 * tok * width * width, 6 * width * width + 10 * tok * width),
        name="project",
    )(x, gain.reshape(1, width), weight)


def input_grad_kernel(steps, x_ref, gain_ref, mid_ref, w_ref, *refs):
    grads, out_ref, acc = refs[:-2], refs[-2], refs[-1]
    step = pl.program_id(0)
    cols = w_ref.shape[1]
    tok = out_ref.shape[0]

    @pl.when(step == 0)
    def _():
        acc[...] = jnp.zeros_like(acc)

    rows = jnp.stack([g[:, 0] for g in grads], axis=1).reshape(cols, tok)
    acc[...] += mm(w_ref[...], rows, NN)

    @pl.when(step == steps - 1)
    def _():
        x = x_ref[...].astype(f32)
        scale = lax.rsqrt(jnp.mean(x * x, axis=1, keepdims=True) + 1e-06)
        dy = acc[...].T * gain_ref[...]
        pull = jnp.mean(x * dy, axis=1, keepdims=True)
        out_ref[...] = mid_ref[...] + scale * dy - x * (scale * scale * scale * pull)


def input_gradient(x, gain, middle_grad, weight, grads, cols=512):
    tok, width = x.shape
    heads = len(grads)
    per = cols // (heads * HEAD_DIM)
    blocks = width // cols
    whole = pl.BlockSpec((tok, width), lambda s: (0, 0))
    return pl.pallas_call(
        functools.partial(input_grad_kernel, 3 * blocks),
        grid=(3 * blocks,),
        in_specs=[
            whole,
            pl.BlockSpec((1, width), lambda s: (0, 0)),
            whole,
            pl.BlockSpec((width, cols), lambda s: (0, s)),
        ]
        + [
            pl.BlockSpec((per, 1, HEAD_DIM, tok), lambda s: (s % blocks, s // blocks, 0, 0))
            for _ in grads
        ],
        out_specs=whole,
        out_shape=jax.ShapeDtypeStruct((tok, width), f32),
        scratch_shapes=[pltpu.VMEM((width, tok), f32)],
        compiler_params=pltpu.CompilerParams(vmem_limit_bytes=48 << 20),
        cost_estimate=cost(6 * tok * width * width, 6 * width * width + 16 * tok * width),
        name="input_grad",
    )(x, gain.reshape(1, width), middle_grad, weight, *grads)


def rms_scale(values, gain_vec):
    return values * lax.rsqrt(jnp.mean(values * values, axis=-1, keepdims=True) + 1e-06) * gain_vec


def dot_f32(left, right, left_dim, right_dim):
    return mm(left, right, (((left_dim,), (right_dim,)), ((), ())))


def swap_blocks(blocks, axes):
    return lax.all_to_all(blocks, axes, split_axis=0, concat_axis=0, tiled=True)


def exchange(parts):
    n = len(parts)
    return [parts[0]] + [
        lax.ppermute(parts[d], "expert", [(i, i ^ d) for i in range(n)]) for d in range(1, n)
    ]


def after(value, *others):
    return lax.optimization_barrier((value, others))[0]


def attention_plan(block_row, bucket_ids, blocks, tok):
    length = blocks * tok
    pad = jnp.full((1,), -1, jnp.int32)
    buck_rev = jnp.broadcast_to(jnp.concatenate([pad, bucket_ids[::-1]])[None], (8, 2 * length))
    buck = jnp.broadcast_to(jnp.concatenate([pad, bucket_ids])[None], (8, 2 * length))
    ids = jnp.arange(16)
    hot = (block_row[None, :] == ids[:, None]).astype(bf16)
    hide = jnp.where(ids[:, None] > block_row[None, :], HIDE, 0.0).astype(bf16)
    kmask_t = jnp.concatenate(
        [hot, jnp.ones((3, length), bf16), jnp.zeros((45, length), bf16)], axis=0
    )
    qmask = jnp.concatenate([hide, jnp.zeros((48, length), bf16)], axis=0)
    last = block_row.reshape(blocks, tok)[:, -1]
    seen = jnp.sum((block_row[None, :] <= last[:, None]).astype(jnp.int32), axis=1)
    return buck_rev, buck, kmask_t.T, kmask_t, qmask, hide, seen


def shards(
    layer_input,
    attn_gain,
    qkv_weight,
    out_weight,
    bias_table,
    moe_gain,
    router_weight,
    expert_in,
    expert_down,
    expert_ids,
    fill_order,
    block_ids,
    bucket_ids,
    cotangent,
):
    tok, width = layer_input.shape
    n_dp, n_ctx, n_exp = lax.axis_size("dp"), lax.axis_size("ctx"), lax.axis_size("expert")
    groups = n_ctx * n_exp
    copies = n_dp * n_ctx
    head_exp = bias_table.shape[1]
    heads = head_exp // n_ctx
    experts = router_weight.shape[1]
    ff_width = expert_down.shape[1]
    capacity = 5 * TOP * tok // (4 * experts)
    cut = (capacity // 2 + 15) // 16 * 16
    spans = ((0, cut), (cut, capacity))
    ctx_index = lax.axis_index("ctx")
    exp_index = lax.axis_index("expert")
    ctx_arg = ctx_index.astype(jnp.int32).reshape(1)
    pair = ("expert", "ctx")
    step_k = 512

    def order(p):
        return (p % n_exp) * n_ctx + p // n_exp

    def in_swap_order(blocks):
        shape = blocks.shape
        return jnp.swapaxes(blocks.reshape((n_ctx, n_exp) + shape[1:]), 0, 1).reshape(shape)

    inputs = layer_input.astype(f32)
    normed, *parts = project(layer_input, attn_gain, qkv_weight, groups, heads)
    qkv = [swap_blocks(part, pair) for part in parts]
    table_dev = lax.dynamic_slice_in_dim(bias_table, ctx_index * heads, heads, 1)
    buck_rev, buck, kmask, kmask_t, qmask, hide, seen = attention_plan(
        block_ids[0], bucket_ids, groups, tok
    )
    chunks = (seen + step_k - 1) // step_k

    flat_ids = expert_ids.reshape(TOP * tok)
    fill_rank = fill_order.reshape(TOP * tok)
    same_expert = flat_ids[:, None] == flat_ids[None, :]
    earlier = fill_rank[None, :] < fill_rank[:, None]
    slot_of = jnp.sum((same_expert & earlier).astype(jnp.int32), axis=1)
    slots = slot_of.reshape(tok, TOP)
    choose = (expert_ids[:, :, None] == jnp.arange(experts)[None, None, :]).astype(f32)

    expert_at = jnp.bitwise_xor(jnp.arange(experts), exp_index)

    def hits(d, low, high):
        slot_at = jnp.arange(low, high)[:, None]
        return [
            (expert_at[d] == expert_ids[None, :, j]) & (slot_at == slots[None, :, j])
            for j in range(TOP)
        ]

    pick = [
        [[one.astype(bf16) for one in hits(d, low, high)] for d in range(experts)]
        for low, high in spans
    ]

    def to_slots(rows, part):
        return [
            dot_f32(first + second, rows, 1, 0).astype(bf16) for first, second in pick[part]
        ]

    forward, mixed, normed_seq = [], [], []
    slots_a = to_slots(cotangent, 0)
    slots_b = to_slots(cotangent, 1)
    qkv[0], pick, slots_a, slots_b, buck_rev, buck, kmask, kmask_t, qmask, hide = (
        lax.optimization_barrier(
            (qkv[0], pick, slots_a, slots_b, buck_rev, buck, kmask, kmask_t, qmask, hide)
        )
    )
    part_width = width // heads
    for h in range(heads):
        arg = after(qkv[h], *forward, *normed_seq)
        piece = after(normed[:, h * part_width : (h + 1) * part_width], arg)
        normed_seq.append(lax.all_gather(piece, pair, axis=0, tiled=True))
        if h == heads - 1:
            grad_a = exchange(after(slots_a, arg))
        out = attention_fwd(order, chunks, table_dev[:, h], buck_rev, kmask, qmask, arg, step_k)
        if h == heads - 1:
            out = after(out, normed_seq, grad_a)
        forward.append(out)
        mixed.append(swap_blocks(out[0], pair).reshape(groups * HEAD_DIM, tok))
    out_heads = out_weight.reshape(groups, heads, HEAD_DIM, width)
    out_weights = [out_heads[:, h].reshape(groups * HEAD_DIM, width) for h in range(heads)]
    branch = sum(dot_f32(m, w, 0, 0) for m, w in zip(mixed, out_weights))
    middle = inputs + branch
    normed_moe_f, norm_moe_back = jax.vjp(rms_scale, middle, moe_gain)
    normed_moe = normed_moe_f.astype(bf16)

    arrived = [exchange(to_slots(normed_moe, 0))]
    arrived.append(exchange(to_slots(after(normed_moe, arrived[0][0]), 1)))
    logits = jnp.dot(normed_moe.astype(f32), router_weight.astype(f32), precision=highest)
    probs = jax.nn.softmax(logits, axis=-1)
    gate_vals = jnp.sum(probs[:, None, :] * choose, axis=2)
    gate_slots = [
        [
            jnp.sum(
                first.astype(f32) * gate_vals[None, :, 0]
                + second.astype(f32) * gate_vals[None, :, 1],
                axis=1,
            )
            for first, second in part
        ]
        for part in pick
    ]
    sent_gates = [jnp.concatenate(both) for both in zip(*gate_slots)]
    gates = jnp.stack(exchange(sent_gates))

    x_a, x_b = [jnp.concatenate(part, axis=0) for part in arrived]
    gate_rows = [gates[:, low:high].reshape(-1, 1) for low, high in spans]
    grad_b = exchange(after(slots_b, x_a))
    run_a = expert_fwd(x_a, expert_in, expert_down, experts)
    run_b = expert_fwd(after(x_b, run_a, grad_b), expert_in, expert_down, experts)
    produced_a = exchange(list(run_a[3:]))
    g_a, g_b = jnp.concatenate(grad_a, axis=0), jnp.concatenate(grad_b, axis=0)
    hidden = [run_a[0], run_b[0]]
    tiles = ff_width // 256
    cuts = (0, (tiles + 1) // 2, tiles)
    g_args = after([g_a, g_b], run_b, produced_a)
    down_1 = down_grad(ctx_arg, hidden, g_args, gate_rows, copies, 0, cuts[1])
    produced_b = exchange(list(run_b[3:]))

    def ctx_sum(own, other):
        came = lax.ppermute(other, "ctx", [(0, 1), (1, 0)])
        return (own.astype(f32) + came.astype(f32)).astype(bf16)

    halves = [ctx_sum(*down_1)]
    g_args = after([g_a, g_b], down_1)
    down_2 = down_grad(ctx_arg, hidden, g_args, gate_rows, copies, cuts[1], tiles - cuts[1])
    undo_a = expert_bwd(
        after(g_a, down_2), gate_rows[0], run_a[1], run_a[2], expert_in, expert_down, experts
    )
    halves.append(ctx_sum(down_2[0], after(down_2[1], halves[0])))
    undo_b = expert_bwd(
        after(g_b, undo_a, halves[0], produced_b),
        gate_rows[1], run_b[1], run_b[2], expert_in, expert_down, experts,
    )
    grads_a = exchange(list(undo_a[1:]))
    grads_in = [undo_a[0], undo_b[0]]
    bounds = (0, 2 * tiles * 4 // 11, 2 * tiles * 8 // 11, 2 * tiles)
    xs = after([x_a, x_b], undo_b, grads_a)
    in_1 = in_grad(ctx_arg, xs, grads_in, copies, bounds[0], bounds[1] - bounds[0])
    grads_b = exchange(list(undo_b[1:]))
    xs = after([x_a, x_b], in_1, halves[1])
    in_2 = in_grad(ctx_arg, xs, grads_in, copies, bounds[1], bounds[2] - bounds[1])
    halves.append(ctx_sum(in_1[0], after(in_1[1], halves[1])))
    xs = after([x_a, x_b], in_2)
    in_3 = in_grad(ctx_arg, xs, grads_in, copies, bounds[2], bounds[3] - bounds[2])
    produced = after([produced_a, produced_b], in_3)
    row_grad = after([grads_a, grads_b], in_3)

    def from_slots(picks, slot_rows):
        rows = jnp.concatenate([one for part in slot_rows for one in part], axis=0)
        return dot_f32(jnp.concatenate([one for part in picks for one in part], axis=0), rows, 0, 0)

    first_out = from_slots([[p[0] for p in part] for part in pick], produced)
    second_out = from_slots([[p[1] for p in part] for part in pick], produced)
    normed_moe_grad = from_slots([[p[0] + p[1] for p in part] for part in pick], row_grad)
    moe_sum = gate_vals[:, 0:1] * first_out + gate_vals[:, 1:2] * second_out
    layer_output = (middle + moe_sum).astype(bf16)
    grad_out = cotangent.astype(f32)
    gate_grad = jnp.stack(
        [jnp.sum(grad_out * first_out, axis=1), jnp.sum(grad_out * second_out, axis=1)], axis=1
    )
    probs_grad = jnp.sum(gate_grad[:, :, None] * choose, axis=1)
    logits_grad = probs * (probs_grad - jnp.sum(probs * probs_grad, axis=1, keepdims=True))
    router_f = router_weight.astype(f32)
    route_grad = jnp.dot(logits_grad, router_f.T, precision=highest)
    middle_norm_grad, moe_gain_grad = norm_moe_back(normed_moe_grad + route_grad)
    middle_grad = grad_out + middle_norm_grad
    branch_grad = middle_grad.astype(bf16)
    branch_grad = after(branch_grad, halves[2])
    mixed_grad = [
        swap_blocks(
            dot_f32(w, branch_grad, 1, 1).astype(bf16).reshape(groups, HEAD_DIM, tok), pair
        )
        for w in out_weights
    ]

    out_grad = jnp.stack(
        [dot_f32(m, branch_grad, 1, 0).astype(bf16).reshape(groups, HEAD_DIM, width) for m in mixed],
        axis=1,
    ).reshape(width, width)
    wide_logits = jnp.pad(logits_grad, ((0, 0), (0, 128 - experts)))
    router_grad = lax.dot_general(
        normed_moe.astype(f32), wide_logits, (((0,), (0,)), ((), ())), precision=highest
    )
    lane = jnp.arange(128)[None, :]
    small = jnp.where(lane == experts, moe_gain_grad[:, None], router_grad).astype(bf16)
    rows_dev = width // (n_dp * groups)
    early = jnp.concatenate([out_grad, small], axis=1)
    early = early.reshape(copies, n_exp, rows_dev, width + 128)

    def sum_dp(half):
        return lax.psum_scatter(half, "dp", scatter_dimension=0, tiled=True)

    summed = [sum_dp(halves[0]), sum_dp(halves[1])]
    last_own, last_other = [sum_dp(half) for half in in_3]

    buckets = bias_table.shape[0] // copies
    lanes = -(-(3 * HEAD_DIM + 1) // 128) * 128
    backward, grads, late = [], [], []
    for h in range(heads):
        arg = after(mixed_grad[h], backward, halves, summed)
        if h == 0:
            halves.append(ctx_sum(in_2[0], after(in_2[1], arg)))
            summed.append(sum_dp(halves[2]))
            pieces = after(early, arg)
            early_parts = exchange(
                [
                    lax.dynamic_index_in_dim(
                        pieces, jnp.bitwise_xor(exp_index, d), 1, False
                    ).reshape(-1, width + 128)
                    for d in range(n_exp)
                ]
            )
            early_sum = sum(part.astype(f32) for part in early_parts).astype(bf16)
            early_half = sum_dp(early_sum).reshape(n_ctx, rows_dev, width + 128)
        else:
            arg = after(arg, early_parts, last_own, last_other)
        out, offsets = attention_bwd(
            order, chunks, table_dev[:, h], buck, kmask_t, hide, qkv[h], forward[h][0],
            arg, forward[h][1], step_k,
        )
        if h == heads - 1:
            summed.append(sum_dp(after(halves[3], arg)))
            summed.append(ctx_sum(last_own, after(last_other, arg)))
            out, offsets = after((out, offsets), grads, late, early_half, summed[4])
        backward.append(out)
        grads.append(swap_blocks(out, pair))
        columns = jnp.transpose(out, (1, 2, 0, 3)).reshape(3 * HEAD_DIM, groups * tok)
        local_grad = jnp.concatenate(
            [dot_f32(piece, columns, 0, 1) for piece in normed_seq], axis=0
        )
        table_grad = jnp.sum(offsets, axis=1)
        spread = jnp.pad(
            jnp.broadcast_to(
                table_grad.reshape(n_dp, n_ctx, 1, buckets), (n_dp, n_ctx, n_exp, buckets)
            ),
            ((0, 0), (0, 0), (0, 0), (0, rows_dev - buckets)),
        ).reshape(width, 1)
        local_grad = jnp.pad(local_grad, ((0, 0), (0, lanes - 3 * HEAD_DIM)))
        lane = jnp.arange(lanes)[None, :]
        packed = jnp.where(lane == 3 * HEAD_DIM, spread, local_grad).astype(bf16)
        late.append(sum_dp(packed))
    input_grad = input_gradient(layer_input, attn_gain, middle_grad, qkv_weight, grads)
    early_own, early_other = [
        lax.dynamic_index_in_dim(early_half, at, 0, False) for at in (ctx_index, 1 - ctx_index)
    ]
    early_rows = early_own.astype(f32) + lax.ppermute(
        early_other, "ctx", [(0, 1), (1, 0)]
    ).astype(f32)
    expert_in_grad = jnp.concatenate(summed[2:], axis=1).astype(f32)
    expert_down_grad = jnp.concatenate(summed[:2], axis=1).astype(f32)
    rows_out = swap_blocks(
        in_swap_order(jnp.concatenate(late, axis=1).reshape(groups, rows_dev, -1)), pair
    )
    late_rows = jnp.swapaxes(rows_out.reshape(groups, rows_dev, heads, lanes), 1, 2)
    qkv_grad = (
        jnp.transpose(
            late_rows[..., : 3 * HEAD_DIM].reshape(groups, heads, rows_dev, 3, HEAD_DIM),
            (2, 3, 0, 1, 4),
        )
        .reshape(rows_dev, 3 * width)
        .astype(f32)
    )
    bias_rows = lax.dynamic_slice(
        late_rows[..., 3 * HEAD_DIM], (exp_index * n_ctx, 0, 0), (n_ctx, heads, buckets)
    )
    bias_grad = bias_rows.reshape(head_exp, buckets).T.astype(f32)
    my_rows = ((lax.axis_index("dp") * n_ctx + ctx_index) * n_exp + exp_index) * rows_dev
    attn_gain_grad = jnp.sum(
        lax.dynamic_slice_in_dim(qkv_weight, my_rows, rows_dev, 0).astype(f32) * qkv_grad, axis=1
    ) / lax.dynamic_slice_in_dim(attn_gain, my_rows, rows_dev, 0)
    return (
        layer_output,
        input_grad,
        attn_gain_grad,
        qkv_grad,
        early_rows[:, :width],
        bias_grad,
        early_rows[:, width + experts],
        early_rows[:, width : width + experts],
        expert_in_grad[None],
        expert_down_grad,
    )


def solution(mesh):
    rows = P(("dp", "ctx", "expert"), None)
    return jax.shard_map(
        shards,
        mesh=mesh,
        in_specs=(
            rows,
            P(),
            P(),
            P(),
            P(None, "expert"),
            P(),
            P(),
            P("expert", None, None),
            P("expert", None, None),
            rows,
            rows,
            P("dp", None),
            P(),
            rows,
        ),
        out_specs=(
            rows,
            rows,
            P(("dp", "ctx", "expert")),
            rows,
            rows,
            P(("dp", "ctx"), "expert"),
            P(("dp", "ctx", "expert")),
            rows,
            P("expert", ("dp", "ctx"), None),
            P("expert", None, ("dp", "ctx")),
        ),
        check_vma=False,
    )
```

profile of v0, /device:TPU:0, one launch (start us, length us, event | category | flops | bytes accessed | tf_op | source)
XLA Modules:
  0.0 697.1 jit_solution(7778601157798103251)
XLA Ops:
  9.1 8.4 %project.1 = (bf16[512,1024]{1,0:T(8,128)(2,1)S(1)}, bf16[8,3,64,512]{3,2,1,0:T(8,128)(2,1)}, bf16[8,3,64,512]{3,2,1,0:T(8,128)(2,1)S(1)}) custom-call(bf16[512,1024]{1,0:T(8,128)(2,1)S(1)} %copy-done.1, f32[1,1024]{1,0:T(1,128)S(1)} %bitcast.125, bf16[1024,3072]{1,0:T(8,128)(2,1)} %w_ref.3), custom_call_target="tpu_custom_call" | custom-call | flops 3221225472 | bytes 11534336 | tf_op jit(solution)/shard_map/project/pallas_call | solution.py:506
  18.6 5.3 all-to-all-start
  46.9 4.2 all-to-all-start.2
  57.5 29.6 %attention_fwd.2 = (bf16[8,64,512]{2,1,0:T(8,128)(2,1)S(1)}, f32[8,1,512]{2,1,0:T(1,128)S(1)}) custom-call(s32[8]{0:T(128)S(1)} %and_select_fusion.nch_ref, f32[32]{0:T(128)S(1)} %get-tuple-element.422.tab_ref, s32[8,8192]{1,0:T(8,128)S(1)} %broadcast_in_dim.114.buck_ref, bf16[4096,64]{1,0:T(8,128)(2,1)S(1)} %copy-done.16, bf16[64,4096]{1,0:T(8,128)(2,1)S(1)} %copy-done.20, ...), custom_call_target="tpu_custom_call" | custom-call | flops 16777216000 | bytes 2097152 | tf_op jit(solution)/shard_map/attention_fwd/pallas_call | solution.py:92
  88.6 8.5 %all-gather.3.cloned.1.call-done = bf16[4096,512]{1,0:T(8,128)(2,1)} async-done(((bf16[512,512]{1,0:T(8,128)(2,1)}), bf16[4096,512]{1,0:T(8,128)(2,1)}) %all-gather.3.cloned.1.call-update) | async-done | bytes 4194320 | tf_op jit(solution)/shard_map/all_gather | solution.py:703
  97.1 4.3 all-to-all-start.1
  104.6 6.5 all-to-all-done.1
  116.7 30.4 %attention_fwd.3 = (bf16[8,64,512]{2,1,0:T(8,128)(2,1)}, f32[8,1,512]{2,1,0:T(1,128)S(1)}) custom-call(s32[8]{0:T(128)S(1)} %and_select_fusion.nch_ref, f32[32]{0:T(128)S(1)} %get-tuple-element.421.tab_ref, s32[8,8192]{1,0:T(8,128)S(1)} %broadcast_in_dim.114.buck_ref, bf16[4096,64]{1,0:T(8,128)(2,1)S(1)} %copy-done.17, bf16[64,4096]{1,0:T(8,128)(2,1)S(1)} %copy-done.21, ...), custom_call_target="tpu_custom_call" | custom-call | flops 16777216000 | bytes 2097152 | tf_op jit(solution)/shard_map/attention_fwd/pallas_call | solution.py:92
  147.8 4.4 all-to-all-start.3
  157.3 4.2 all-to-all-done.3
  178.9 6.3 collective-permute-done.4
  185.2 5.7 collective-permute-done.5
  195.0 20.2 %expert_fwd.2 = (bf16[640,2816]{1,0:T(8,128)(2,1)S(1)}, bf16[640,2816]{1,0:T(8,128)(2,1)}, bf16[640,2816]{1,0:T(8,128)(2,1)}, bf16[160,1024]{1,0:T(8,128)(2,1)S(...) custom-call(bf16[640,1024]{1,0:T(8,128)(2,1)S(1)} %pad_maximum_fusion.2.x_ref.refs_0, ...), custom_call_target="tpu_custom_call" | custom-call | flops 18454937600 | bytes 30736384 | tf_op jit(solution)/shard_map/expert_fwd/pallas_call | solution.py:294
  220.9 20.4 %expert_fwd.3 = (bf16[640,2816]{1,0:T(8,128)(2,1)S(1)}, bf16[640,2816]{1,0:T(8,128)(2,1)}, bf16[640,2816]{1,0:T(8,128)(2,1)}, bf16[160,1024]{1,0:T(8,128)(2,1)S(...) custom-call(bf16[640,1024]{1,0:T(8,128)(2,1)S(1)} %pad_maximum_fusion.3.x_ref.refs_1_, ...), custom_call_target="tpu_custom_call" | custom-call | flops 18454937600 | bytes 30736384 | tf_op jit(solution)/shard_map/expert_fwd/pallas_call | solution.py:294
  245.3 9.4 %down_grad.2 = (bf16[4,1536,128]{2,1,0:T(8,128)(2,1)S(1)}, bf16[4,1536,128]{2,1,0:T(8,128)(2,1)}) custom-call(s32[1]{0:T(128)} %bitcast.17.ctx_ref, bf16[640,2816]{1,0:T(8,128)(2,1)} %copy-done.57, bf16[640,2816]{1,0:T(8,128)(2,1)} %copy-done.58, bf16[640,1024]{1,0:T(8,128)(2,1)S(1)} %copy-done.38, ...), custom_call_target="tpu_custom_call" | custom-call | flops 8053063680 | bytes 9699328 | tf_op jit(solution)/shard_map/down_grad/pallas_call | solution.py:464
  255.9 7.4 %down_grad.3 = (bf16[4,1280,128]{2,1,0:T(8,128)(2,1)S(1)}, bf16[4,1280,128]{2,1,0:T(8,128)(2,1)S(1)}) custom-call(s32[1]{0:T(128)} %bitcast.17.ctx_ref, bf16[640,2816]{1,0:T(8,128)(2,1)} %copy-done.57, bf16[640,2816]{1,0:T(8,128)(2,1)} %copy-done.58, bf16[640,1024]{1,0:T(8,128)(2,1)S(1)} %copy-done.38, ...), custom_call_target="tpu_custom_call" | custom-call | flops 6710886400 | bytes 8519680 | tf_op jit(solution)/shard_map/down_grad/pallas_call | solution.py:464
  264.4 24.7 %expert_bwd.2 = (bf16[2,640,2816]{2,1,0:T(8,128)(2,1)}, bf16[160,1024]{1,0:T(8,128)(2,1)S(1)}, bf16[160,1024]{1,0:T(8,128)(2,1)}, bf16[160,1024]{1,0:T(8,128)(2,1)}, bf16[160,1024]{1,0:T(8,128)(2,1)}) custom-call(bf16[640,1024]{1,0:T(8,128)(2,1)S(1)} %copy-done.38, f32[640,1]{1,0:T(8,128)S(1)} %reshape.324.refs_4_.gate_ref, ...), custom_call_target="tpu_custom_call" | custom-call | flops 18454937600 | bytes 34340864 | tf_op jit(solution)/shard_map/expert_bwd/pallas_call | solution.py:346
  295.9 24.3 %expert_bwd.3 = (bf16[2,640,2816]{2,1,0:T(8,128)(2,1)}, bf16[160,1024]{1,0:T(8,128)(2,1)S(1)}, bf16[160,1024]{1,0:T(8,128)(2,1)S(1)}, bf16[160,1024]{1,0:T(8,128)(2,1)S(1)}, bf16[160,1024]{1,0:T(8,128)(2,1)S(1)}) custom-call(bf16[640,1024]{1,0:T(8,128)(2,1)S(1)} %constant_dynamic-update-slice_fusion.8.refs_3_.g_ref, f32[640,1]{1,0:T(8,128)S(1)} %reshape.325.refs_5_.gate_ref, ...), custom_call_target="tpu_custom_call" | custom-call | flops 18454937600 | bytes 34340864 | tf_op jit(solution)/shard_map/expert_bwd/pallas_call | solution.py:346
  323.2 10.7 %in_grad.3 = (bf16[512,2048]{1,0:T(8,128)(2,1)S(1)}, bf16[512,2048]{1,0:T(8,128)(2,1)}) custom-call(s32[1]{0:T(128)} %bitcast.17.ctx_ref, bf16[640,1024]{1,0:T(8,128)(2,1)S(1)} %pad_maximum_fusion.2.x_ref.refs_0_, bf16[640,1024]{1,0:T(8,128)(2,1)S(1)} %copy-done.12, bf16[2,640,2816]{2,1,0:T(8,128)(2,1)} %get-tuple-element.213.refs_2_, ...), custom_call_target="tpu_custom_call" | custom-call | flops 10737418240 | bytes 12058624 | tf_op jit(solution)/shard_map/in_grad/pallas_call | solution.py:413
  336.4 47.4 %collective-permute-done.29 = bf16[512,2048]{1,0:T(8,128)(2,1)} collective-permute-done((bf16[512,2048]{1,0:T(8,128)(2,1)}, bf16[512,2048]{1,0:T(8,128)(2,1)}, u32[]{:S(2)}, u32[]{:S(2)}) %collective-permute-start.29) | collective-permute-done | bytes 2097184 | tf_op jit(solution)/shard_map/ppermute | solution.py:752
  396.5 10.6 %in_grad.4 = (bf16[512,2048]{1,0:T(8,128)(2,1)S(1)}, bf16[512,2048]{1,0:T(8,128)(2,1)}) custom-call(s32[1]{0:T(128)} %bitcast.17.ctx_ref, bf16[640,1024]{1,0:T(8,128)(2,1)S(1)} %pad_maximum_fusion.2.x_ref.refs_0_, bf16[640,1024]{1,0:T(8,128)(2,1)S(1)} %copy-done.13, bf16[2,640,2816]{2,1,0:T(8,128)(2,1)} %get-tuple-element.213.refs_2_, ...), custom_call_target="tpu_custom_call" | custom-call | flops 10737418240 | bytes 12058624 | tf_op jit(solution)/shard_map/in_grad/pallas_call | solution.py:413
  407.2 7.6 %in_grad.5 = (bf16[512,1536]{1,0:T(8,128)(2,1)S(1)}, bf16[512,1536]{1,0:T(8,128)(2,1)S(1)}) custom-call(s32[1]{0:T(128)} %bitcast.17.ctx_ref, bf16[640,1024]{1,0:T(8,128)(2,1)S(1)} %pad_maximum_fusion.2.x_ref.refs_0_, bf16[640,1024]{1,0:T(8,128)(2,1)S(1)} %copy-done.13, bf16[2,640,2816]{2,1,0:T(8,128)(2,1)} %get-tuple-element.213.refs_2_, ...), custom_call_target="tpu_custom_call" | custom-call | flops 8053063680 | bytes 9699328 | tf_op jit(solution)/shard_map/in_grad/pallas_call | solution.py:413
  432.6 4.4 fusion
  440.5 4.5 multiply_reduce_fusion
  445.0 4.3 fusion.70
  465.0 5.4 all-to-all-done.4.do_ref
  476.6 45.4 %attention_bwd.2 = (bf16[8,3,64,512]{3,2,1,0:T(8,128)(2,1)}, f32[32,128]{1,0:T(8,128)S(1)}) custom-call(s32[8]{0:T(128)S(1)} %copy-done.56, f32[32]{0:T(128)S(1)} %copy-done.47, s32[8,8192]{1,0:T(8,128)S(1)} %copy-done.35, bf16[64,4096]{1,0:T(8,128)(2,1)S(1)} %copy-done.24, bf16[16,4096]{1,0:T(8,128)(2,1)S(1)} %copy-done.27, ...), custom_call_target="tpu_custom_call" | custom-call | flops 41943040000 | bytes 4194304 | tf_op jit(solution)/shard_map/attention_bwd/pallas_call | solution.py:209
  558.5 46.4 %attention_bwd.3 = (bf16[8,3,64,512]{3,2,1,0:T(8,128)(2,1)}, f32[32,128]{1,0:T(8,128)S(1)}) custom-call(s32[8]{0:T(128)S(1)} %copy-done.56, f32[32]{0:T(128)S(1)} %copy-done.45, s32[8,8192]{1,0:T(8,128)S(1)} %copy-done.36, bf16[64,4096]{1,0:T(8,128)(2,1)S(1)} %copy-done.25, bf16[16,4096]{1,0:T(8,128)(2,1)S(1)} %copy-done.27, ...), custom_call_target="tpu_custom_call" | custom-call | flops 41943040000 | bytes 4194304 | tf_op jit(solution)/shard_map/attention_bwd/pallas_call | solution.py:209
  615.8 23.5 %reduce-scatter.24.cloned.1.call-done = bf16[256,256]{0,1:T(8,128)(2,1)} async-done(((bf16[1024,256]{0,1:T(8,128)(2,1)}), bf16[256,256]{0,1:T(8,128)(2,1)}) %reduce-scatter.24.cloned.1.call-update) | async-done | bytes 131088 | tf_op jit(solution)/shard_map/reduce_scatter | solution.py:823
  646.8 4.4 all-to-all-done.8
  651.1 3.9 all-to-all-start.7
  676.7 10.3 %input_grad.1 = f32[512,1024]{1,0:T(8,128)} custom-call(bf16[512,1024]{1,0:T(8,128)(2,1)S(1)} %copy-done.3, f32[1,1024]{1,0:T(1,128)S(1)} %bitcast.126, f32[512,1024]{1,0:T(8,128)} %get-tuple-element.365.mid_ref, bf16[1024,3072]{1,0:T(8,128)(2,1)} %w_ref.3, bf16[8,3,64,512]{3,2,1,0:T(8,128)(2,1)S(1)} %all-to-all-done.5.refs_0_, ...), custom_call_target="tpu_custom_call" | custom-call | flops 3221225472 | bytes 14680064 | tf_op jit(solution)/shard_map/input_grad/pallas_call | solution.py:553
  (576 shorter events, 228.0 us)
Async XLA Ops:
  23.9 73.1 %all-gather.3.cloned.1.call-start = ((), (), s32[]{:S(2)}) async-start(), calls=%async_computation.18 | async-start | bytes 4718592 | tf_op jit(solution)/shard_map/all_gather | solution.py:703
  46.9 41.7 %all-to-all-start.2 = ((bf16[8,3,64,512]{3,2,1,0:T(8,128)(2,1)}), bf16[8,3,64,512]{3,2,1,0:T(8,128)(2,1)S(1)}, u32[]{:S(2)}, u32[]{:S(2)}) async-start(bf16[8,3,64,512]{3,2,1,0:T(8,128)(2,1)} %copy-done.10), calls=%async_computation.2 | async-start | bytes 3145728 | tf_op jit(solution)/shard_map/all_to_all | solution.py:584
  51.1 96.7 %all-gather.5.cloned.1.call-start = ((), (), s32[]{:S(2)}) async-start(), calls=%async_computation.19 | async-start | bytes 4718592 | tf_op jit(solution)/shard_map/all_gather | solution.py:703
  114.6 33.2 %collective-permute-start = (bf16[160,1024]{1,0:T(8,128)(2,1)S(1)}, bf16[160,1024]{1,0:T(8,128)(2,1)}, u32[]{:S(2)}, u32[]{:S(2)}) collective-permute-start(bf16[160,1024]{1,0:T(8,128)(2,1)S(1)} %copy-done.147), channel_id=1, source_target_pairs={{0,1},{1,0},{2,3},{3,2},{4,5},{5,4},{6,7},{7,6},{8,9},{9,8},{10,11... | collective-permute-start | bytes 983048 | tf_op jit(solution)/shard_map/ppermute | solution.py:590
  115.2 32.6 %collective-permute-start.1 = (bf16[160,1024]{1,0:T(8,128)(2,1)S(1)}, bf16[160,1024]{1,0:T(8,128)(2,1)}, u32[]{:S(2)}, u32[]{:S(2)}) collective-permute-start(bf16[160,1024]{1,0:T(8,128)(2,1)S(1)} %copy-done.146), channel_id=1, source_target_pairs={{0,2},{1,3},{2,0},{3,1},{4,6},{5,7},{6,4},{7,5},{8,10},{9,11},{10,... | collective-permute-start | bytes 983048 | tf_op jit(solution)/shard_map/ppermute | solution.py:590
  116.7 31.1 %collective-permute-start.2 = (bf16[160,1024]{1,0:T(8,128)(2,1)S(1)}, bf16[160,1024]{1,0:T(8,128)(2,1)}, u32[]{:S(2)}, u32[]{:S(2)}) collective-permute-start(bf16[160,1024]{1,0:T(8,128)(2,1)S(1)} %copy-done.145), channel_id=1, source_target_pairs={{0,3},{1,2},{2,1},{3,0},{4,7},{5,6},{6,5},{7,4},{8,11},{9,10},{10,... | collective-permute-start | bytes 983048 | tf_op jit(solution)/shard_map/ppermute | solution.py:590
  152.2 312.7 %reduce-scatter.10.cloned.1.call-start = ((), (), s32[]{:S(2)}) async-start(), calls=%async_computation.20 | async-start | bytes 1966080 | tf_op jit(solution)/shard_map/reduce_scatter | solution.py:823
  176.8 40.2 %collective-permute-start.10 = (bf16[160,1024]{1,0:T(8,128)(2,1)}, bf16[160,1024]{1,0:T(8,128)(2,1)}, u32[]{:S(2)}, u32[]{:S(2)}) collective-permute-start(bf16[160,1024]{1,0:T(8,128)(2,1)} %convolution_convert_fusion.5), channel_id=1, source_target_pairs={{0,2},{1,3},{2,0},{3,1},{4,6},{5,7},{6,4},{7,5},{8,10},{9,11},{10,... | collective-permute-start | bytes 983048 | tf_op jit(solution)/shard_map/ppermute | solution.py:590
  178.3 39.3 %collective-permute-start.11 = (bf16[160,1024]{1,0:T(8,128)(2,1)}, bf16[160,1024]{1,0:T(8,128)(2,1)S(1)}, u32[]{:S(2)}, u32[]{:S(2)}) collective-permute-start(bf16[160,1024]{1,0:T(8,128)(2,1)} %convolution_convert_fusion.4), channel_id=1, source_target_pairs={{0,3},{1,2},{2,1},{3,0},{4,7},{5,6},{6,5},{7,4},{8,11},{9,10},{10,... | collective-permute-start | bytes 983048 | tf_op jit(solution)/shard_map/ppermute | solution.py:590
  192.0 28.1 %collective-permute-start.12 = (bf16[160,1024]{1,0:T(8,128)(2,1)}, bf16[160,1024]{1,0:T(8,128)(2,1)S(1)}, u32[]{:S(2)}, u32[]{:S(2)}) collective-permute-start(bf16[160,1024]{1,0:T(8,128)(2,1)} %convolution_convert_fusion.14), channel_id=1, source_target_pairs={{0,1},{1,0},{2,3},{3,2},{4,5},{5,4},{6,7},{7,6},{8,9},{9,8},{10,11... | collective-permute-start | bytes 983048 | tf_op jit(solution)/shard_map/ppermute | solution.py:590
  243.2 51.5 %collective-permute-start.15 = (bf16[160,1024]{1,0:T(8,128)(2,1)}, bf16[160,1024]{1,0:T(8,128)(2,1)}, u32[]{:S(2)}, u32[]{:S(2)}) collective-permute-start(bf16[160,1024]{1,0:T(8,128)(2,1)} %get-tuple-element.198), channel_id=1, source_target_pairs={{0,1},{1,0},{2,3},{3,2},{4,5},{5,4},{6,7},{7,6},{8,9},{9,8},{10,11... | collective-permute-start | bytes 983048 | tf_op jit(solution)/shard_map/ppermute | solution.py:590
  243.5 51.3 %collective-permute-start.16 = (bf16[160,1024]{1,0:T(8,128)(2,1)}, bf16[160,1024]{1,0:T(8,128)(2,1)}, u32[]{:S(2)}, u32[]{:S(2)}) collective-permute-start(bf16[160,1024]{1,0:T(8,128)(2,1)} %get-tuple-element.199), channel_id=1, source_target_pairs={{0,2},{1,3},{2,0},{3,1},{4,6},{5,7},{6,4},{7,5},{8,10},{9,11},{10,... | collective-permute-start | bytes 983048 | tf_op jit(solution)/shard_map/ppermute | solution.py:590
  244.8 51.1 %collective-permute-start.17 = (bf16[160,1024]{1,0:T(8,128)(2,1)}, bf16[160,1024]{1,0:T(8,128)(2,1)}, u32[]{:S(2)}, u32[]{:S(2)}) collective-permute-start(bf16[160,1024]{1,0:T(8,128)(2,1)} %get-tuple-element.200), channel_id=1, source_target_pairs={{0,3},{1,2},{2,1},{3,0},{4,7},{5,6},{6,5},{7,4},{8,11},{9,10},{10,... | collective-permute-start | bytes 983048 | tf_op jit(solution)/shard_map/ppermute | solution.py:590
  254.8 37.1 %collective-permute-start.21 = (bf16[4,1536,128]{2,1,0:T(8,128)(2,1)}, bf16[4,1536,128]{2,1,0:T(8,128)(2,1)S(1)}, u32[]{:S(2)}, u32[]{:S(2)}) collective-permute-start(bf16[4,1536,128]{2,1,0:T(8,128)(2,1)} %get-tuple-element.207), channel_id=1, source_target_pairs={{0,4},{4,0},{1,5},{5,1},{2,6},{6,2},{3,7},{7,3},{8,12},{12,8},{9,1... | collective-permute-start | bytes 4718600 | tf_op jit(solution)/shard_map/ppermute | solution.py:752
  289.8 32.6 %collective-permute-start.22 = (bf16[160,1024]{1,0:T(8,128)(2,1)}, bf16[160,1024]{1,0:T(8,128)(2,1)}, u32[]{:S(2)}, u32[]{:S(2)}) collective-permute-start(bf16[160,1024]{1,0:T(8,128)(2,1)} %get-tuple-element.215), channel_id=1, source_target_pairs={{0,1},{1,0},{2,3},{3,2},{4,5},{5,4},{6,7},{7,6},{8,9},{9,8},{10,11... | collective-permute-start | bytes 983048 | tf_op jit(solution)/shard_map/ppermute | solution.py:590
  291.9 30.5 %collective-permute-start.23 = (bf16[160,1024]{1,0:T(8,128)(2,1)}, bf16[160,1024]{1,0:T(8,128)(2,1)}, u32[]{:S(2)}, u32[]{:S(2)}) collective-permute-start(bf16[160,1024]{1,0:T(8,128)(2,1)} %get-tuple-element.216), channel_id=1, source_target_pairs={{0,2},{1,3},{2,0},{3,1},{4,6},{5,7},{6,4},{7,5},{8,10},{9,11},{10,... | collective-permute-start | bytes 983048 | tf_op jit(solution)/shard_map/ppermute | solution.py:590
  294.6 175.7 %reduce-scatter.12.cloned.1.call-start = ((), (), s32[]{:S(2)}) async-start(), calls=%async_computation.21 | async-start | bytes 1638400 | tf_op jit(solution)/shard_map/reduce_scatter | solution.py:823
  294.8 39.2 %collective-permute-start.25 = (bf16[4,1280,128]{2,1,0:T(8,128)(2,1)}, bf16[4,1280,128]{2,1,0:T(8,128)(2,1)S(1)}, u32[]{:S(2)}, u32[]{:S(2)}) collective-permute-start(bf16[4,1280,128]{2,1,0:T(8,128)(2,1)} %copy-done.48), channel_id=1, source_target_pairs={{0,4},{4,0},{1,5},{5,1},{2,6},{6,2},{3,7},{7,3},{8,12},{12,8},{9,1... | collective-permute-start | bytes 3932168 | tf_op jit(solution)/shard_map/ppermute | solution.py:752
  335.4 48.3 %collective-permute-start.29 = (bf16[512,2048]{1,0:T(8,128)(2,1)}, bf16[512,2048]{1,0:T(8,128)(2,1)}, u32[]{:S(2)}, u32[]{:S(2)}) collective-permute-start(bf16[512,2048]{1,0:T(8,128)(2,1)} %get-tuple-element.256), channel_id=1, source_target_pairs={{0,4},{4,0},{1,5},{5,1},{2,6},{6,2},{3,7},{7,3},{8,12},{12,8},{9,1... | collective-permute-start | bytes 6291464 | tf_op jit(solution)/shard_map/ppermute | solution.py:752
  336.3 217.3 %reduce-scatter.14.cloned.1.call-start = ((), (), s32[]{:S(2)}) async-start(), calls=%async_computation.22 | async-start | bytes 2621440 | tf_op jit(solution)/shard_map/reduce_scatter | solution.py:823
  387.6 166.0 %reduce-scatter.16.cloned.1.call-start = ((), (), s32[]{:S(2)}) async-start(), calls=%async_computation.23 | async-start | bytes 1966080 | tf_op jit(solution)/shard_map/reduce_scatter | solution.py:823
  420.6 133.1 %reduce-scatter.18.cloned.1.call-start = ((), (), s32[]{:S(2)}) async-start(), calls=%async_computation.24 | async-start | bytes 1966080 | tf_op jit(solution)/shard_map/reduce_scatter | solution.py:823
  461.2 145.1 %reduce-scatter.20.cloned.1.call-start = ((), (), s32[]{:S(2)}) async-start(), calls=%async_computation.25 | async-start | bytes 655360 | tf_op jit(solution)/shard_map/reduce_scatter | solution.py:823
  473.6 66.2 %collective-permute-start.31 = (bf16[256,1152]{1,0:T(8,128)(2,1)}, bf16[256,1152]{1,0:T(8,128)(2,1)}, u32[]{:S(2)}, u32[]{:S(2)}) collective-permute-start(bf16[256,1152]{1,0:T(8,128)(2,1)} %bitcast.32), channel_id=1, source_target_pairs={{0,1},{1,0},{2,3},{3,2},{4,5},{5,4},{6,7},{7,6},{8,9},{9,8},{10,11... | collective-permute-start | bytes 1769480 | tf_op jit(solution)/shard_map/ppermute | solution.py:590
  473.7 66.2 %collective-permute-start.32 = (bf16[256,1152]{1,0:T(8,128)(2,1)}, bf16[256,1152]{1,0:T(8,128)(2,1)}, u32[]{:S(2)}, u32[]{:S(2)}) collective-permute-start(bf16[256,1152]{1,0:T(8,128)(2,1)} %bitcast.33), channel_id=1, source_target_pairs={{0,2},{1,3},{2,0},{3,1},{4,6},{5,7},{6,4},{7,5},{8,10},{9,11},{10,... | collective-permute-start | bytes 1769480 | tf_op jit(solution)/shard_map/ppermute | solution.py:590
  474.5 65.3 %collective-permute-start.33 = (bf16[256,1152]{1,0:T(8,128)(2,1)}, bf16[256,1152]{1,0:T(8,128)(2,1)}, u32[]{:S(2)}, u32[]{:S(2)}) collective-permute-start(bf16[256,1152]{1,0:T(8,128)(2,1)} %bitcast.34), channel_id=1, source_target_pairs={{0,3},{1,2},{2,1},{3,0},{4,7},{5,6},{6,5},{7,4},{8,11},{9,10},{10,... | collective-permute-start | bytes 1769480 | tf_op jit(solution)/shard_map/ppermute | solution.py:590
  475.5 67.1 %collective-permute-start.30 = (bf16[512,2048]{1,0:T(8,128)(2,1)}, bf16[512,2048]{1,0:T(8,128)(2,1)}, u32[]{:S(2)}, u32[]{:S(2)}) collective-permute-start(bf16[512,2048]{1,0:T(8,128)(2,1)} %get-tuple-element.260), channel_id=1, source_target_pairs={{0,4},{4,0},{1,5},{5,1},{2,6},{6,2},{3,7},{7,3},{8,12},{12,8},{9,1... | collective-permute-start | bytes 6291464 | tf_op jit(solution)/shard_map/ppermute | solution.py:752
  539.8 66.5 %reduce-scatter.22.cloned.1.call-start = ((), (), s32[]{:S(2)}) async-start(), calls=%async_computation.26 | async-start | bytes 737280 | tf_op jit(solution)/shard_map/reduce_scatter | solution.py:823
  549.7 56.6 %all-to-all-start.5 = ((bf16[8,3,64,512]{3,2,1,0:T(8,128)(2,1)}), bf16[8,3,64,512]{3,2,1,0:T(8,128)(2,1)S(1)}, u32[]{:S(2)}, u32[]{:S(2)}) async-start(bf16[8,3,64,512]{3,2,1,0:T(8,128)(2,1)} %get-tuple-element.259), calls=%async_computation.7 | async-start | bytes 3145728 | tf_op jit(solution)/shard_map/all_to_all | solution.py:584
  553.3 86.0 %reduce-scatter.24.cloned.1.call-start = ((), (), s32[]{:S(2)}) async-start(), calls=%async_computation.27 | async-start | bytes 655360 | tf_op jit(solution)/shard_map/reduce_scatter | solution.py:823
  553.7 51.8 %collective-permute-start.34 = (bf16[128,1536]{1,0:T(8,128)(2,1)}, bf16[128,1536]{1,0:T(8,128)(2,1)S(1)}, u32[]{:S(2)}, u32[]{:S(2)}) collective-permute-start(bf16[128,1536]{1,0:T(8,128)(2,1)} %reduce-scatter.18.cloned.1.call-done), channel_id=1, source_target_pairs={{0,4},{4,0},{1,5},{5,1},{2,6},{6,2},{3,7},{7,3},{8,12},{12,8},{9,1... | collective-permute-start | bytes 1179656 | tf_op jit(solution)/shard_map/ppermute | solution.py:752
  615.1 71.9 %reduce-scatter.26.cloned.1.call-start = ((), (), s32[]{:S(2)}) async-start(), calls=%async_computation.28 | async-start | bytes 2621440 | tf_op jit(solution)/shard_map/reduce_scatter | solution.py:823
  (172 other events, 1555.0 us)
Sparse Core Ops, SparseCore 0:
  47.0 50.0 all-gather.2
  99.0 45.8 all-gather.4
  294.8 35.6 reduce-scatter.9
  336.4 32.1 reduce-scatter.11
  387.7 44.7 reduce-scatter.13
  434.8 34.5 reduce-scatter.15
  471.8 34.2 reduce-scatter.17
  533.6 22.6 reduce-scatter.19
  559.3 20.3 reduce-scatter.21
  615.2 24.0 reduce-scatter.23
  642.3 42.0 reduce-scatter.25
where the time goes:
time: 709 us; the launch traced here: 697 us
  Pallas kernels  306 us (43%)
  waiting for transfers between devices  120 us (17%)
  local copies, waits for them, and re-layouts  78.9 us (11%)
  starting transfers between devices  65.7 us (9%)
  matrix products  57.1 us (8%)
  other arithmetic  53.1 us (7%)
  between operations  16 us (2%)
    pallas_call x2, Pallas kernels, attention_bwd(): pl.pallas_call(functools.partial(attention_bwd_kernel, bk, order), grid_s...  91.8 us
    pallas_call x2, Pallas kernels, attention_fwd(): pl.pallas_call(functools.partial(attention_fwd_kernel, bk, order), grid_s...  60 us
    dot_general x29, matrix products, mm(): return lax.dot_general(left, right, dims, preferred_element_type=f32)  54.4 us
    ppermute x5, waiting for transfers between devices, ctx_sum(): came = lax.ppermute(other, 'ctx', [(0, 1), (1, 0)])  49.3 us
    pallas_call x2, Pallas kernels, expert_bwd(): pl.pallas_call(functools.partial(expert_bwd_kernel, steps), grid=(steps,)...  49 us
    unnamed x325, local copies, waits for them, and re-layouts  47.1 us
    pallas_call x2, Pallas kernels, expert_fwd(): pl.pallas_call(functools.partial(expert_fwd_kernel, steps), grid=(steps,)...  40.6 us
    all_to_all x9, starting transfers between devices, swap_blocks(): return lax.all_to_all(blocks, axes, split_axis=0, concat_axis=0, tiled=True)  36.3 us
  transfers between devices with their start and end apart: 56, of which 12 were waited for; matrix products, arithmetic and copies ran while one was open for 20% of the time, Pallas kernels for 43%

commit v1 on v0

--- a/solution.py
+++ b/solution.py
@@ -65,7 +65,7 @@
         vaug[HEAD_DIM:, :] = first.astype(f32).astype(bf16)
         for p in range(blocks):
             rows = slice(p * tok, (p + 1) * tok)
-            kaug[rows, :] = jnp.concatenate([k_ref[order(p), 0].T, kmask_ref[rows, :]], axis=1)
+            kaug[rows, :] = jnp.concatenate([k_ref[order(p), 0], kmask_ref[:, rows]], axis=0).T
             vaug[0:HEAD_DIM, rows] = v_ref[order(p), 0]
 
     qaug = jnp.concatenate([q_ref[0, 0], qmask_ref[...]], axis=0)
@@ -96,7 +96,7 @@
             grid=(blocks,),
             in_specs=[
                 pl.BlockSpec((8, 2 * length), lambda i, *_: (0, 0)),
-                pl.BlockSpec((length, 64), lambda i, *_: (0, 0)),
+                pl.BlockSpec((64, length), lambda i, *_: (0, 0)),
                 pl.BlockSpec((64, tok), lambda i, *_: (0, i)),
                 pl.BlockSpec((1, 1, dim, tok), lambda i, *_: (order(i), 0, 0, 0)),
                 pl.BlockSpec((blocks, 1, dim, tok), lambda i, *_: (0, 1, 0, 0)),
@@ -116,7 +116,7 @@
             jax.ShapeDtypeStruct((blocks, dim, tok), bf16),
             jax.ShapeDtypeStruct((blocks, 1, tok), f32),
         ],
-        compiler_params=pltpu.CompilerParams(vmem_limit_bytes=48 << 20),
+        compiler_params=pltpu.CompilerParams(vmem_limit_bytes=60 << 20),
         cost_estimate=cost(2000 * length * length // 2, 4 * length * 2 * dim, length * length // 2),
         name="attention_fwd",
     )(chunks, table, buck, kmask, qmask, qkv, qkv, qkv)
@@ -240,7 +240,7 @@
             jax.ShapeDtypeStruct((blocks, 3, dim, tok), bf16),
             jax.ShapeDtypeStruct((table.shape[0], 128), f32),
         ],
-        compiler_params=pltpu.CompilerParams(vmem_limit_bytes=48 << 20),
+        compiler_params=pltpu.CompilerParams(vmem_limit_bytes=60 << 20),
         cost_estimate=cost(5000 * length * length // 2, 8 * length * 2 * dim, length * length // 2),
         name="attention_bwd",
     )(chunks, table, buck, kmask, qmask, qkv, qkv, qkv, mixed, mixed_grad, lse)
@@ -252,17 +252,30 @@
         ref[...] = acc[d * rows : (d + 1) * rows, :].astype(bf16)
 
 
-def expert_fwd_kernel(
-    steps, x_ref, wg_ref, wu_ref, wd_ref, h_ref, act_ref, slope_ref, *refs
-):
-    outs, acc = refs[:-1], refs[-1]
+def join_rows(refs, scratch):
+    at = 0
+    for ref in refs:
+        scratch[at : at + ref.shape[0], :] = ref[:, : scratch.shape[1]]
+        at += ref.shape[0]
+
+
+def gate_column(refs):
+    return jnp.concatenate(
+        [jnp.sum(ref[...].astype(f32), axis=1, keepdims=True) for ref in refs], axis=0
+    )
+
+
+def expert_fwd_kernel(steps, groups, wg_ref, wu_ref, wd_ref, *refs):
+    xs, refs = refs[:groups], refs[groups:]
+    h_ref, act_ref, slope_ref, *outs, rows, acc = refs
     f = pl.program_id(0)
 
     @pl.when(f == 0)
     def _():
+        join_rows(xs, rows)
         acc[...] = jnp.zeros_like(acc)
 
-    x = x_ref[...]
+    x = rows[...]
     gate = mm(x, wg_ref[0], NN)
     up = mm(x, wu_ref[0], NN)
     square = gate * gate
@@ -283,45 +296,44 @@
         write_groups(acc, outs)
 
 
-def expert_fwd(x, w_in, w_down, groups, tile=256):
-    rows, width = x.shape
-    ff = w_down.shape[1]
+def expert_fwd(xs, w_in, w_down, tile=256):
+    groups = len(xs)
+    ff, width = w_down.shape[1:]
+    rows = groups * xs[0].shape[0]
     steps = ff // tile
-    whole = pl.BlockSpec((rows, width), lambda f: (0, 0))
     part = pl.BlockSpec((rows, tile), lambda f: (0, f))
     inner = jax.ShapeDtypeStruct((rows, ff), bf16)
     one = pl.BlockSpec((rows // groups, width), lambda f: (0, 0))
     return pl.pallas_call(
-        functools.partial(expert_fwd_kernel, steps),
+        functools.partial(expert_fwd_kernel, steps, groups),
         grid=(steps,),
         in_specs=[
-            whole,
             pl.BlockSpec((1, width, tile), lambda f: (0, 0, f)),
             pl.BlockSpec((1, width, tile), lambda f: (0, 0, f + steps)),
             pl.BlockSpec((1, tile, width), lambda f: (0, f, 0)),
-        ],
+        ]
+        + [pl.BlockSpec(xs[0].shape, lambda f: (0, 0))] * groups,
         out_specs=[part, part, part] + [one] * groups,
         out_shape=[inner, inner, inner]
         + [jax.ShapeDtypeStruct((rows // groups, width), bf16)] * groups,
-        scratch_shapes=[pltpu.VMEM((rows, width), f32)],
-        compiler_params=pltpu.CompilerParams(vmem_limit_bytes=48 << 20),
+        scratch_shapes=[pltpu.VMEM((rows, width), bf16), pltpu.VMEM((rows, width), f32)],
+        compiler_params=pltpu.CompilerParams(vmem_limit_bytes=60 << 20),
         cost_estimate=cost(
             10 * rows * width * ff, 6 * width * ff + rows * (4 * width + 6 * ff), rows * ff
         ),
         name="expert_fwd",
-    )(x, w_in, w_in, w_down)
-
-
-def expert_bwd_kernel(
-    steps, g_ref, gate_ref, act_ref, slope_ref, wg_ref, wu_ref, wd_ref,
-    grads_ref, *refs,
-):
-    outs, pg, acc = refs[:-2], refs[-2], refs[-1]
+    )(w_in, w_in, w_down, *xs)
+
+
+def expert_bwd_kernel(steps, groups, act_ref, slope_ref, wg_ref, wu_ref, wd_ref, *refs):
+    gs, gates, refs = refs[:groups], refs[groups : 2 * groups], refs[2 * groups :]
+    grads_ref, *outs, pg, acc = refs
     f = pl.program_id(0)
 
     @pl.when(f == 0)
     def _():
-        pg[...] = (g_ref[...].astype(f32) * gate_ref[...]).astype(bf16)
+        join_rows(gs, pg)
+        pg[...] = (pg[...].astype(f32) * gate_column(gates)).astype(bf16)
         acc[...] = jnp.zeros_like(acc)
 
     hidden_grad = mm(pg[...], wd_ref[0], NT)
@@ -336,49 +348,50 @@
         write_groups(acc, outs)
 
 
-def expert_bwd(g, gate, act, slope, w_in, w_down, groups, tile=256):
-    rows, width = g.shape
+def gate_block(x, width):
+    return pl.BlockSpec((x.shape[0], 128), lambda f, *_: (0, width // 128))
+
+
+def expert_bwd(gs, xs, act, slope, w_in, w_down, tile=256):
+    groups = len(gs)
+    rows, width = groups * gs[0].shape[0], gs[0].shape[1]
     ff = w_down.shape[1]
     steps = ff // tile
-    whole = pl.BlockSpec((rows, width), lambda f: (0, 0))
     part = pl.BlockSpec((rows, tile), lambda f: (0, f))
     one = pl.BlockSpec((rows // groups, width), lambda f: (0, 0))
     return pl.pallas_call(
-        functools.partial(expert_bwd_kernel, steps),
+        functools.partial(expert_bwd_kernel, steps, groups),
         grid=(steps,),
         in_specs=[
-            whole,
-            pl.BlockSpec((rows, 1), lambda f: (0, 0)),
             part,
             part,
             pl.BlockSpec((1, width, tile), lambda f: (0, 0, f)),
             pl.BlockSpec((1, width, tile), lambda f: (0, 0, f + steps)),
             pl.BlockSpec((1, tile, width), lambda f: (0, f, 0)),
-        ],
+        ]
+        + [one] * groups
+        + [gate_block(x, width) for x in xs],
         out_specs=[pl.BlockSpec((2, rows, tile), lambda f: (0, 0, f))] + [one] * groups,
         out_shape=[jax.ShapeDtypeStruct((2, rows, ff), bf16)]
         + [jax.ShapeDtypeStruct((rows // groups, width), bf16)] * groups,
         scratch_shapes=[pltpu.VMEM((rows, width), bf16), pltpu.VMEM((rows, width), f32)],
-        compiler_params=pltpu.CompilerParams(vmem_limit_bytes=48 << 20),
+        compiler_params=pltpu.CompilerParams(vmem_limit_bytes=60 << 20),
         cost_estimate=cost(
             10 * rows * width * ff, 6 * width * ff + rows * (4 * width + 8 * ff)
         ),
         name="expert_bwd",
-    )(g, gate, act, slope, w_in, w_in, w_down)
-
-
-def column_block(ref, copies, ctx, flip, a):
-    blk = ref.shape[1] // copies
+    )(act, slope, w_in, w_in, w_down, *gs, *xs)
+
+
+def column_block(ref, blk, ctx, flip, a):
     low = ref[:, 2 * a * blk : (2 * a + 1) * blk]
     high = ref[:, (2 * a + 1) * blk : (2 * a + 2) * blk]
     return jnp.where(lax.rem(ctx + flip, 2) == 0, low, high)
 
 
-def in_grad_kernel(copies, ctx_ref, *refs):
-    n = (len(refs) - 3) // 2
-    xs, gs = refs[:n], refs[n : 2 * n]
-    own_ref, other_ref, xt = refs[2 * n :]
-    width = xs[0].shape[1]
+def in_grad_kernel(copies, n, ctx_ref, *refs):
+    xs, (*gs, own_ref, other_ref, xt) = refs[:n], refs[n:]
+    width = xt.shape[0]
     blk = width // copies
 
     @pl.when(pl.program_id(0) == 0)
@@ -390,7 +403,7 @@
                 for a in range(copies // 2):
                     to = (flip * (copies // 2) + a) * blk
                     xt[to : to + blk, at : at + rows] = column_block(
-                        x_ref, copies, ctx_ref[0], flip, a
+                        x_ref, blk, ctx_ref[0], flip, a
                     ).T
             at += rows
 
@@ -401,7 +414,7 @@
 
 
 def in_grad(ctx, xs, grads, copies, first, count, tile=256):
-    width = xs[0].shape[1]
+    width = xs[0].shape[1] - 128
     steps = grads[0].shape[2] // tile
     total = sum(x.shape[0] for x in xs)
     half = jax.ShapeDtypeStruct((width // 2, count * tile), bf16)
@@ -411,7 +424,7 @@
         return ((f + first) // steps, 0, (f + first) % steps)
 
     return pl.pallas_call(
-        functools.partial(in_grad_kernel, copies),
+        functools.partial(in_grad_kernel, copies, len(xs)),
         grid_spec=pltpu.PrefetchScalarGridSpec(
             num_scalar_prefetch=1,
             grid=(count,),
@@ -421,7 +434,7 @@
             scratch_shapes=[pltpu.VMEM((width, total), bf16)],
         ),
         out_shape=[half, half],
-        compiler_params=pltpu.CompilerParams(vmem_limit_bytes=48 << 20),
+        compiler_params=pltpu.CompilerParams(vmem_limit_bytes=60 << 20),
         cost_estimate=cost(
             4 * total * width * count * tile, 2 * (total + width) * count * tile + 2 * total * width
         ),
@@ -429,10 +442,8 @@
     )(ctx, *xs, *grads)
 
 
-def down_grad_kernel(copies, ctx_ref, *refs):
-    n = (len(refs) - 3) // 3
-    hs, ps, gates = refs[:n], refs[n : 2 * n], refs[2 * n : 3 * n]
-    own_ref, other_ref, pg = refs[3 * n :]
+def down_grad_kernel(copies, n, ctx_ref, *refs):
+    ps, gates, (*hs, own_ref, other_ref, pg) = refs[:n], refs[n : 2 * n], refs[2 * n :]
     blk = ps[0].shape[1] // copies
 
     @pl.when(pl.program_id(0) == 0)
@@ -440,11 +451,12 @@
         at = 0
         for p_ref, gate_ref in zip(ps, gates):
             rows = p_ref.shape[0]
+            gate = gate_column([gate_ref])
             for flip in range(2):
                 for a in range(copies // 2):
                     to = (flip * (copies // 2) + a) * blk
-                    block = column_block(p_ref, copies, ctx_ref[0], flip, a).astype(f32)
-                    pg[at : at + rows, to : to + blk] = (block * gate_ref[...]).astype(bf16)
+                    block = column_block(p_ref, blk, ctx_ref[0], flip, a).astype(f32)
+                    pg[at : at + rows, to : to + blk] = (block * gate).astype(bf16)
             at += rows
 
     grad = mm(jnp.concatenate([h[...] for h in hs], axis=0), pg[...], TN).astype(bf16)
@@ -454,7 +466,7 @@
         other_ref[a] = grad[:, to : to + blk]
 
 
-def down_grad(ctx, hs, ps, gates, copies, first, count, tile=256):
+def down_grad(ctx, hs, ps, xs, copies, first, count, tile=256):
     ff = count * tile
     width = ps[0].shape[1]
     total = sum(h.shape[0] for h in hs)
@@ -462,21 +474,21 @@
     half = jax.ShapeDtypeStruct((copies // 2, ff, blk), bf16)
     out = pl.BlockSpec((copies // 2, tile, blk), lambda f, c: (0, f, 0))
     return pl.pallas_call(
-        functools.partial(down_grad_kernel, copies),
+        functools.partial(down_grad_kernel, copies, len(ps)),
         grid_spec=pltpu.PrefetchScalarGridSpec(
             num_scalar_prefetch=1,
             grid=(count,),
-            in_specs=[pl.BlockSpec((h.shape[0], tile), lambda f, c: (0, f + first)) for h in hs]
-            + [pl.BlockSpec(p.shape, lambda f, c: (0, 0)) for p in ps]
-            + [pl.BlockSpec(g.shape, lambda f, c: (0, 0)) for g in gates],
+            in_specs=[pl.BlockSpec(p.shape, lambda f, c: (0, 0)) for p in ps]
+            + [gate_block(x, width) for x in xs]
+            + [pl.BlockSpec((h.shape[0], tile), lambda f, c: (0, f + first)) for h in hs],
             out_specs=[out, out],
             scratch_shapes=[pltpu.VMEM((total, width), bf16)],
         ),
         out_shape=[half, half],
-        compiler_params=pltpu.CompilerParams(vmem_limit_bytes=48 << 20),
+        compiler_params=pltpu.CompilerParams(vmem_limit_bytes=60 << 20),
         cost_estimate=cost(4 * total * width * ff, 2 * (total * (width + ff) + width * ff)),
         name="down_grad",
-    )(ctx, *hs, *ps, *gates)
+    )(ctx, *ps, *xs, *hs)
 
 
 def project_kernel(x_ref, gain_ref, w_ref, normed_ref, *refs):
@@ -516,7 +528,7 @@
         out_shape=[jax.ShapeDtypeStruct((tok, width), bf16)]
         + [jax.ShapeDtypeStruct((groups, 3, HEAD_DIM, tok), bf16)] * heads,
         scratch_shapes=[pltpu.VMEM((width, tok), bf16)],
-        compiler_params=pltpu.CompilerParams(vmem_limit_bytes=48 << 20),
+        compiler_params=pltpu.CompilerParams(vmem_limit_bytes=60 << 20),
         cost_estimate=cost(6 * tok * width * width, 6 * width * width + 10 * tok * width),
         name="project",
     )(x, gain.reshape(1, width), weight)
@@ -566,14 +578,222 @@
         out_specs=whole,
         out_shape=jax.ShapeDtypeStruct((tok, width), f32),
         scratch_shapes=[pltpu.VMEM((width, tok), f32)],
-        compiler_params=pltpu.CompilerParams(vmem_limit_bytes=48 << 20),
+        compiler_params=pltpu.CompilerParams(vmem_limit_bytes=60 << 20),
         cost_estimate=cost(6 * tok * width * width, 6 * width * width + 16 * tok * width),
         name="input_grad",
     )(x, gain.reshape(1, width), middle_grad, weight, *grads)
 
 
-def rms_scale(values, gain_vec):
-    return values * lax.rsqrt(jnp.mean(values * values, axis=-1, keepdims=True) + 1e-06) * gain_vec
+def wide_thirds(values):
+    high = values.astype(bf16)
+    rest = values - high.astype(f32)
+    mid = rest.astype(bf16)
+    low = (rest - mid.astype(f32)).astype(bf16)
+    rows, lanes = values.shape
+    blank = jnp.zeros((rows, 128 - 3 * lanes), bf16)
+    return jnp.concatenate([high, mid, low, blank], axis=1)
+
+
+def combine_kernel(
+    counts, exp_ref, place_ref, ids_ref, probs_ref, middle_ref, cot_ref, normed_ref, gain_ref,
+    router_ref, weight_ref, *refs,
+):
+    blocks, heads, parts, copies = counts
+    experts = probs_ref.shape[1]
+    backs, refs = refs[:blocks], refs[blocks:]
+    row_grads, refs = refs[:blocks], refs[blocks:]
+    mixed, refs = refs[:heads], refs[heads:]
+    out_ref, mid_ref, refs = refs[0], refs[1], refs[2:]
+    mixed_grads, refs = refs[:heads], refs[heads:]
+    early, (slot_rows, slot_grads, wide) = refs[:parts], refs[parts:]
+    tok, width = middle_ref.shape
+    total = slot_rows.shape[0]
+
+    at = 0
+    for back, row_grad in zip(backs, row_grads):
+        rows = slice(at, at + back.shape[0])
+        slot_rows[rows, :] = back[...]
+        slot_grads[rows, :] = row_grad[...]
+        at += back.shape[0]
+
+    slot = lax.broadcasted_iota(jnp.int32, (tok, total), 1)
+    one = (slot == place_ref[:, 0:1]).astype(f32).astype(bf16)
+    two = (slot == place_ref[:, 1:2]).astype(f32).astype(bf16)
+    first = mm(one, slot_rows[...], NN)
+    second = mm(two, slot_rows[...], NN)
+    dy = mm(one + two, slot_grads[...], NN)
+
+    lane = lax.broadcasted_iota(jnp.int32, (tok, experts), 1)
+    is_first, is_second = lane == ids_ref[:, 0:1], lane == ids_ref[:, 1:2]
+    probs = probs_ref[...]
+    gate_first = jnp.sum(jnp.where(is_first, probs, 0.0), axis=1, keepdims=True)
+    gate_second = jnp.sum(jnp.where(is_second, probs, 0.0), axis=1, keepdims=True)
+    middle = middle_ref[...]
+    cot = cot_ref[...].astype(f32)
+    out_ref[...] = (middle + gate_first * first + gate_second * second).astype(bf16)
+    grad_first = jnp.sum(cot * first, axis=1, keepdims=True)
+    grad_second = jnp.sum(cot * second, axis=1, keepdims=True)
+    probs_grad = jnp.where(is_first, grad_first, 0.0) + jnp.where(is_second, grad_second, 0.0)
+    logits_grad = probs * (probs_grad - jnp.sum(probs * probs_grad, axis=1, keepdims=True))
+    for e in range(experts):
+        dy = dy + logits_grad[:, e : e + 1] * router_ref[e : e + 1, :]
+
+    scale = lax.rsqrt(jnp.mean(middle * middle, axis=1, keepdims=True) + 1e-06)
+    unit = middle * scale
+    gain_terms = unit * dy
+    dy = dy * gain_ref[...]
+    middle_grad = cot + scale * (dy - unit * jnp.mean(unit * dy, axis=1, keepdims=True))
+    mid_ref[...] = middle_grad
+    branch = middle_grad.astype(bf16)
+
+    groups, dim, _ = mixed_grads[0].shape
+    back = mm(weight_ref[...], branch, NT).astype(bf16).reshape(groups, heads, dim, tok)
+    for h in range(heads):
+        mixed_grads[h][...] = back[:, h]
+    for h in range(heads):
+        grad = mm(mixed[h][...], branch, NN)
+        for g in range(groups):
+            at = (g * heads + h) * dim
+            wide[at : at + dim, 0:width] = grad[g * dim : (g + 1) * dim]
+    mark = lax.broadcasted_iota(jnp.int32, (tok, 128), 1) == 3 * experts
+    mark = mark.astype(f32).astype(bf16)
+    high = gain_terms.astype(bf16)
+    low = (gain_terms - high.astype(f32)).astype(bf16)
+    wide[:, width:] = (
+        mm(normed_ref[...], wide_thirds(logits_grad), TN) + mm(high, mark, TN) + mm(low, mark, TN)
+    )
+    per = wide.shape[0] // (parts * copies)
+    for d in range(parts):
+        e = jnp.bitwise_xor(exp_ref[0], d)
+        rows = [
+            wide[pl.ds(pl.multiple_of((k * parts + e) * per, per), per), :] for k in range(copies)
+        ]
+        early[d][...] = jnp.concatenate(rows, axis=0).astype(bf16)
+
+
+def combine(
+    exp, place, ids, probs, middle, cot, normed, gain, router, weight, backs, row_grads, mixed,
+    copies,
+):
+    tok, width = middle.shape
+    heads = len(mixed)
+    parts = probs.shape[1]
+    groups = width // (heads * HEAD_DIM)
+    total = sum(b.shape[0] for b in backs)
+    sds = jax.ShapeDtypeStruct
+    return pl.pallas_call(
+        functools.partial(combine_kernel, (len(backs), heads, parts, copies)),
+        in_specs=[pl.BlockSpec(memory_space=pltpu.SMEM)]
+        + [pl.BlockSpec(memory_space=pltpu.VMEM)] * (9 + 2 * len(backs) + heads),
+        out_specs=[pl.BlockSpec(memory_space=pltpu.VMEM)] * (2 + heads + parts),
+        out_shape=[sds((tok, width), bf16), sds((tok, width), f32)]
+        + [sds((groups, HEAD_DIM, tok), bf16)] * heads
+        + [sds((width // parts, width + 128), bf16)] * parts,
+        scratch_shapes=[
+            pltpu.VMEM((total, width), bf16),
+            pltpu.VMEM((total, width), bf16),
+            pltpu.VMEM((width, width + 128), f32),
+        ],
+        compiler_params=pltpu.CompilerParams(vmem_limit_bytes=60 << 20),
+        cost_estimate=cost(
+            6 * tok * total * width + 4 * tok * width * width,
+            4 * total * width + 18 * tok * width + 4 * width * width,
+        ),
+        name="combine",
+    )(exp, place, ids, probs, middle, cot, normed, gain.reshape(1, width), router, weight,
+      *backs, *row_grads, *mixed)
+
+
+def finish_kernel(heads, lanes, n_ctx, exp_ref, rows_ref, weight_ref, gain_ref, grad_ref, gain_grad_ref, bias_ref):
+    groups = rows_ref.shape[0]
+    width = weight_ref.shape[1] // 3
+    for part in range(3):
+        pieces = []
+        for g in range(groups):
+            for h in range(heads):
+                lo = h * lanes + part * HEAD_DIM
+                pieces.append(rows_ref[g][:, lo : lo + HEAD_DIM].astype(f32))
+        grad_ref[:, part * width : (part + 1) * width] = jnp.concatenate(pieces, axis=1)
+    terms = weight_ref[...].astype(f32) * grad_ref[...]
+    gain_grad_ref[...] = jnp.sum(terms, axis=1, keepdims=True) / gain_ref[...]
+    columns = []
+    for c in range(n_ctx):
+        mine = rows_ref[exp_ref[0] * n_ctx + c].astype(f32)
+        for h in range(heads):
+            lo = h * lanes + 3 * HEAD_DIM
+            columns.append(mine[:, lo : lo + 1])
+    bias_ref[...] = jnp.concatenate(columns, axis=1)
+
+
+def finish(exp, rows, weight_rows, gain_rows, heads, lanes, n_ctx):
+    count, columns = weight_rows.shape
+    sds = jax.ShapeDtypeStruct
+    vmem = pl.BlockSpec(memory_space=pltpu.VMEM)
+    return pl.pallas_call(
+        functools.partial(finish_kernel, heads, lanes, n_ctx),
+        in_specs=[pl.BlockSpec(memory_space=pltpu.SMEM), vmem, vmem, vmem],
+        out_specs=[vmem, vmem, vmem],
+        out_shape=[
+            sds((count, columns), f32), sds((count, 1), f32), sds((count, heads * n_ctx), f32)
+        ],
+        cost_estimate=cost(4 * count * columns, 8 * count * columns),
+        name="finish",
+    )(exp, rows, weight_rows, gain_rows)
+
+
+def route_kernel(heads, x_ref, place_ref, ids_ref, gain_ref, router_ref, weight_ref, *refs):
+    mixed, (middle_ref, normed_ref, probs_ref, *slots, joined) = refs[:heads], refs[heads:]
+    tok, width = x_ref.shape
+    experts = probs_ref.shape[1]
+    for h in range(heads):
+        for g in range(width // (heads * HEAD_DIM)):
+            at = (g * heads + h) * HEAD_DIM
+            joined[at : at + HEAD_DIM, :] = mixed[h][g * HEAD_DIM : (g + 1) * HEAD_DIM, :]
+    middle = x_ref[...].astype(f32) + mm(joined[...], weight_ref[...], TN)
+    middle_ref[...] = middle
+    scale = lax.rsqrt(jnp.mean(middle * middle, axis=1, keepdims=True) + 1e-06)
+    normed = (middle * scale * gain_ref[...]).astype(bf16)
+    normed_ref[...] = normed
+    logits = mm(normed, router_ref[...], NN)[:, :experts]
+    weights = jnp.exp(logits - jnp.max(logits, axis=1, keepdims=True))
+    probs = weights / jnp.sum(weights, axis=1, keepdims=True)
+    probs_ref[...] = probs
+    lane = lax.broadcasted_iota(jnp.int32, (tok, experts), 1)
+    gates = [
+        wide_thirds(jnp.sum(jnp.where(lane == ids_ref[:, j : j + 1], probs, 0.0), axis=1, keepdims=True))
+        for j in range(2)
+    ]
+    at = 0
+    for slot_ref in slots:
+        rows = slot_ref.shape[0]
+        slot = lax.broadcasted_iota(jnp.int32, (rows, tok), 0) + at
+        one = (slot == place_ref[0:1, :]).astype(f32).astype(bf16)
+        two = (slot == place_ref[1:2, :]).astype(f32).astype(bf16)
+        slot_ref[:, 0:width] = mm(one + two, normed, NN).astype(bf16)
+        slot_ref[:, width:] = (mm(one, gates[0], NN) + mm(two, gates[1], NN)).astype(bf16)
+        at += rows
+
+
+def route(x, place, ids, gain, router, weight, mixed, sizes):
+    tok, width = x.shape
+    experts = router.shape[1]
+    heads = len(mixed)
+    sds = jax.ShapeDtypeStruct
+    vmem = pl.BlockSpec(memory_space=pltpu.VMEM)
+    return pl.pallas_call(
+        functools.partial(route_kernel, heads),
+        in_specs=[vmem] * (6 + heads),
+        out_specs=[vmem] * (3 + len(sizes)),
+        out_shape=[sds((tok, width), f32), sds((tok, width), bf16), sds((tok, experts), f32)]
+        + [sds((size, width + 128), bf16) for size in sizes],
+        scratch_shapes=[pltpu.VMEM((width, tok), bf16)],
+        compiler_params=pltpu.CompilerParams(vmem_limit_bytes=60 << 20),
+        cost_estimate=cost(
+            2 * tok * width * (width + sum(sizes)), 12 * tok * width + 2 * width * width
+        ),
+        name="route",
+    )(x, place.T, ids, gain.reshape(1, width), jnp.pad(router, ((0, 0), (0, 128 - experts))),
+      weight, *mixed)
 
 
 def dot_f32(left, right, left_dim, right_dim):
@@ -584,11 +804,28 @@
     return lax.all_to_all(blocks, axes, split_axis=0, concat_axis=0, tiled=True)
 
 
-def exchange(parts):
+def exchange(parts, axis="expert"):
     n = len(parts)
     return [parts[0]] + [
-        lax.ppermute(parts[d], "expert", [(i, i ^ d) for i in range(n)]) for d in range(1, n)
+        lax.ppermute(parts[d], axis, [(i, i ^ d) for i in range(n)]) for d in range(1, n)
     ]
+
+
+def scatter_dp(rows):
+    n = lax.axis_size("dp")
+    shares = rows.reshape((n, rows.shape[0] // n) + rows.shape[1:])
+    mine = lax.axis_index("dp")
+    return exchange(
+        [
+            lax.dynamic_index_in_dim(shares, jnp.bitwise_xor(mine, d), 0, False)
+            for d in range(n)
+        ],
+        "dp",
+    )
+
+
+def add_low(parts):
+    return sum(part.astype(f32) for part in parts).astype(bf16)
 
 
 def after(value, *others):
@@ -609,7 +846,7 @@
     qmask = jnp.concatenate([hide, jnp.zeros((48, length), bf16)], axis=0)
     last = block_row.reshape(blocks, tok)[:, -1]
     seen = jnp.sum((block_row[None, :] <= last[:, None]).astype(jnp.int32), axis=1)
-    return buck_rev, buck, kmask_t.T, kmask_t, qmask, hide, seen
+    return buck_rev, buck, kmask_t, qmask, hide, seen
 
 
 def shards(
@@ -652,11 +889,11 @@
         shape = blocks.shape
         return jnp.swapaxes(blocks.reshape((n_ctx, n_exp) + shape[1:]), 0, 1).reshape(shape)
 
-    inputs = layer_input.astype(f32)
+    exp_arg = exp_index.astype(jnp.int32).reshape(1)
     normed, *parts = project(layer_input, attn_gain, qkv_weight, groups, heads)
     qkv = [swap_blocks(part, pair) for part in parts]
     table_dev = lax.dynamic_slice_in_dim(bias_table, ctx_index * heads, heads, 1)
-    buck_rev, buck, kmask, kmask_t, qmask, hide, seen = attention_plan(
+    buck_rev, buck, kmask, qmask, hide, seen = attention_plan(
         block_ids[0], bucket_ids, groups, tok
     )
     chunks = (seen + step_k - 1) // step_k
@@ -667,199 +904,143 @@
     earlier = fill_rank[None, :] < fill_rank[:, None]
     slot_of = jnp.sum((same_expert & earlier).astype(jnp.int32), axis=1)
     slots = slot_of.reshape(tok, TOP)
-    choose = (expert_ids[:, :, None] == jnp.arange(experts)[None, None, :]).astype(f32)
-
-    expert_at = jnp.bitwise_xor(jnp.arange(experts), exp_index)
-
-    def hits(d, low, high):
-        slot_at = jnp.arange(low, high)[:, None]
-        return [
-            (expert_at[d] == expert_ids[None, :, j]) & (slot_at == slots[None, :, j])
-            for j in range(TOP)
-        ]
-
-    pick = [
-        [[one.astype(bf16) for one in hits(d, low, high)] for d in range(experts)]
-        for low, high in spans
-    ]
-
-    def to_slots(rows, part):
-        return [
-            dot_f32(first + second, rows, 1, 0).astype(bf16) for first, second in pick[part]
-        ]
-
-    forward, mixed, normed_seq = [], [], []
-    slots_a = to_slots(cotangent, 0)
-    slots_b = to_slots(cotangent, 1)
-    qkv[0], pick, slots_a, slots_b, buck_rev, buck, kmask, kmask_t, qmask, hide = (
+    part_at = jnp.where(slots < cut, 0, experts * cut - cut)
+    stride = jnp.where(slots < cut, cut, capacity - cut)
+    place = jnp.where(
+        slots < capacity,
+        part_at + jnp.bitwise_xor(expert_ids, exp_index) * stride + slots,
+        -1,
+    )
+    sizes = [high - low for low, high in spans for _ in range(experts)]
+
+    def to_slots(rows):
+        parts, at = [], 0
+        for size in sizes:
+            slot = jnp.arange(at, at + size)[:, None]
+            hot = (slot == place[None, :, 0]) | (slot == place[None, :, 1])
+            parts.append(dot_f32(hot.astype(bf16), rows, 1, 0).astype(bf16))
+            at += size
+        return parts
+
+    forward, mixed = [], []
+    cot_slots = to_slots(cotangent)
+    slots_a, slots_b = cot_slots[:experts], cot_slots[experts:]
+    qkv[0], place, slots_a, slots_b, buck_rev, buck, kmask, qmask, hide = (
         lax.optimization_barrier(
-            (qkv[0], pick, slots_a, slots_b, buck_rev, buck, kmask, kmask_t, qmask, hide)
+            (qkv[0], place, slots_a, slots_b, buck_rev, buck, kmask, qmask, hide)
         )
     )
-    part_width = width // heads
+    normed_seq = lax.all_gather(after(normed, qkv[0]), pair, axis=0, tiled=True)
     for h in range(heads):
-        arg = after(qkv[h], *forward, *normed_seq)
-        piece = after(normed[:, h * part_width : (h + 1) * part_width], arg)
-        normed_seq.append(lax.all_gather(piece, pair, axis=0, tiled=True))
+        arg = after(qkv[h], forward)
         if h == heads - 1:
             grad_a = exchange(after(slots_a, arg))
         out = attention_fwd(order, chunks, table_dev[:, h], buck_rev, kmask, qmask, arg, step_k)
-        if h == heads - 1:
-            out = after(out, normed_seq, grad_a)
+        out = after(out, qkv[h + 1] if h < heads - 1 else grad_a, mixed)
         forward.append(out)
         mixed.append(swap_blocks(out[0], pair).reshape(groups * HEAD_DIM, tok))
-    out_heads = out_weight.reshape(groups, heads, HEAD_DIM, width)
-    out_weights = [out_heads[:, h].reshape(groups * HEAD_DIM, width) for h in range(heads)]
-    branch = sum(dot_f32(m, w, 0, 0) for m, w in zip(mixed, out_weights))
-    middle = inputs + branch
-    normed_moe_f, norm_moe_back = jax.vjp(rms_scale, middle, moe_gain)
-    normed_moe = normed_moe_f.astype(bf16)
-
-    arrived = [exchange(to_slots(normed_moe, 0))]
-    arrived.append(exchange(to_slots(after(normed_moe, arrived[0][0]), 1)))
-    logits = jnp.dot(normed_moe.astype(f32), router_weight.astype(f32), precision=highest)
-    probs = jax.nn.softmax(logits, axis=-1)
-    gate_vals = jnp.sum(probs[:, None, :] * choose, axis=2)
-    gate_slots = [
-        [
-            jnp.sum(
-                first.astype(f32) * gate_vals[None, :, 0]
-                + second.astype(f32) * gate_vals[None, :, 1],
-                axis=1,
-            )
-            for first, second in part
-        ]
-        for part in pick
-    ]
-    sent_gates = [jnp.concatenate(both) for both in zip(*gate_slots)]
-    gates = jnp.stack(exchange(sent_gates))
-
-    x_a, x_b = [jnp.concatenate(part, axis=0) for part in arrived]
-    gate_rows = [gates[:, low:high].reshape(-1, 1) for low, high in spans]
+    mixed = after(mixed, forward)
+    middle, normed_moe, probs, *sent = route(
+        layer_input, place, expert_ids, moe_gain, router_weight, out_weight, mixed, sizes
+    )
+    x_a, x_b = exchange(sent[:experts]), exchange(sent[experts:])
+
     grad_b = exchange(after(slots_b, x_a))
-    run_a = expert_fwd(x_a, expert_in, expert_down, experts)
-    run_b = expert_fwd(after(x_b, run_a, grad_b), expert_in, expert_down, experts)
+    run_a = after(expert_fwd(x_a, expert_in, expert_down), x_b, grad_b)
     produced_a = exchange(list(run_a[3:]))
-    g_a, g_b = jnp.concatenate(grad_a, axis=0), jnp.concatenate(grad_b, axis=0)
+    run_b = expert_fwd(after(x_b, run_a), expert_in, expert_down)
+    run_b = after(run_b, produced_a, normed_seq)
+    produced_b = exchange(list(run_b[3:]))
     hidden = [run_a[0], run_b[0]]
     tiles = ff_width // 256
     cuts = (0, (tiles + 1) // 2, tiles)
-    g_args = after([g_a, g_b], run_b, produced_a)
-    down_1 = down_grad(ctx_arg, hidden, g_args, gate_rows, copies, 0, cuts[1])
-    produced_b = exchange(list(run_b[3:]))
-
-    def ctx_sum(own, other):
-        came = lax.ppermute(other, "ctx", [(0, 1), (1, 0)])
-        return (own.astype(f32) + came.astype(f32)).astype(bf16)
-
-    halves = [ctx_sum(*down_1)]
-    g_args = after([g_a, g_b], down_1)
-    down_2 = down_grad(ctx_arg, hidden, g_args, gate_rows, copies, cuts[1], tiles - cuts[1])
+    g_args = after(grad_a + grad_b, run_b)
+    down_1 = down_grad(ctx_arg, hidden, g_args, x_a + x_b, copies, 0, cuts[1])
+
+    def to_ctx(half):
+        return lax.ppermute(half, "ctx", [(0, 1), (1, 0)])
+
+    came = to_ctx(down_1[1])
+    g_args = after(grad_a + grad_b, down_1)
+    down_2 = down_grad(ctx_arg, hidden, g_args, x_a + x_b, copies, cuts[1], tiles - cuts[1])
     undo_a = expert_bwd(
-        after(g_a, down_2), gate_rows[0], run_a[1], run_a[2], expert_in, expert_down, experts
-    )
-    halves.append(ctx_sum(down_2[0], after(down_2[1], halves[0])))
+        after(grad_a, down_2), x_a, run_a[1], run_a[2], expert_in, expert_down
+    )
+    undo_a, came = lax.optimization_barrier((after(undo_a, produced_b), came))
+    halves = [add_low((down_1[0], came))]
+    grads_a = exchange(list(undo_a[1:]))
+    came = to_ctx(after(down_2[1], undo_a))
     undo_b = expert_bwd(
-        after(g_b, undo_a, halves[0], produced_b),
-        gate_rows[1], run_b[1], run_b[2], expert_in, expert_down, experts,
-    )
-    grads_a = exchange(list(undo_a[1:]))
+        after(grad_b, undo_a), x_b, run_b[1], run_b[2], expert_in, expert_down
+    )
+    undo_b, came = lax.optimization_barrier((after(undo_b, grads_a), came))
+    halves.append(add_low((down_2[0], came)))
+    grads_b = exchange(list(undo_b[1:]))
     grads_in = [undo_a[0], undo_b[0]]
-    bounds = (0, 2 * tiles * 4 // 11, 2 * tiles * 8 // 11, 2 * tiles)
-    xs = after([x_a, x_b], undo_b, grads_a)
-    in_1 = in_grad(ctx_arg, xs, grads_in, copies, bounds[0], bounds[1] - bounds[0])
-    grads_b = exchange(list(undo_b[1:]))
-    xs = after([x_a, x_b], in_1, halves[1])
-    in_2 = in_grad(ctx_arg, xs, grads_in, copies, bounds[1], bounds[2] - bounds[1])
-    halves.append(ctx_sum(in_1[0], after(in_1[1], halves[1])))
-    xs = after([x_a, x_b], in_2)
-    in_3 = in_grad(ctx_arg, xs, grads_in, copies, bounds[2], bounds[3] - bounds[2])
-    produced = after([produced_a, produced_b], in_3)
-    row_grad = after([grads_a, grads_b], in_3)
-
-    def from_slots(picks, slot_rows):
-        rows = jnp.concatenate([one for part in slot_rows for one in part], axis=0)
-        return dot_f32(jnp.concatenate([one for part in picks for one in part], axis=0), rows, 0, 0)
-
-    first_out = from_slots([[p[0] for p in part] for part in pick], produced)
-    second_out = from_slots([[p[1] for p in part] for part in pick], produced)
-    normed_moe_grad = from_slots([[p[0] + p[1] for p in part] for part in pick], row_grad)
-    moe_sum = gate_vals[:, 0:1] * first_out + gate_vals[:, 1:2] * second_out
-    layer_output = (middle + moe_sum).astype(bf16)
-    grad_out = cotangent.astype(f32)
-    gate_grad = jnp.stack(
-        [jnp.sum(grad_out * first_out, axis=1), jnp.sum(grad_out * second_out, axis=1)], axis=1
-    )
-    probs_grad = jnp.sum(gate_grad[:, :, None] * choose, axis=1)
-    logits_grad = probs * (probs_grad - jnp.sum(probs * probs_grad, axis=1, keepdims=True))
-    router_f = router_weight.astype(f32)
-    route_grad = jnp.dot(logits_grad, router_f.T, precision=highest)
-    middle_norm_grad, moe_gain_grad = norm_moe_back(normed_moe_grad + route_grad)
-    middle_grad = grad_out + middle_norm_grad
-    branch_grad = middle_grad.astype(bf16)
-    branch_grad = after(branch_grad, halves[2])
-    mixed_grad = [
-        swap_blocks(
-            dot_f32(w, branch_grad, 1, 1).astype(bf16).reshape(groups, HEAD_DIM, tok), pair
-        )
-        for w in out_weights
-    ]
-
-    out_grad = jnp.stack(
-        [dot_f32(m, branch_grad, 1, 0).astype(bf16).reshape(groups, HEAD_DIM, width) for m in mixed],
-        axis=1,
-    ).reshape(width, width)
-    wide_logits = jnp.pad(logits_grad, ((0, 0), (0, 128 - experts)))
-    router_grad = lax.dot_general(
-        normed_moe.astype(f32), wide_logits, (((0,), (0,)), ((), ())), precision=highest
-    )
-    lane = jnp.arange(128)[None, :]
-    small = jnp.where(lane == experts, moe_gain_grad[:, None], router_grad).astype(bf16)
+    share = 2 * tiles * 2 // 11
+    sizes = (share, 2 * tiles - 4 * share, share, 2 * share)
+    in_parts, first = [], 0
+    xs = after(x_a + x_b, undo_b)
+    for size in sizes:
+        in_parts.append(in_grad(ctx_arg, xs, grads_in, copies, first, size))
+        first += size
+        xs = after(x_a + x_b, in_parts[-1])
+        if len(in_parts) == 1:
+            came = to_ctx(after(in_parts[0][1], halves[1]))
+    in_parts[3], came, grads_b = lax.optimization_barrier((in_parts[3], came, grads_b))
+    halves.append(add_low((in_parts[0][0], came)))
+    came = to_ctx(after(in_parts[2][1], halves[2]))
+
+    produced, row_grad = after((produced_a + produced_b, grads_a + grads_b), in_parts)
+    layer_output, middle_grad, *outs = combine(
+        exp_arg, place, expert_ids, probs, middle, cotangent, normed_moe, moe_gain,
+        router_weight.T.astype(f32), out_weight, produced, row_grad, mixed, copies,
+    )
+    outs, came = lax.optimization_barrier((outs, came))
+    halves.append(add_low((in_parts[2][0], came)))
+    early = outs[heads:]
+    mixed_grad = [swap_blocks(part, pair) for part in outs[:heads]]
     rows_dev = width // (n_dp * groups)
-    early = jnp.concatenate([out_grad, small], axis=1)
-    early = early.reshape(copies, n_exp, rows_dev, width + 128)
 
     def sum_dp(half):
         return lax.psum_scatter(half, "dp", scatter_dimension=0, tiled=True)
 
-    summed = [sum_dp(halves[0]), sum_dp(halves[1])]
-    last_own, last_other = [sum_dp(half) for half in in_3]
+    down_sums = [sum_dp(halves[0]), sum_dp(halves[1])]
+    last_own, last_other = [sum_dp(half) for half in in_parts[1]]
+    in_sums = [sum_dp(halves[2]), None, sum_dp(halves[3]), None]
 
     buckets = bias_table.shape[0] // copies
     lanes = -(-(3 * HEAD_DIM + 1) // 128) * 128
-    backward, grads, late = [], [], []
+    backward, grads = [], []
     for h in range(heads):
-        arg = after(mixed_grad[h], backward, halves, summed)
+        arg = after(mixed_grad[h], backward)
+        beside = [grads[h - 1]] if h else []
         if h == 0:
-            halves.append(ctx_sum(in_2[0], after(in_2[1], arg)))
-            summed.append(sum_dp(halves[2]))
-            pieces = after(early, arg)
-            early_parts = exchange(
-                [
-                    lax.dynamic_index_in_dim(
-                        pieces, jnp.bitwise_xor(exp_index, d), 1, False
-                    ).reshape(-1, width + 128)
-                    for d in range(n_exp)
-                ]
-            )
-            early_sum = sum(part.astype(f32) for part in early_parts).astype(bf16)
-            early_half = sum_dp(early_sum).reshape(n_ctx, rows_dev, width + 128)
-        else:
-            arg = after(arg, early_parts, last_own, last_other)
-        out, offsets = attention_bwd(
-            order, chunks, table_dev[:, h], buck, kmask_t, hide, qkv[h], forward[h][0],
+            came = to_ctx(after(in_parts[3][1], arg))
+            early_parts = exchange(after(early, arg))
+            beside += [came, early_parts, last_own, last_other] + mixed_grad[1:2]
+        if h == heads - 1:
+            last_came = to_ctx(after(last_other, arg))
+            beside += [last_came, in_sums[0]] + ([early_parts] if h else [])
+        out = attention_bwd(
+            order, chunks, table_dev[:, h], buck, kmask, hide, qkv[h], forward[h][0],
             arg, forward[h][1], step_k,
         )
+        out, beside = lax.optimization_barrier((out, beside))
+        if h == 0:
+            came, early_parts = beside[0], beside[1]
+            in_sums[3] = sum_dp(add_low((in_parts[3][0], came)))
+            early_parts = scatter_dp(add_low(early_parts))
         if h == heads - 1:
-            summed.append(sum_dp(after(halves[3], arg)))
-            summed.append(ctx_sum(last_own, after(last_other, arg)))
-            out, offsets = after((out, offsets), grads, late, early_half, summed[4])
+            in_sums[1] = add_low((last_own, after(last_came, out)))
+            early_half = add_low(early_parts)
         backward.append(out)
-        grads.append(swap_blocks(out, pair))
-        columns = jnp.transpose(out, (1, 2, 0, 3)).reshape(3 * HEAD_DIM, groups * tok)
-        local_grad = jnp.concatenate(
-            [dot_f32(piece, columns, 0, 1) for piece in normed_seq], axis=0
-        )
+        grads.append(swap_blocks(out[0], pair))
+    packed = []
+    for out, offsets in backward:
+        columns = jnp.transpose(after(out, backward), (1, 2, 0, 3))
+        columns = columns.reshape(3 * HEAD_DIM, groups * tok)
+        local_grad = dot_f32(normed_seq, columns, 0, 1)
         table_grad = jnp.sum(offsets, axis=1)
         spread = jnp.pad(
             jnp.broadcast_to(
@@ -869,46 +1050,44 @@
         ).reshape(width, 1)
         local_grad = jnp.pad(local_grad, ((0, 0), (0, lanes - 3 * HEAD_DIM)))
         lane = jnp.arange(lanes)[None, :]
-        packed = jnp.where(lane == 3 * HEAD_DIM, spread, local_grad).astype(bf16)
-        late.append(sum_dp(packed))
+        packed.append(jnp.where(lane == 3 * HEAD_DIM, spread, local_grad).astype(bf16))
+    packed, grads = lax.optimization_barrier((jnp.concatenate(packed, axis=1), grads))
+    late = scatter_dp(packed)
     input_grad = input_gradient(layer_input, attn_gain, middle_grad, qkv_weight, grads)
+    input_grad, late = lax.optimization_barrier((input_grad, late))
+    late = add_low(late)
+    early_half = early_half.reshape(n_ctx, rows_dev, width + 128)
     early_own, early_other = [
         lax.dynamic_index_in_dim(early_half, at, 0, False) for at in (ctx_index, 1 - ctx_index)
     ]
     early_rows = early_own.astype(f32) + lax.ppermute(
         early_other, "ctx", [(0, 1), (1, 0)]
     ).astype(f32)
-    expert_in_grad = jnp.concatenate(summed[2:], axis=1).astype(f32)
-    expert_down_grad = jnp.concatenate(summed[:2], axis=1).astype(f32)
-    rows_out = swap_blocks(
-        in_swap_order(jnp.concatenate(late, axis=1).reshape(groups, rows_dev, -1)), pair
-    )
-    late_rows = jnp.swapaxes(rows_out.reshape(groups, rows_dev, heads, lanes), 1, 2)
-    qkv_grad = (
-        jnp.transpose(
-            late_rows[..., : 3 * HEAD_DIM].reshape(groups, heads, rows_dev, 3, HEAD_DIM),
-            (2, 3, 0, 1, 4),
-        )
-        .reshape(rows_dev, 3 * width)
-        .astype(f32)
-    )
-    bias_rows = lax.dynamic_slice(
-        late_rows[..., 3 * HEAD_DIM], (exp_index * n_ctx, 0, 0), (n_ctx, heads, buckets)
-    )
-    bias_grad = bias_rows.reshape(head_exp, buckets).T.astype(f32)
+    expert_in_grad = jnp.concatenate(in_sums, axis=1).astype(f32)
+    expert_down_grad = jnp.concatenate(down_sums, axis=1).astype(f32)
+    rows_out = swap_blocks(in_swap_order(late.reshape(groups, rows_dev, -1)), pair)
     my_rows = ((lax.axis_index("dp") * n_ctx + ctx_index) * n_exp + exp_index) * rows_dev
-    attn_gain_grad = jnp.sum(
-        lax.dynamic_slice_in_dim(qkv_weight, my_rows, rows_dev, 0).astype(f32) * qkv_grad, axis=1
-    ) / lax.dynamic_slice_in_dim(attn_gain, my_rows, rows_dev, 0)
+    qkv_grad, attn_gain_grad, bias_rows = finish(
+        exp_arg,
+        rows_out,
+        lax.dynamic_slice_in_dim(qkv_weight, my_rows, rows_dev, 0),
+        lax.dynamic_slice_in_dim(attn_gain, my_rows, rows_dev, 0).reshape(rows_dev, 1),
+        heads,
+        lanes,
+        n_ctx,
+    )
+    router_grad = sum(
+        early_rows[:, width + i * experts : width + (i + 1) * experts] for i in range(3)
+    )
     return (
         layer_output,
         input_grad,
-        attn_gain_grad,
+        attn_gain_grad.reshape(rows_dev),
         qkv_grad,
         early_rows[:, :width],
-        bias_grad,
-        early_rows[:, width + experts],
-        early_rows[:, width : width + experts],
+        bias_rows[:buckets],
+        early_rows[:, width + 3 * experts],
+        router_grad,
         expert_in_grad[None],
         expert_down_grad,
     )

time: 709 us -> 621 us (0.88)
  the two profiles are of different devices: /device:TPU:0 before, /device:TPU:9 now
where the time goes in v1:
time: 621 us; the launch traced here: 612 us
  Pallas kernels  371 us (60%)
  waiting for transfers between devices  78.8 us (13%)
  starting transfers between devices  74.8 us (12%)
  other arithmetic  28.2 us (5%)
  local copies, waits for them, and re-layouts  23.8 us (4%)
  matrix products  20 us (3%)
  between operations  15.3 us (2%)
    pallas_call x2, Pallas kernels, attention_bwd(): pl.pallas_call(functools.partial(attention_bwd_kernel, bk, order), grid_s...  96.2 us
    pallas_call x2, Pallas kernels, attention_fwd(): pl.pallas_call(functools.partial(attention_fwd_kernel, bk, order), grid_s...  65.4 us
    pallas_call x2, Pallas kernels, expert_bwd(): pl.pallas_call(functools.partial(expert_bwd_kernel, steps, groups), grid=...  60.9 us
    ppermute x33, waiting for transfers between devices, exchange(): lax.ppermute(parts[d], axis, [(i, i ^ d) for i in range(n)])  44.9 us
    pallas_call x2, Pallas kernels, expert_fwd(): pl.pallas_call(functools.partial(expert_fwd_kernel, steps, groups), grid=...  43.2 us
    all_to_all x9, starting transfers between devices, swap_blocks(): return lax.all_to_all(blocks, axes, split_axis=0, concat_axis=0, tiled=True)  41.9 us
    pallas_call x4, Pallas kernels, in_grad(): pl.pallas_call(functools.partial(in_grad_kernel, copies, len(xs)), grid_s...  41.2 us
    ppermute x33, starting transfers between devices, exchange(): lax.ppermute(parts[d], axis, [(i, i ^ d) for i in range(n)])  25.4 us
  transfers between devices with their start and end apart: 57, of which 15 were waited for; matrix products, arithmetic and copies ran while one was open for 10% of the time, Pallas kernels for 59%

profile of v1, /device:TPU:9, one launch (start us, length us, event | category | flops | bytes accessed | tf_op | source)
XLA Modules:
  0.0 612.0 jit_solution(4635599416757754439)
XLA Ops:
  7.2 9.0 %project.1 = (bf16[512,1024]{1,0:T(8,128)(2,1)}, bf16[8,3,64,512]{3,2,1,0:T(8,128)(2,1)}, bf16[8,3,64,512]{3,2,1,0:T(8,128)(2,1)}) custom-call(bf16[512,1024]{1,0:T(8,128)(2,1)} %x_ref.5, f32[1,1024]{1,0:T(1,128)} %bitcast.97, bf16[1024,3072]{1,0:T(8,128)(2,1)} %w_ref.3), custom_call_target="tpu_custom_call" | custom-call | flops 3221225472 | bytes 11534336 | tf_op jit(solution)/shard_map/project/pallas_call | solution.py:518
  49.0 32.8 %attention_fwd.2 = (bf16[8,64,512]{2,1,0:T(8,128)(2,1)}, f32[8,1,512]{2,1,0:T(1,128)}) custom-call(s32[8]{0:T(128)} %and_select_fusion.nch_ref, f32[32]{0:T(128)} %get-tuple-element.574.tab_ref, s32[8,8192]{1,0:T(8,128)} %broadcast_in_dim.101.buck_ref, bf16[64,4096]{1,0:T(8,128)(2,1)} %maximum_maximum_fusion.kmask_ref, ...), custom_call_target="tpu_custom_call" | custom-call | flops 16777216000 | bytes 2097152 | tf_op jit(solution)/shard_map/attention_fwd/pallas_call | solution.py:92
  88.2 32.6 %attention_fwd.3 = (bf16[8,64,512]{2,1,0:T(8,128)(2,1)}, f32[8,1,512]{2,1,0:T(1,128)}) custom-call(s32[8]{0:T(128)} %and_select_fusion.nch_ref, f32[32]{0:T(128)} %get-tuple-element.573.tab_ref, s32[8,8192]{1,0:T(8,128)} %broadcast_in_dim.101.buck_ref, bf16[64,4096]{1,0:T(8,128)(2,1)} %maximum_maximum_fusion.kmask_ref, ...), custom_call_target="tpu_custom_call" | custom-call | flops 16777216000 | bytes 2097152 | tf_op jit(solution)/shard_map/attention_fwd/pallas_call | solution.py:92
  131.3 6.3 %all-to-all-done.3 = bf16[8,64,512]{2,1,0:T(8,128)(2,1)S(1)} async-done(((bf16[8,64,512]{2,1,0:T(8,128)(2,1)}), bf16[8,64,512]{2,1,0:T(8,128)(2,1)S(1)}, u32[]{:S(2)}, u32[]{:S(2)}) %all-to-all-start.3) | async-done | bytes 524320 | tf_op jit(solution)/shard_map/all_to_all | solution.py:804
  138.3 7.9 %route.1 = (f32[512,1024]{1,0:T(8,128)}, bf16[512,1024]{1,0:T(8,128)(2,1)}, f32[512,4]{1,0:T(8,128)}, bf16[160,1152]{1,0:T(8,128)(2,1)}, bf16[160,1152]{1,0:T(8,...) custom-call(bf16[512,1024]{1,0:T(8,128)(2,1)} %x_ref.5, ...), custom_call_target="tpu_custom_call" | custom-call | flops 2415919104 | bytes 8388608 | tf_op jit(solution)/shard_map/route/pallas_call | solution.py:783
  151.0 6.5 %collective-permute-done.4.refs_2_.refs_10_.refs_6_ = bf16[160,1152]{1,0:T(8,128)(2,1)S(1)} collective-permute-done((bf16[160,1152]{1,0:T(8,128)(2,1)}, bf16[160,1152]{1,0:T(8,128)(2,1)S(1)}, u32[]{:S(2)}, u32[]{:S(2)}) %collective-permute-start.4) | collective-permute-done | bytes 368672 | tf_op jit(solution)/shard_map/ppermute | solution.py:810
  157.5 8.5 %collective-permute-done.5.refs_3_.refs_11_.refs_7_ = bf16[160,1152]{1,0:T(8,128)(2,1)S(1)} collective-permute-done((bf16[160,1152]{1,0:T(8,128)(2,1)}, bf16[160,1152]{1,0:T(8,128)(2,1)S(1)}, u32[]{:S(2)}, u32[]{:S(2)}) %collective-permute-start.5) | collective-permute-done | bytes 368672 | tf_op jit(solution)/shard_map/ppermute | solution.py:810
  167.9 21.6 %expert_fwd.2 = (bf16[640,2816]{1,0:T(8,128)(2,1)}, bf16[640,2816]{1,0:T(8,128)(2,1)}, bf16[640,2816]{1,0:T(8,128)(2,1)}, bf16[160,1024]{1,0:T(8,128)(2,1)}, bf1...) custom-call(bf16[1,1024,5632]{2,1,0:T(8,128)(2,1)} %wu_ref.7, ...), custom_call_target="tpu_custom_call" | custom-call | flops 18454937600 | bytes 30736384 | tf_op jit(solution)/shard_map/expert_fwd/pallas_call | solution.py:307
  189.6 5.8 collective-permute-done.11.refs_7_.refs_3_
  197.9 21.6 %expert_fwd.3 = (bf16[640,2816]{1,0:T(8,128)(2,1)}, bf16[640,2816]{1,0:T(8,128)(2,1)}, bf16[640,2816]{1,0:T(8,128)(2,1)}, bf16[160,1024]{1,0:T(8,128)(2,1)}, bf1...) custom-call(bf16[1,1024,5632]{2,1,0:T(8,128)(2,1)} %wu_ref.7, ...), custom_call_target="tpu_custom_call" | custom-call | flops 18454937600 | bytes 30736384 | tf_op jit(solution)/shard_map/expert_fwd/pallas_call | solution.py:307
  221.9 9.8 %down_grad.2 = (bf16[4,1536,128]{2,1,0:T(8,128)(2,1)}, bf16[4,1536,128]{2,1,0:T(8,128)(2,1)}) custom-call(s32[1]{0:T(128)} %bitcast.12.ctx_ref, bf16[160,1024]{1,0:T(8,128)(2,1)} %convolution_convert_fusion.7.refs_0_, bf16[160,1024]{1,0:T(8,128)(2,1)} %copy-done.50, bf16[160,1024]{1,0:T(8,128)(2,1)} %collective-permute-done.1.refs_2_, ...), custom_call_target="tpu_custom_call" | custom-call | flops 8053063680 | bytes 9699328 | tf_op jit(solution)/shard_map/down_grad/pallas_call | solution.py:476
  232.5 8.7 %down_grad.3 = (bf16[4,1280,128]{2,1,0:T(8,128)(2,1)}, bf16[4,1280,128]{2,1,0:T(8,128)(2,1)}) custom-call(s32[1]{0:T(128)} %bitcast.12.ctx_ref, bf16[160,1024]{1,0:T(8,128)(2,1)} %convolution_convert_fusion.7.refs_0_, bf16[160,1024]{1,0:T(8,128)(2,1)} %copy-done.50, bf16[160,1024]{1,0:T(8,128)(2,1)} %collective-permute-done.1.refs_2_, ...), custom_call_target="tpu_custom_call" | custom-call | flops 6710886400 | bytes 8519680 | tf_op jit(solution)/shard_map/down_grad/pallas_call | solution.py:476
  241.3 25.5 %expert_bwd.2 = (bf16[2,640,2816]{2,1,0:T(8,128)(2,1)}, bf16[160,1024]{1,0:T(8,128)(2,1)}, bf16[160,1024]{1,0:T(8,128)(2,1)}, bf16[160,1024]{1,0:T(8,128)(2,1)}, bf16[160,1024]{1,0:T(8,128)(2,1)}) custom-call(bf16[640,2816]{1,0:T(8,128)(2,1)} %get-tuple-element.323.act_ref, bf16[640,2816]{1,0:T(8,128)(2,1)} %get-tuple-element.324.slope_ref, ...), custom_call_target="tpu_custom_call" | custom-call | flops 18454937600 | bytes 34340864 | tf_op jit(solution)/shard_map/expert_bwd/pallas_call | solution.py:362
  273.0 35.4 %expert_bwd.3 = (bf16[2,640,2816]{2,1,0:T(8,128)(2,1)}, bf16[160,1024]{1,0:T(8,128)(2,1)}, bf16[160,1024]{1,0:T(8,128)(2,1)}, bf16[160,1024]{1,0:T(8,128)(2,1)}, bf16[160,1024]{1,0:T(8,128)(2,1)}) custom-call(bf16[640,2816]{1,0:T(8,128)(2,1)} %get-tuple-element.343.act_ref, bf16[640,2816]{1,0:T(8,128)(2,1)} %get-tuple-element.344.slope_ref, ...), custom_call_target="tpu_custom_call" | custom-call | flops 18454937600 | bytes 34340864 | tf_op jit(solution)/shard_map/expert_bwd/pallas_call | solution.py:362
  310.7 8.6 %in_grad.4 = (bf16[512,1024]{1,0:T(8,128)(2,1)}, bf16[512,1024]{1,0:T(8,128)(2,1)}) custom-call(s32[1]{0:T(128)} %bitcast.12.ctx_ref, bf16[160,1152]{1,0:T(8,128)(2,1)} %get-tuple-element.434.refs_0_.refs_8_.refs_4_, bf16[160,1152]{1,0:T(8,128)(2,1)} %copy-done.40, bf16[160,1152]{1,0:T(8,128)(2,1)} %copy-done.41, bf16[160,1152]{1,0:T(8,128)(2,1)} %copy-done.42, ...), custom_call_target="tpu_custom_call" | custom-call | flops 5368709120 | bytes 7340032 | tf_op jit(solution)/shard_map/in_grad/pallas_call | solution.py:426
  319.3 10.7 %in_grad.5 = (bf16[512,1536]{1,0:T(8,128)(2,1)}, bf16[512,1536]{1,0:T(8,128)(2,1)}) custom-call(s32[1]{0:T(128)} %bitcast.12.ctx_ref, bf16[160,1152]{1,0:T(8,128)(2,1)} %get-tuple-element.434.refs_0_.refs_8_.refs_4_, bf16[160,1152]{1,0:T(8,128)(2,1)} %copy-done.40, bf16[160,1152]{1,0:T(8,128)(2,1)} %copy-done.41, bf16[160,1152]{1,0:T(8,128)(2,1)} %copy-done.42, ...), custom_call_target="tpu_custom_call" | custom-call | flops 8053063680 | bytes 9699328 | tf_op jit(solution)/shard_map/in_grad/pallas_call | solution.py:426
  333.7 8.6 %in_grad.6 = (bf16[512,1024]{1,0:T(8,128)(2,1)}, bf16[512,1024]{1,0:T(8,128)(2,1)}) custom-call(s32[1]{0:T(128)} %bitcast.12.ctx_ref, bf16[160,1152]{1,0:T(8,128)(2,1)} %get-tuple-element.434.refs_0_.refs_8_.refs_4_, bf16[160,1152]{1,0:T(8,128)(2,1)} %copy-done.40, bf16[160,1152]{1,0:T(8,128)(2,1)} %copy-done.41, bf16[160,1152]{1,0:T(8,128)(2,1)} %copy-done.42, ...), custom_call_target="tpu_custom_call" | custom-call | flops 5368709120 | bytes 7340032 | tf_op jit(solution)/shard_map/in_grad/pallas_call | solution.py:426
  342.3 13.3 %in_grad.7 = (bf16[512,2048]{1,0:T(8,128)(2,1)}, bf16[512,2048]{1,0:T(8,128)(2,1)}) custom-call(s32[1]{0:T(128)} %bitcast.12.ctx_ref, bf16[160,1152]{1,0:T(8,128)(2,1)} %get-tuple-element.434.refs_0_.refs_8_.refs_4_, bf16[160,1152]{1,0:T(8,128)(2,1)} %copy-done.40, bf16[160,1152]{1,0:T(8,128)(2,1)} %copy-done.41, bf16[160,1152]{1,0:T(8,128)(2,1)} %copy-done.42, ...), custom_call_target="tpu_custom_call" | custom-call | flops 10737418240 | bytes 12058624 | tf_op jit(solution)/shard_map/in_grad/pallas_call | solution.py:426
  362.1 15.6 %combine.1 = (bf16[512,1024]{1,0:T(8,128)(2,1)}, f32[512,1024]{1,0:T(8,128)}, bf16[8,64,512]{2,1,0:T(8,128)(2,1)}, bf16[8,64,512]{2,1,0:T(8,128)(2,1)}, bf16[256...) custom-call(s32[1]{0:T(128)} %bitcast.exp_ref, ...), custom_call_target="tpu_custom_call" | custom-call | flops 6174015488 | bytes 18874368 | tf_op jit(solution)/shard_map/combine/pallas_call | solution.py:684
  377.7 5.5 collective-permute-done.27
  383.2 5.0 all-to-all-start.4
  391.2 5.7 all-to-all-done.4.do_ref
  396.8 5.0 all-to-all-start.5
  405.4 48.2 %attention_bwd.2 = (bf16[8,3,64,512]{3,2,1,0:T(8,128)(2,1)}, f32[32,128]{1,0:T(8,128)}) custom-call(s32[8]{0:T(128)} %and_select_fusion.nch_ref, f32[32]{0:T(128)} %get-tuple-element.574.tab_ref, s32[8,8192]{1,0:T(8,128)} %broadcast_in_dim.102.buck_ref, bf16[64,4096]{1,0:T(8,128)(2,1)} %maximum_maximum_fusion.kmask_ref, ...), custom_call_target="tpu_custom_call" | custom-call | flops 41943040000 | bytes 4194304 | tf_op jit(solution)/shard_map/attention_bwd/pallas_call | solution.py:209
  475.3 5.7 collective-permute-done.35
  482.3 48.1 %attention_bwd.3 = (bf16[8,3,64,512]{3,2,1,0:T(8,128)(2,1)}, f32[32,128]{1,0:T(8,128)}) custom-call(s32[8]{0:T(128)} %and_select_fusion.nch_ref, f32[32]{0:T(128)} %get-tuple-element.573.tab_ref, s32[8,8192]{1,0:T(8,128)} %broadcast_in_dim.102.buck_ref, bf16[64,4096]{1,0:T(8,128)(2,1)} %maximum_maximum_fusion.kmask_ref, ...), custom_call_target="tpu_custom_call" | custom-call | flops 41943040000 | bytes 4194304 | tf_op jit(solution)/shard_map/attention_bwd/pallas_call | solution.py:209
  533.7 5.4 all-to-all-start.7
  543.8 5.2 fusion.49
  549.0 5.2 fusion.48
  562.2 11.0 %input_grad.1 = f32[512,1024]{1,0:T(8,128)} custom-call(bf16[512,1024]{1,0:T(8,128)(2,1)} %x_ref.5, f32[1,1024]{1,0:T(1,128)} %bitcast.98, f32[512,1024]{1,0:T(8,128)} %get-tuple-element.469.mid_ref, bf16[1024,3072]{1,0:T(8,128)(2,1)} %w_ref.3, bf16[8,3,64,512]{3,2,1,0:T(8,128)(2,1)} %copy-done.4, bf16[8,3,64,512]{3,2,1,0:T(8,128)(2,1)} %all-to-all-done.7.refs_1_), custom_call_target="tpu_custom_call" | custom-call | flops 3221225472 | bytes 14680064 | tf_op jit(solution)/shard_map/input_grad/pallas_call | solution.py:565
  573.3 11.1 %collective-permute-done.38 = bf16[256,512]{1,0:T(8,128)(2,1)S(1)} collective-permute-done((bf16[256,512]{1,0:T(8,128)(2,1)S(1)}, bf16[256,512]{1,0:T(8,128)(2,1)S(1)}, u32[]{:S(2)}, u32[]{:S(2)}) %collective-permute-start.38) | collective-permute-done | bytes 262176 | tf_op jit(solution)/shard_map/ppermute | solution.py:810
  585.3 5.3 all-to-all-start.8
  (317 shorter events, 141.4 us)
Async XLA Ops:
  20.8 198.9 %all-gather.2.cloned.1.call-start = ((), (), s32[]{:S(2)}) async-start(), calls=%async_computation.16 | async-start | bytes 9437184 | tf_op jit(solution)/shard_map/all_gather | solution.py:933
  42.0 39.8 %all-to-all-start.1 = ((bf16[8,3,64,512]{3,2,1,0:T(8,128)(2,1)}), bf16[8,3,64,512]{3,2,1,0:T(8,128)(2,1)S(1)}, u32[]{:S(2)}, u32[]{:S(2)}) async-start(bf16[8,3,64,512]{3,2,1,0:T(8,128)(2,1)} %get-tuple-element.274), calls=%async_computation.1 | async-start | bytes 3145728 | tf_op jit(solution)/shard_map/all_to_all | solution.py:804
  81.8 44.0 %all-to-all-start.2 = ((bf16[8,64,512]{2,1,0:T(8,128)(2,1)}), bf16[8,64,512]{2,1,0:T(8,128)(2,1)S(1)}, u32[]{:S(2)}, u32[]{:S(2)}) async-start(bf16[8,64,512]{2,1,0:T(8,128)(2,1)} %get-tuple-element.275.o_ref), calls=%async_computation.2 | async-start | bytes 1048576 | tf_op jit(solution)/shard_map/all_to_all | solution.py:804
  86.0 34.7 %collective-permute-start = (bf16[160,1024]{1,0:T(8,128)(2,1)S(1)}, bf16[160,1024]{1,0:T(8,128)(2,1)S(1)}, u32[]{:S(2)}, u32[]{:S(2)}) collective-permute-start(bf16[160,1024]{1,0:T(8,128)(2,1)S(1)} %copy-done.26), channel_id=1, source_target_pairs={{0,1},{1,0},{2,3},{3,2},{4,5},{5,4},{6,7},{7,6},{8,9},{9,8},{10,11... | collective-permute-start | bytes 983048 | tf_op jit(solution)/shard_map/ppermute | solution.py:810
  86.1 34.7 %collective-permute-start.1 = (bf16[160,1024]{1,0:T(8,128)(2,1)S(1)}, bf16[160,1024]{1,0:T(8,128)(2,1)}, u32[]{:S(2)}, u32[]{:S(2)}) collective-permute-start(bf16[160,1024]{1,0:T(8,128)(2,1)S(1)} %copy-done.25), channel_id=1, source_target_pairs={{0,2},{1,3},{2,0},{3,1},{4,6},{5,7},{6,4},{7,5},{8,10},{9,11},{10,... | collective-permute-start | bytes 983048 | tf_op jit(solution)/shard_map/ppermute | solution.py:810
  87.8 38.0 %collective-permute-start.2 = (bf16[160,1024]{1,0:T(8,128)(2,1)S(1)}, bf16[160,1024]{1,0:T(8,128)(2,1)}, u32[]{:S(2)}, u32[]{:S(2)}) collective-permute-start(bf16[160,1024]{1,0:T(8,128)(2,1)S(1)} %copy-done.24), channel_id=1, source_target_pairs={{0,3},{1,2},{2,1},{3,0},{4,7},{5,6},{6,5},{7,4},{8,11},{9,10},{10,... | collective-permute-start | bytes 983048 | tf_op jit(solution)/shard_map/ppermute | solution.py:810
  129.3 324.4 %reduce-scatter.18.cloned.1.call-start = ((), (), s32[]{:S(2)}) async-start(), calls=%async_computation.22 | async-start | bytes 1966080 | tf_op jit(solution)/shard_map/reduce_scatter | solution.py:1006
  149.0 40.6 %collective-permute-start.7 = (bf16[160,1152]{1,0:T(8,128)(2,1)}, bf16[160,1152]{1,0:T(8,128)(2,1)S(1)}, u32[]{:S(2)}, u32[]{:S(2)}) collective-permute-start(bf16[160,1152]{1,0:T(8,128)(2,1)} %get-tuple-element.308), channel_id=1, source_target_pairs={{0,2},{1,3},{2,0},{3,1},{4,6},{5,7},{6,4},{7,5},{8,10},{9,11},{10,... | collective-permute-start | bytes 1105928 | tf_op jit(solution)/shard_map/ppermute | solution.py:810
  149.3 40.2 %collective-permute-start.8 = (bf16[160,1152]{1,0:T(8,128)(2,1)}, bf16[160,1152]{1,0:T(8,128)(2,1)S(1)}, u32[]{:S(2)}, u32[]{:S(2)}) collective-permute-start(bf16[160,1152]{1,0:T(8,128)(2,1)} %get-tuple-element.309), channel_id=1, source_target_pairs={{0,3},{1,2},{2,1},{3,0},{4,7},{5,6},{6,5},{7,4},{8,11},{9,10},{10,... | collective-permute-start | bytes 1105928 | tf_op jit(solution)/shard_map/ppermute | solution.py:810
  166.5 28.8 %collective-permute-start.11 = (bf16[160,1024]{1,0:T(8,128)(2,1)S(1)}, bf16[160,1024]{1,0:T(8,128)(2,1)S(1)}, u32[]{:S(2)}, u32[]{:S(2)}) collective-permute-start(bf16[160,1024]{1,0:T(8,128)(2,1)S(1)} %copy-done.21), channel_id=1, source_target_pairs={{0,3},{1,2},{2,1},{3,0},{4,7},{5,6},{6,5},{7,4},{8,11},{9,10},{10,... | collective-permute-start | bytes 983048 | tf_op jit(solution)/shard_map/ppermute | solution.py:810
  219.7 47.1 %collective-permute-start.15 = (bf16[160,1024]{1,0:T(8,128)(2,1)}, bf16[160,1024]{1,0:T(8,128)(2,1)S(1)}, u32[]{:S(2)}, u32[]{:S(2)}) collective-permute-start(bf16[160,1024]{1,0:T(8,128)(2,1)} %get-tuple-element.339), channel_id=1, source_target_pairs={{0,1},{1,0},{2,3},{3,2},{4,5},{5,4},{6,7},{7,6},{8,9},{9,8},{10,11... | collective-permute-start | bytes 983048 | tf_op jit(solution)/shard_map/ppermute | solution.py:810
  219.7 47.0 %collective-permute-start.16 = (bf16[160,1024]{1,0:T(8,128)(2,1)}, bf16[160,1024]{1,0:T(8,128)(2,1)}, u32[]{:S(2)}, u32[]{:S(2)}) collective-permute-start(bf16[160,1024]{1,0:T(8,128)(2,1)} %get-tuple-element.340), channel_id=1, source_target_pairs={{0,2},{1,3},{2,0},{3,1},{4,6},{5,7},{6,4},{7,5},{8,10},{9,11},{10,... | collective-permute-start | bytes 983048 | tf_op jit(solution)/shard_map/ppermute | solution.py:810
  220.0 46.8 %collective-permute-start.17 = (bf16[160,1024]{1,0:T(8,128)(2,1)}, bf16[160,1024]{1,0:T(8,128)(2,1)}, u32[]{:S(2)}, u32[]{:S(2)}) collective-permute-start(bf16[160,1024]{1,0:T(8,128)(2,1)} %get-tuple-element.341), channel_id=1, source_target_pairs={{0,3},{1,2},{2,1},{3,0},{4,7},{5,6},{6,5},{7,4},{8,11},{9,10},{10,... | collective-permute-start | bytes 983048 | tf_op jit(solution)/shard_map/ppermute | solution.py:810
  231.7 36.4 %collective-permute-start.18 = (bf16[4,1536,128]{2,1,0:T(8,128)(2,1)}, bf16[4,1536,128]{2,1,0:T(8,128)(2,1)S(1)}, u32[]{:S(2)}, u32[]{:S(2)}) collective-permute-start(bf16[4,1536,128]{2,1,0:T(8,128)(2,1)} %get-tuple-element.354), channel_id=1, source_target_pairs={{0,4},{4,0},{1,5},{5,1},{2,6},{6,2},{3,7},{7,3},{8,12},{12,8},{9,1... | collective-permute-start | bytes 4718600 | tf_op jit(solution)/shard_map/ppermute | solution.py:961
  269.7 184.0 %reduce-scatter.20.cloned.1.call-start = ((), (), s32[]{:S(2)}) async-start(), calls=%async_computation.23 | async-start | bytes 1638400 | tf_op jit(solution)/shard_map/reduce_scatter | solution.py:1006
  269.7 38.6 %collective-permute-start.19 = (bf16[160,1024]{1,0:T(8,128)(2,1)}, bf16[160,1024]{1,0:T(8,128)(2,1)S(1)}, u32[]{:S(2)}, u32[]{:S(2)}) collective-permute-start(bf16[160,1024]{1,0:T(8,128)(2,1)} %get-tuple-element.380), channel_id=1, source_target_pairs={{0,1},{1,0},{2,3},{3,2},{4,5},{5,4},{6,7},{7,6},{8,9},{9,8},{10,11... | collective-permute-start | bytes 983048 | tf_op jit(solution)/shard_map/ppermute | solution.py:810
  270.5 37.9 %collective-permute-start.20 = (bf16[160,1024]{1,0:T(8,128)(2,1)}, bf16[160,1024]{1,0:T(8,128)(2,1)S(1)}, u32[]{:S(2)}, u32[]{:S(2)}) collective-permute-start(bf16[160,1024]{1,0:T(8,128)(2,1)} %get-tuple-element.381), channel_id=1, source_target_pairs={{0,2},{1,3},{2,0},{3,1},{4,6},{5,7},{6,4},{7,5},{8,10},{9,11},{10,... | collective-permute-start | bytes 983048 | tf_op jit(solution)/shard_map/ppermute | solution.py:810
  270.5 38.0 %collective-permute-start.21 = (bf16[160,1024]{1,0:T(8,128)(2,1)}, bf16[160,1024]{1,0:T(8,128)(2,1)S(1)}, u32[]{:S(2)}, u32[]{:S(2)}) collective-permute-start(bf16[160,1024]{1,0:T(8,128)(2,1)} %get-tuple-element.382), channel_id=1, source_target_pairs={{0,3},{1,2},{2,1},{3,0},{4,7},{5,6},{6,5},{7,4},{8,11},{9,10},{10,... | collective-permute-start | bytes 983048 | tf_op jit(solution)/shard_map/ppermute | solution.py:810
  272.2 36.3 %collective-permute-start.22 = (bf16[4,1280,128]{2,1,0:T(8,128)(2,1)}, bf16[4,1280,128]{2,1,0:T(8,128)(2,1)S(1)}, u32[]{:S(2)}, u32[]{:S(2)}) collective-permute-start(bf16[4,1280,128]{2,1,0:T(8,128)(2,1)} %get-tuple-element.398), channel_id=1, source_target_pairs={{0,4},{4,0},{1,5},{5,1},{2,6},{6,2},{3,7},{7,3},{8,12},{12,8},{9,1... | collective-permute-start | bytes 3932168 | tf_op jit(solution)/shard_map/ppermute | solution.py:961
  310.7 145.4 %reduce-scatter.10.cloned.1.call-start = ((), (), s32[]{:S(2)}) async-start(), calls=%async_computation.18 | async-start | bytes 1966080 | tf_op jit(solution)/shard_map/reduce_scatter | solution.py:1006
  330.1 126.0 %reduce-scatter.8.cloned.1.call-start = ((), (), s32[]{:S(2)}) async-start(), calls=%async_computation.17 | async-start | bytes 1966080 | tf_op jit(solution)/shard_map/reduce_scatter | solution.py:1006
  330.7 202.2 %reduce-scatter.12.cloned.1.call-start = ((), (), s32[]{:S(2)}) async-start(), calls=%async_computation.19 | async-start | bytes 1310720 | tf_op jit(solution)/shard_map/reduce_scatter | solution.py:1006
  388.3 213.6 %reduce-scatter.14.cloned.1.call-start = ((), (), s32[]{:S(2)}) async-start(), calls=%async_computation.20 | async-start | bytes 1310720 | tf_op jit(solution)/shard_map/reduce_scatter | solution.py:1006
  396.8 59.2 %all-to-all-start.5 = ((bf16[8,64,512]{2,1,0:T(8,128)(2,1)}), bf16[8,64,512]{2,1,0:T(8,128)(2,1)}, u32[]{:S(2)}, u32[]{:S(2)}) async-start(bf16[8,64,512]{2,1,0:T(8,128)(2,1)} %get-tuple-element.492), calls=%async_computation.7 | async-start | bytes 1048576 | tf_op jit(solution)/shard_map/all_to_all | solution.py:804
  401.8 54.2 %collective-permute-start.29 = (bf16[256,1152]{1,0:T(8,128)(2,1)}, bf16[256,1152]{1,0:T(8,128)(2,1)S(1)}, u32[]{:S(2)}, u32[]{:S(2)}) collective-permute-start(bf16[256,1152]{1,0:T(8,128)(2,1)} %get-tuple-element.489), channel_id=1, source_target_pairs={{0,1},{1,0},{2,3},{3,2},{4,5},{5,4},{6,7},{7,6},{8,9},{9,8},{10,11... | collective-permute-start | bytes 1769480 | tf_op jit(solution)/shard_map/ppermute | solution.py:810
  402.0 54.0 %collective-permute-start.30 = (bf16[256,1152]{1,0:T(8,128)(2,1)}, bf16[256,1152]{1,0:T(8,128)(2,1)}, u32[]{:S(2)}, u32[]{:S(2)}) collective-permute-start(bf16[256,1152]{1,0:T(8,128)(2,1)} %get-tuple-element.490), channel_id=1, source_target_pairs={{0,2},{1,3},{2,0},{3,1},{4,6},{5,7},{6,4},{7,5},{8,10},{9,11},{10,... | collective-permute-start | bytes 1769480 | tf_op jit(solution)/shard_map/ppermute | solution.py:810
  403.7 52.4 %collective-permute-start.31 = (bf16[256,1152]{1,0:T(8,128)(2,1)}, bf16[256,1152]{1,0:T(8,128)(2,1)}, u32[]{:S(2)}, u32[]{:S(2)}) collective-permute-start(bf16[256,1152]{1,0:T(8,128)(2,1)} %get-tuple-element.491), channel_id=1, source_target_pairs={{0,3},{1,2},{2,1},{3,0},{4,7},{5,6},{6,5},{7,4},{8,11},{9,10},{10,... | collective-permute-start | bytes 1769480 | tf_op jit(solution)/shard_map/ppermute | solution.py:810
  404.0 52.0 %collective-permute-start.28 = (bf16[512,2048]{1,0:T(8,128)(2,1)}, bf16[512,2048]{1,0:T(8,128)(2,1)S(1)}, u32[]{:S(2)}, u32[]{:S(2)}) collective-permute-start(bf16[512,2048]{1,0:T(8,128)(2,1)} %get-tuple-element.483), channel_id=1, source_target_pairs={{0,4},{4,0},{1,5},{5,1},{2,6},{6,2},{3,7},{7,3},{8,12},{12,8},{9,1... | collective-permute-start | bytes 6291464 | tf_op jit(solution)/shard_map/ppermute | solution.py:961
  461.8 71.1 %all-to-all-start.6 = ((bf16[8,3,64,512]{3,2,1,0:T(8,128)(2,1)}), bf16[8,3,64,512]{3,2,1,0:T(8,128)(2,1)S(1)}, u32[]{:S(2)}, u32[]{:S(2)}) async-start(bf16[8,3,64,512]{3,2,1,0:T(8,128)(2,1)} %get-tuple-element.505), calls=%async_computation.8 | async-start | bytes 3145728 | tf_op jit(solution)/shard_map/all_to_all | solution.py:804
  466.5 135.4 %reduce-scatter.16.cloned.1.call-start = ((), (), s32[]{:S(2)}) async-start(), calls=%async_computation.21 | async-start | bytes 2621440 | tf_op jit(solution)/shard_map/reduce_scatter | solution.py:1006
  466.5 66.4 %collective-permute-start.32 = (bf16[128,1536]{1,0:T(8,128)(2,1)}, bf16[128,1536]{1,0:T(8,128)(2,1)}, u32[]{:S(2)}, u32[]{:S(2)}) collective-permute-start(bf16[128,1536]{1,0:T(8,128)(2,1)} %reduce-scatter.10.cloned.1.call-done), channel_id=1, source_target_pairs={{0,4},{4,0},{1,5},{5,1},{2,6},{6,2},{3,7},{7,3},{8,12},{12,8},{9,1... | collective-permute-start | bytes 1179656 | tf_op jit(solution)/shard_map/ppermute | solution.py:961
  481.1 49.7 %collective-permute-start.39 = (bf16[32,1152]{1,0:T(8,128)(2,1)S(1)}, bf16[32,1152]{1,0:T(8,128)(2,1)S(1)}, u32[]{:S(2)}, u32[]{:S(2)}) collective-permute-start(bf16[32,1152]{1,0:T(8,128)(2,1)S(1)} %dynamic-slice_bitcast_fusion.8), channel_id=1, source_target_pairs={{0,4},{4,0},{1,5},{5,1},{2,6},{6,2},{3,7},{7,3},{8,12},{12,8},{9,1... | collective-permute-start | bytes 221192 | tf_op jit(solution)/shard_map/ppermute | solution.py:1063
  (83 other events, 1315.3 us)
Sparse Core Ops, SparseCore 0:
  42.1 87.2 all-gather.1
  269.8 33.1 reduce-scatter.17
  310.8 28.5 reduce-scatter.19
  341.5 34.1 reduce-scatter.9
  377.9 34.2 reduce-scatter.7
  414.4 25.9 reduce-scatter.11
  442.8 28.2 reduce-scatter.13
  473.3 47.2 reduce-scatter.15

commit v2 on v1

--- a/solution.py
+++ b/solution.py
@@ -23,6 +23,10 @@
 
 def mm(left, right, dims):
     return lax.dot_general(left, right, dims, preferred_element_type=f32)
+
+
+def stack_refs(refs):
+    return jnp.concatenate([ref[...] for ref in refs], axis=0)
 
 
 def cost(flops, bytes_accessed, transcendentals=0):
@@ -267,7 +271,7 @@
 
 def expert_fwd_kernel(steps, groups, wg_ref, wu_ref, wd_ref, *refs):
     xs, refs = refs[:groups], refs[groups:]
-    h_ref, act_ref, slope_ref, *outs, rows, acc = refs
+    ht_ref, act_ref, slope_ref, *outs, rows, acc = refs
     f = pl.program_id(0)
 
     @pl.when(f == 0)
@@ -286,7 +290,7 @@
         0.7978845608028654 + 0.10703222440890037 * square
     )
     hidden = (act * up).astype(bf16)
-    h_ref[...] = hidden
+    ht_ref[...] = hidden.T
     act_ref[...] = act.astype(bf16)
     slope_ref[...] = (slope * up).astype(bf16)
     acc[...] += mm(hidden, wd_ref[0], NN)
@@ -313,8 +317,8 @@
             pl.BlockSpec((1, tile, width), lambda f: (0, f, 0)),
         ]
         + [pl.BlockSpec(xs[0].shape, lambda f: (0, 0))] * groups,
-        out_specs=[part, part, part] + [one] * groups,
-        out_shape=[inner, inner, inner]
+        out_specs=[pl.BlockSpec((tile, rows), lambda f: (f, 0)), part, part] + [one] * groups,
+        out_shape=[jax.ShapeDtypeStruct((ff, rows), bf16), inner, inner]
         + [jax.ShapeDtypeStruct((rows // groups, width), bf16)] * groups,
         scratch_shapes=[pltpu.VMEM((rows, width), bf16), pltpu.VMEM((rows, width), f32)],
         compiler_params=pltpu.CompilerParams(vmem_limit_bytes=60 << 20),
@@ -389,57 +393,66 @@
     return jnp.where(lax.rem(ctx + flip, 2) == 0, low, high)
 
 
-def in_grad_kernel(copies, n, ctx_ref, *refs):
-    xs, (*gs, own_ref, other_ref, xt) = refs[:n], refs[n:]
-    width = xt.shape[0]
-    blk = width // copies
-
-    @pl.when(pl.program_id(0) == 0)
-    def _():
-        at = 0
-        for x_ref in xs:
-            rows = x_ref.shape[0]
-            for flip in range(2):
-                for a in range(copies // 2):
-                    to = (flip * (copies // 2) + a) * blk
-                    xt[to : to + blk, at : at + rows] = column_block(
-                        x_ref, blk, ctx_ref[0], flip, a
-                    ).T
-            at += rows
-
+def turn_kernel(copies, ctx_ref, *refs):
+    xs, xt_ref = refs[:-1], refs[-1]
+    blk = xt_ref.shape[0] // copies
+    at = 0
+    for x_ref in xs:
+        rows = x_ref.shape[0]
+        for flip in range(2):
+            for a in range(copies // 2):
+                to = (flip * (copies // 2) + a) * blk
+                block = column_block(x_ref, blk, ctx_ref[0], flip, a)
+                xt_ref[to : to + blk, at : at + rows] = block.T
+        at += rows
+
+
+def turn(ctx, xs, copies):
+    width = xs[0].shape[1] - 128
+    total = sum(x.shape[0] for x in xs)
+    return pl.pallas_call(
+        functools.partial(turn_kernel, copies),
+        in_specs=[pl.BlockSpec(memory_space=pltpu.SMEM)]
+        + [pl.BlockSpec(memory_space=pltpu.VMEM)] * len(xs),
+        out_specs=pl.BlockSpec(memory_space=pltpu.VMEM),
+        out_shape=jax.ShapeDtypeStruct((width, total), bf16),
+        compiler_params=pltpu.CompilerParams(vmem_limit_bytes=60 << 20),
+        cost_estimate=cost(2 * total * width, 4 * total * width),
+        name="turn",
+    )(ctx, *xs)
+
+
+def in_grad_kernel(*refs):
+    x_refs, (*gs, own_ref, other_ref) = refs[:4], refs[4:]
     grads = jnp.concatenate([g[0] for g in gs], axis=0)
-    grad = mm(xt[...], grads, NN).astype(bf16)
-    own_ref[...] = grad[: width // 2]
-    other_ref[...] = grad[width // 2 :]
-
-
-def in_grad(ctx, xs, grads, copies, first, count, tile=256):
-    width = xs[0].shape[1] - 128
+    half = own_ref.shape[0]
+    grad = mm(stack_refs(x_refs), grads, NN).astype(bf16)
+    own_ref[...] = grad[:half]
+    other_ref[...] = grad[half:]
+
+
+def in_grad(xt, grads, first, count, tile=256):
+    width, total = xt.shape
     steps = grads[0].shape[2] // tile
-    total = sum(x.shape[0] for x in xs)
     half = jax.ShapeDtypeStruct((width // 2, count * tile), bf16)
-    out = pl.BlockSpec((width // 2, tile), lambda f, c: (0, f))
-
-    def at(f, c):
+    out = pl.BlockSpec((width // 2, tile), lambda f: (0, f))
+
+    def at(f):
         return ((f + first) // steps, 0, (f + first) % steps)
 
     return pl.pallas_call(
-        functools.partial(in_grad_kernel, copies, len(xs)),
-        grid_spec=pltpu.PrefetchScalarGridSpec(
-            num_scalar_prefetch=1,
-            grid=(count,),
-            in_specs=[pl.BlockSpec(x.shape, lambda f, c: (0, 0)) for x in xs]
-            + [pl.BlockSpec((1, g.shape[1], tile), at) for g in grads],
-            out_specs=[out, out],
-            scratch_shapes=[pltpu.VMEM((width, total), bf16)],
-        ),
+        in_grad_kernel,
+        grid=(count,),
+        in_specs=[pl.BlockSpec((width // 4, total), lambda f, i=i: (i, 0)) for i in range(4)]
+        + [pl.BlockSpec((1, g.shape[1], tile), at) for g in grads],
+        out_specs=[out, out],
         out_shape=[half, half],
         compiler_params=pltpu.CompilerParams(vmem_limit_bytes=60 << 20),
         cost_estimate=cost(
             4 * total * width * count * tile, 2 * (total + width) * count * tile + 2 * total * width
         ),
         name="in_grad",
-    )(ctx, *xs, *grads)
+    )(*[xt] * 4, *grads)
 
 
 def down_grad_kernel(copies, n, ctx_ref, *refs):
@@ -459,7 +472,7 @@
                     pg[at : at + rows, to : to + blk] = (block * gate).astype(bf16)
             at += rows
 
-    grad = mm(jnp.concatenate([h[...] for h in hs], axis=0), pg[...], TN).astype(bf16)
+    grad = mm(jnp.concatenate([h[...] for h in hs], axis=1), pg[...], NN).astype(bf16)
     for a in range(copies // 2):
         own_ref[a] = grad[:, a * blk : (a + 1) * blk]
         to = (copies // 2 + a) * blk
@@ -469,7 +482,7 @@
 def down_grad(ctx, hs, ps, xs, copies, first, count, tile=256):
     ff = count * tile
     width = ps[0].shape[1]
-    total = sum(h.shape[0] for h in hs)
+    total = sum(h.shape[1] for h in hs)
     blk = width // copies
     half = jax.ShapeDtypeStruct((copies // 2, ff, blk), bf16)
     out = pl.BlockSpec((copies // 2, tile, blk), lambda f, c: (0, f, 0))
@@ -480,7 +493,7 @@
             grid=(count,),
             in_specs=[pl.BlockSpec(p.shape, lambda f, c: (0, 0)) for p in ps]
             + [gate_block(x, width) for x in xs]
-            + [pl.BlockSpec((h.shape[0], tile), lambda f, c: (0, f + first)) for h in hs],
+            + [pl.BlockSpec((tile, h.shape[1]), lambda f, c: (f + first, 0)) for h in hs],
             out_specs=[out, out],
             scratch_shapes=[pltpu.VMEM((total, width), bf16)],
         ),
@@ -491,8 +504,8 @@
     )(ctx, *ps, *xs, *hs)
 
 
-def project_kernel(x_ref, gain_ref, w_ref, normed_ref, *refs):
-    outs, normed_t = refs[:-1], refs[-1]
+def project_kernel(x_ref, gain_ref, *refs):
+    w_refs, (normed_t, *outs) = refs[:4], refs[4:]
     heads = len(outs)
 
     @pl.when((pl.program_id(0) == 0) & (pl.program_id(1) == 0))
@@ -500,12 +513,11 @@
         x = x_ref[...].astype(f32)
         scale = lax.rsqrt(jnp.mean(x * x, axis=1, keepdims=True) + 1e-06)
         normed = (x * scale * gain_ref[...]).astype(bf16)
-        normed_ref[...] = normed
         normed_t[...] = normed.T
 
-    cols = w_ref.shape[1]
+    cols = w_refs[0].shape[1]
     tok = normed_t.shape[1]
-    rows = mm(w_ref[...], normed_t[...], TN).astype(bf16)
+    rows = mm(stack_refs(w_refs), normed_t[...], TN).astype(bf16)
     rows = rows.reshape(cols // (heads * HEAD_DIM), heads, HEAD_DIM, tok)
     for h in range(heads):
         outs[h][:, 0] = rows[:, h]
@@ -521,23 +533,25 @@
         in_specs=[
             pl.BlockSpec((tok, width), lambda p, j: (0, 0)),
             pl.BlockSpec((1, width), lambda p, j: (0, 0)),
-            pl.BlockSpec((width, cols), lambda p, j: (0, p * blocks + j)),
+        ]
+        + [
+            pl.BlockSpec((width // 4, cols), lambda p, j, i=i: (i, p * blocks + j))
+            for i in range(4)
         ],
-        out_specs=[pl.BlockSpec((tok, width), lambda p, j: (0, 0))]
+        out_specs=[pl.BlockSpec((width, tok), lambda p, j: (0, 0))]
         + [pl.BlockSpec((per, 1, HEAD_DIM, tok), lambda p, j: (j, p, 0, 0))] * heads,
-        out_shape=[jax.ShapeDtypeStruct((tok, width), bf16)]
+        out_shape=[jax.ShapeDtypeStruct((width, tok), bf16)]
         + [jax.ShapeDtypeStruct((groups, 3, HEAD_DIM, tok), bf16)] * heads,
-        scratch_shapes=[pltpu.VMEM((width, tok), bf16)],
         compiler_params=pltpu.CompilerParams(vmem_limit_bytes=60 << 20),
         cost_estimate=cost(6 * tok * width * width, 6 * width * width + 10 * tok * width),
         name="project",
-    )(x, gain.reshape(1, width), weight)
-
-
-def input_grad_kernel(steps, x_ref, gain_ref, mid_ref, w_ref, *refs):
-    grads, out_ref, acc = refs[:-2], refs[-2], refs[-1]
+    )(x, gain.reshape(1, width), *[weight] * 4)
+
+
+def input_grad_kernel(steps, x_ref, gain_ref, mid_ref, *refs):
+    w_refs, (*grads, out_ref, acc) = refs[:4], refs[4:]
     step = pl.program_id(0)
-    cols = w_ref.shape[1]
+    cols = w_refs[0].shape[1]
     tok = out_ref.shape[0]
 
     @pl.when(step == 0)
@@ -545,7 +559,7 @@
         acc[...] = jnp.zeros_like(acc)
 
     rows = jnp.stack([g[:, 0] for g in grads], axis=1).reshape(cols, tok)
-    acc[...] += mm(w_ref[...], rows, NN)
+    acc[...] += mm(stack_refs(w_refs), rows, NN)
 
     @pl.when(step == steps - 1)
     def _():
@@ -569,8 +583,8 @@
             whole,
             pl.BlockSpec((1, width), lambda s: (0, 0)),
             whole,
-            pl.BlockSpec((width, cols), lambda s: (0, s)),
         ]
+        + [pl.BlockSpec((width // 4, cols), lambda s, i=i: (i, s)) for i in range(4)]
         + [
             pl.BlockSpec((per, 1, HEAD_DIM, tok), lambda s: (s % blocks, s // blocks, 0, 0))
             for _ in grads
@@ -581,7 +595,7 @@
         compiler_params=pltpu.CompilerParams(vmem_limit_bytes=60 << 20),
         cost_estimate=cost(6 * tok * width * width, 6 * width * width + 16 * tok * width),
         name="input_grad",
-    )(x, gain.reshape(1, width), middle_grad, weight, *grads)
+    )(x, gain.reshape(1, width), middle_grad, *[weight] * 4, *grads)
 
 
 def wide_thirds(values):
@@ -796,6 +810,65 @@
       weight, *mixed)
 
 
+def sequence_grad_kernel(n_exp, copies, dp_ref, out_ref, offsets_ref, *refs):
+    normed_refs, (*shares, acc) = refs[:4], refs[4:]
+    step = pl.program_id(0)
+    width, lanes = acc.shape
+    own = 3 * HEAD_DIM
+
+    @pl.when(step == 0)
+    def _():
+        acc[...] = jnp.zeros_like(acc)
+
+    normed = jnp.concatenate([ref[0] for ref in normed_refs], axis=0)
+    acc[:, 0:own] += mm(normed, out_ref[0].reshape(own, out_ref.shape[3]), NT)
+
+    @pl.when(step == pl.num_programs(0) - 1)
+    def _():
+        count = offsets_ref.shape[0]
+        buckets, rows_dev = count // copies, width // (copies * n_exp)
+        row = lax.broadcasted_iota(jnp.int32, (width, count), 0)
+        bucket = lax.broadcasted_iota(jnp.int32, (width, count), 1)
+        place = row // (n_exp * rows_dev) * buckets + row % rows_dev
+        here = ((place == bucket) & (row % rows_dev < buckets)).astype(f32).astype(bf16)
+        table = jnp.sum(offsets_ref[...], axis=1, keepdims=True)
+        column = jnp.sum(mm(here, wide_thirds(table), NN), axis=1, keepdims=True)
+        base = own // 128 * 128
+        lane = lax.broadcasted_iota(jnp.int32, (width, 128), 1) + base
+        acc[:, base : base + 128] += jnp.where(lane == own, column, 0.0)
+        per = shares[0].shape[0]
+        for d, share in enumerate(shares):
+            start = pl.multiple_of(jnp.bitwise_xor(dp_ref[0], d) * per, per)
+            share[...] = acc[pl.ds(start, per), :].astype(bf16)
+
+
+def sequence_grad(dp, normed, out, offsets, n_dp, n_exp, copies, lanes):
+    groups, _, dim, tok = out.shape
+    width = normed.shape[1]
+    return pl.pallas_call(
+        functools.partial(sequence_grad_kernel, n_exp, copies),
+        grid_spec=pltpu.PrefetchScalarGridSpec(
+            num_scalar_prefetch=1,
+            grid=(groups,),
+            in_specs=[
+                pl.BlockSpec((1, 3, dim, tok), lambda g, d: (g, 0, 0, 0)),
+                pl.BlockSpec(offsets.shape, lambda g, d: (0, 0)),
+            ]
+            + [
+                pl.BlockSpec((1, width // 4, tok), lambda g, d, i=i: (g, i, 0)) for i in range(4)
+            ],
+            out_specs=[pl.BlockSpec((width // n_dp, lanes), lambda g, d: (0, 0))] * n_dp,
+            scratch_shapes=[pltpu.VMEM((width, lanes), f32)],
+        ),
+        out_shape=[jax.ShapeDtypeStruct((width // n_dp, lanes), bf16)] * n_dp,
+        compiler_params=pltpu.CompilerParams(vmem_limit_bytes=60 << 20),
+        cost_estimate=cost(
+            6 * dim * groups * tok * width, 2 * groups * tok * (width + 3 * dim)
+        ),
+        name="sequence_grad",
+    )(dp, out, offsets, *[normed] * 4)
+
+
 def dot_f32(left, right, left_dim, right_dim):
     return mm(left, right, (((left_dim,), (right_dim,)), ((), ())))
 
@@ -809,19 +882,6 @@
     return [parts[0]] + [
         lax.ppermute(parts[d], axis, [(i, i ^ d) for i in range(n)]) for d in range(1, n)
     ]
-
-
-def scatter_dp(rows):
-    n = lax.axis_size("dp")
-    shares = rows.reshape((n, rows.shape[0] // n) + rows.shape[1:])
-    mine = lax.axis_index("dp")
-    return exchange(
-        [
-            lax.dynamic_index_in_dim(shares, jnp.bitwise_xor(mine, d), 0, False)
-            for d in range(n)
-        ],
-        "dp",
-    )
 
 
 def add_low(parts):
@@ -890,13 +950,14 @@
         return jnp.swapaxes(blocks.reshape((n_ctx, n_exp) + shape[1:]), 0, 1).reshape(shape)
 
     exp_arg = exp_index.astype(jnp.int32).reshape(1)
-    normed, *parts = project(layer_input, attn_gain, qkv_weight, groups, heads)
+    normed_t, *parts = project(layer_input, attn_gain, qkv_weight, groups, heads)
     qkv = [swap_blocks(part, pair) for part in parts]
     table_dev = lax.dynamic_slice_in_dim(bias_table, ctx_index * heads, heads, 1)
     buck_rev, buck, kmask, qmask, hide, seen = attention_plan(
         block_ids[0], bucket_ids, groups, tok
     )
     chunks = (seen + step_k - 1) // step_k
+    chunks_fwd = (seen + 2 * step_k - 1) // (2 * step_k)
 
     flat_ids = expert_ids.reshape(TOP * tok)
     fill_rank = fill_order.reshape(TOP * tok)
@@ -930,12 +991,14 @@
             (qkv[0], place, slots_a, slots_b, buck_rev, buck, kmask, qmask, hide)
         )
     )
-    normed_seq = lax.all_gather(after(normed, qkv[0]), pair, axis=0, tiled=True)
+    normed_seq = lax.all_gather(after(normed_t, qkv[0]), pair)
     for h in range(heads):
         arg = after(qkv[h], forward)
         if h == heads - 1:
             grad_a = exchange(after(slots_a, arg))
-        out = attention_fwd(order, chunks, table_dev[:, h], buck_rev, kmask, qmask, arg, step_k)
+        out = attention_fwd(
+            order, chunks_fwd, table_dev[:, h], buck_rev, kmask, qmask, arg, 2 * step_k
+        )
         out = after(out, qkv[h + 1] if h < heads - 1 else grad_a, mixed)
         forward.append(out)
         mixed.append(swap_blocks(out[0], pair).reshape(groups * HEAD_DIM, tok))
@@ -957,6 +1020,9 @@
     g_args = after(grad_a + grad_b, run_b)
     down_1 = down_grad(ctx_arg, hidden, g_args, x_a + x_b, copies, 0, cuts[1])
 
+    def sum_dp(half):
+        return lax.psum_scatter(half, "dp", scatter_dimension=0, tiled=True)
+
     def to_ctx(half):
         return lax.ppermute(half, "ctx", [(0, 1), (1, 0)])
 
@@ -977,85 +1043,70 @@
     halves.append(add_low((down_2[0], came)))
     grads_b = exchange(list(undo_b[1:]))
     grads_in = [undo_a[0], undo_b[0]]
-    share = 2 * tiles * 2 // 11
-    sizes = (share, 2 * tiles - 4 * share, share, 2 * share)
-    in_parts, first = [], 0
-    xs = after(x_a + x_b, undo_b)
-    for size in sizes:
-        in_parts.append(in_grad(ctx_arg, xs, grads_in, copies, first, size))
-        first += size
-        xs = after(x_a + x_b, in_parts[-1])
-        if len(in_parts) == 1:
-            came = to_ctx(after(in_parts[0][1], halves[1]))
-    in_parts[3], came, grads_b = lax.optimization_barrier((in_parts[3], came, grads_b))
-    halves.append(add_low((in_parts[0][0], came)))
-    came = to_ctx(after(in_parts[2][1], halves[2]))
-
-    produced, row_grad = after((produced_a + produced_b, grads_a + grads_b), in_parts)
+    total = 2 * tiles
+    size_a, size_d = total * 3 // 22, total * 8 // 22
+    xt = turn(ctx_arg, x_a + x_b, copies)
+    part_a = in_grad(after(xt, undo_b), grads_in, 0, size_a)
+    came_a = to_ctx(after(part_a[1], halves[1]))
+    part_b = in_grad(after(xt, part_a), grads_in, size_a, size_a)
+    part_d = in_grad(after(xt, part_b), grads_in, 2 * size_a, size_d)
+
+    part_d, grads_b, came_a = lax.optimization_barrier((part_d, grads_b, came_a))
+    came_b = to_ctx(after(part_b[1], came_a))
     layer_output, middle_grad, *outs = combine(
         exp_arg, place, expert_ids, probs, middle, cotangent, normed_moe, moe_gain,
-        router_weight.T.astype(f32), out_weight, produced, row_grad, mixed, copies,
-    )
-    outs, came = lax.optimization_barrier((outs, came))
-    halves.append(add_low((in_parts[2][0], came)))
+        router_weight.T.astype(f32), out_weight, produced_a + produced_b, grads_a + grads_b, mixed,
+        copies,
+    )
+    down_sums = [sum_dp(half) for half in halves]
+    outs, came_b, down_sums[0] = lax.optimization_barrier((outs, came_b, down_sums[0]))
+    half_a = jnp.concatenate(
+        [add_low((part_a[0], came_a)), add_low((part_b[0], came_b))], axis=1
+    )
+    first = 2 * size_a + size_d
+    part_c = in_grad(after(xt, outs), grads_in, first, total - first)
     early = outs[heads:]
     mixed_grad = [swap_blocks(part, pair) for part in outs[:heads]]
     rows_dev = width // (n_dp * groups)
 
-    def sum_dp(half):
-        return lax.psum_scatter(half, "dp", scatter_dimension=0, tiled=True)
-
-    down_sums = [sum_dp(halves[0]), sum_dp(halves[1])]
-    last_own, last_other = [sum_dp(half) for half in in_parts[1]]
-    in_sums = [sum_dp(halves[2]), None, sum_dp(halves[3]), None]
-
-    buckets = bias_table.shape[0] // copies
+    last_own, last_other = [sum_dp(half) for half in part_d]
+    sum_a = sum_dp(half_a)
+
     lanes = -(-(3 * HEAD_DIM + 1) // 128) * 128
-    backward, grads = [], []
+    dp_arg = lax.axis_index("dp").astype(jnp.int32).reshape(1)
+    backward, grads, late = [], [], []
     for h in range(heads):
-        arg = after(mixed_grad[h], backward)
+        arg = after(mixed_grad[h], backward if h else part_c)
         beside = [grads[h - 1]] if h else []
         if h == 0:
-            came = to_ctx(after(in_parts[3][1], arg))
+            came_c = to_ctx(after(part_c[1], arg))
             early_parts = exchange(after(early, arg))
-            beside += [came, early_parts, last_own, last_other] + mixed_grad[1:2]
+            beside += [came_c, early_parts, last_own, last_other, down_sums[1]] + mixed_grad[1:2]
+        else:
+            arg = after(arg, half_c)
         if h == heads - 1:
             last_came = to_ctx(after(last_other, arg))
-            beside += [last_came, in_sums[0]] + ([early_parts] if h else [])
+            beside += [last_came, sum_a] + ([late] if h else [])
         out = attention_bwd(
             order, chunks, table_dev[:, h], buck, kmask, hide, qkv[h], forward[h][0],
             arg, forward[h][1], step_k,
         )
         out, beside = lax.optimization_barrier((out, beside))
         if h == 0:
-            came, early_parts = beside[0], beside[1]
-            in_sums[3] = sum_dp(add_low((in_parts[3][0], came)))
-            early_parts = scatter_dp(add_low(early_parts))
-        if h == heads - 1:
-            in_sums[1] = add_low((last_own, after(last_came, out)))
-            early_half = add_low(early_parts)
+            half_c = add_low((part_c[0], beside[0]))
+            sum_c = sum_dp(half_c)
+            early_half = sum_dp(add_low(beside[1]))
+        elif h == heads - 1:
+            late = beside[-1]
         backward.append(out)
         grads.append(swap_blocks(out[0], pair))
-    packed = []
-    for out, offsets in backward:
-        columns = jnp.transpose(after(out, backward), (1, 2, 0, 3))
-        columns = columns.reshape(3 * HEAD_DIM, groups * tok)
-        local_grad = dot_f32(normed_seq, columns, 0, 1)
-        table_grad = jnp.sum(offsets, axis=1)
-        spread = jnp.pad(
-            jnp.broadcast_to(
-                table_grad.reshape(n_dp, n_ctx, 1, buckets), (n_dp, n_ctx, n_exp, buckets)
-            ),
-            ((0, 0), (0, 0), (0, 0), (0, rows_dev - buckets)),
-        ).reshape(width, 1)
-        local_grad = jnp.pad(local_grad, ((0, 0), (0, lanes - 3 * HEAD_DIM)))
-        lane = jnp.arange(lanes)[None, :]
-        packed.append(jnp.where(lane == 3 * HEAD_DIM, spread, local_grad).astype(bf16))
-    packed, grads = lax.optimization_barrier((jnp.concatenate(packed, axis=1), grads))
-    late = scatter_dp(packed)
+        shares = sequence_grad(dp_arg, normed_seq, *out, n_dp, n_exp, copies, lanes)
+        late.append(exchange(shares, "dp"))
+    in_sums = [sum_a, add_low((last_own, after(last_came, backward))), sum_c]
+    late, grads = lax.optimization_barrier((late, grads))
+    late = jnp.concatenate([add_low(parts) for parts in late], axis=1)
+    rows_out = swap_blocks(in_swap_order(late.reshape(groups, rows_dev, -1)), pair)
     input_grad = input_gradient(layer_input, attn_gain, middle_grad, qkv_weight, grads)
-    input_grad, late = lax.optimization_barrier((input_grad, late))
-    late = add_low(late)
     early_half = early_half.reshape(n_ctx, rows_dev, width + 128)
     early_own, early_other = [
         lax.dynamic_index_in_dim(early_half, at, 0, False) for at in (ctx_index, 1 - ctx_index)
@@ -1065,7 +1116,11 @@
     ).astype(f32)
     expert_in_grad = jnp.concatenate(in_sums, axis=1).astype(f32)
     expert_down_grad = jnp.concatenate(down_sums, axis=1).astype(f32)
-    rows_out = swap_blocks(in_swap_order(late.reshape(groups, rows_dev, -1)), pair)
+    rows_out, input_grad, expert_in_grad, expert_down_grad, early_rows = (
+        lax.optimization_barrier(
+            (rows_out, input_grad, expert_in_grad, expert_down_grad, early_rows)
+        )
+    )
     my_rows = ((lax.axis_index("dp") * n_ctx + ctx_index) * n_exp + exp_index) * rows_dev
     qkv_grad, attn_gain_grad, bias_rows = finish(
         exp_arg,
@@ -1085,7 +1140,7 @@
         attn_gain_grad.reshape(rows_dev),
         qkv_grad,
         early_rows[:, :width],
-        bias_rows[:buckets],
+        bias_rows[: bias_table.shape[0] // copies],
         early_rows[:, width + 3 * experts],
         router_grad,
         expert_in_grad[None],

time: 621 us -> 594 us (0.957)
  the two profiles are of different devices: /device:TPU:9 before, /device:TPU:1 now
where the time goes in v2:
time: 594 us; the launch traced here: 582 us
  Pallas kernels  370 us (62%)
  starting transfers between devices  76.8 us (13%)
  waiting for transfers between devices  58.9 us (10%)
  other arithmetic  31.7 us (5%)
  local copies, waits for them, and re-layouts  20 us (3%)
  between operations  15.7 us (3%)
  matrix products  9.59 us (2%)
    pallas_call x2, Pallas kernels, attention_bwd(): pl.pallas_call(functools.partial(attention_bwd_kernel, bk, order), grid_s...  94.6 us
    pallas_call x2, Pallas kernels, attention_fwd(): pl.pallas_call(functools.partial(attention_fwd_kernel, bk, order), grid_s...  60.5 us
    pallas_call x2, Pallas kernels, expert_bwd(): pl.pallas_call(functools.partial(expert_bwd_kernel, steps, groups), grid=...  51.4 us
    pallas_call x2, Pallas kernels, expert_fwd(): pl.pallas_call(functools.partial(expert_fwd_kernel, steps, groups), grid=...  43.2 us
    all_to_all x9, starting transfers between devices, swap_blocks(): return lax.all_to_all(blocks, axes, split_axis=0, concat_axis=0, tiled=True)  41.1 us
    ppermute x33, waiting for transfers between devices, exchange(): lax.ppermute(parts[d], axis, [(i, i ^ d) for i in range(n)])  39.2 us
    pallas_call x4, Pallas kernels, in_grad(): pl.pallas_call(in_grad_kernel, grid=(count,), in_specs=[pl.BlockSpec((wid...  32.7 us
    ppermute x33, starting transfers between devices, exchange(): lax.ppermute(parts[d], axis, [(i, i ^ d) for i in range(n)])  28.4 us
  transfers between devices with their start and end apart: 57, of which 13 were waited for; matrix products, arithmetic and copies ran while one was open for 8% of the time, Pallas kernels for 62%

profile of v2, /device:TPU:1, one launch (start us, length us, event | category | flops | bytes accessed | tf_op | source)
XLA Modules:
  0.0 582.3 jit_solution(4881442640532507711)
XLA Ops:
  7.2 9.0 %project.1 = (bf16[1024,512]{1,0:T(8,128)(2,1)}, bf16[8,3,64,512]{3,2,1,0:T(8,128)(2,1)}, bf16[8,3,64,512]{3,2,1,0:T(8,128)(2,1)}) custom-call(bf16[512,1024]{1,0:T(8,128)(2,1)} %x_ref.5, f32[1,1024]{1,0:T(1,128)} %bitcast.62, bf16[1024,3072]{1,0:T(8,128)(2,1)} %refs_3_.3, bf16[1024,3072]{1,0:T(8,128)(2,1)} %refs_3_.3, bf16[1024,3072]{1,0:T(8,128)(2,1)} %refs_3_.3, ...), custom_call_target="tpu_custom_call" | custom-call | flops 3221225472 | bytes 11534336 | tf_op jit(solution)/shard_map/project/pallas_call | solution.py:530
  16.2 5.4 all-to-all-start
  49.9 30.3 %attention_fwd.2 = (bf16[8,64,512]{2,1,0:T(8,128)(2,1)}, f32[8,1,512]{2,1,0:T(1,128)}) custom-call(s32[8]{0:T(128)} %get-tuple-element.511.nch_ref, f32[32]{0:T(128)} %get-tuple-element.509.tab_ref, s32[8,8192]{1,0:T(8,128)} %broadcast_in_dim.57.buck_ref, bf16[64,4096]{1,0:T(8,128)(2,1)} %maximum_maximum_fusion.kmask_ref, ...), custom_call_target="tpu_custom_call" | custom-call | flops 16777216000 | bytes 2097152 | tf_op jit(solution)/shard_map/attention_fwd/pallas_call | solution.py:96
  86.7 30.1 %attention_fwd.3 = (bf16[8,64,512]{2,1,0:T(8,128)(2,1)}, f32[8,1,512]{2,1,0:T(1,128)}) custom-call(s32[8]{0:T(128)} %get-tuple-element.511.nch_ref, f32[32]{0:T(128)} %get-tuple-element.508.tab_ref, s32[8,8192]{1,0:T(8,128)} %broadcast_in_dim.57.buck_ref, bf16[64,4096]{1,0:T(8,128)(2,1)} %maximum_maximum_fusion.kmask_ref, ...), custom_call_target="tpu_custom_call" | custom-call | flops 16777216000 | bytes 2097152 | tf_op jit(solution)/shard_map/attention_fwd/pallas_call | solution.py:96
  117.6 6.6 %collective-permute-done.2.refs_3_ = bf16[160,1024]{1,0:T(8,128)(2,1)} collective-permute-done((bf16[160,1024]{1,0:T(8,128)(2,1)S(1)}, bf16[160,1024]{1,0:T(8,128)(2,1)}, u32[]{:S(2)}, u32[]{:S(2)}) %collective-permute-start.2) | collective-permute-done | bytes 327712 | tf_op jit(solution)/shard_map/ppermute | solution.py:883
  129.6 6.2 %all-to-all-done.3 = bf16[8,64,512]{2,1,0:T(8,128)(2,1)S(1)} async-done(((bf16[8,64,512]{2,1,0:T(8,128)(2,1)}), bf16[8,64,512]{2,1,0:T(8,128)(2,1)S(1)}, u32[]{:S(2)}, u32[]{:S(2)}) %all-to-all-start.3) | async-done | bytes 524320 | tf_op jit(solution)/shard_map/all_to_all | solution.py:877
  136.6 7.9 %route.1 = (f32[512,1024]{1,0:T(8,128)}, bf16[512,1024]{1,0:T(8,128)(2,1)}, f32[512,4]{1,0:T(8,128)}, bf16[160,1152]{1,0:T(8,128)(2,1)}, bf16[160,1152]{1,0:T(8,...) custom-call(bf16[512,1024]{1,0:T(8,128)(2,1)} %x_ref.5, ...), custom_call_target="tpu_custom_call" | custom-call | flops 2415919104 | bytes 8388608 | tf_op jit(solution)/shard_map/route/pallas_call | solution.py:797
  149.2 6.5 %collective-permute-done.4.refs_2_.refs_10_.refs_6_ = bf16[160,1152]{1,0:T(8,128)(2,1)S(1)} collective-permute-done((bf16[160,1152]{1,0:T(8,128)(2,1)}, bf16[160,1152]{1,0:T(8,128)(2,1)S(1)}, u32[]{:S(2)}, u32[]{:S(2)}) %collective-permute-start.4) | collective-permute-done | bytes 368672 | tf_op jit(solution)/shard_map/ppermute | solution.py:883
  155.7 8.5 %collective-permute-done.5.refs_3_.refs_11_.refs_7_ = bf16[160,1152]{1,0:T(8,128)(2,1)S(1)} collective-permute-done((bf16[160,1152]{1,0:T(8,128)(2,1)}, bf16[160,1152]{1,0:T(8,128)(2,1)S(1)}, u32[]{:S(2)}, u32[]{:S(2)}) %collective-permute-start.5) | collective-permute-done | bytes 368672 | tf_op jit(solution)/shard_map/ppermute | solution.py:883
  166.2 21.6 %expert_fwd.2 = (bf16[2816,640]{1,0:T(8,128)(2,1)}, bf16[640,2816]{1,0:T(8,128)(2,1)}, bf16[640,2816]{1,0:T(8,128)(2,1)}, bf16[160,1024]{1,0:T(8,128)(2,1)}, bf1...) custom-call(bf16[1,1024,5632]{2,1,0:T(8,128)(2,1)} %wu_ref.7, ...), custom_call_target="tpu_custom_call" | custom-call | flops 18454937600 | bytes 30736384 | tf_op jit(solution)/shard_map/expert_fwd/pallas_call | solution.py:311
  187.8 5.9 %collective-permute-done.11.refs_7_.refs_3_ = bf16[160,1024]{1,0:T(8,128)(2,1)} collective-permute-done((bf16[160,1024]{1,0:T(8,128)(2,1)S(1)}, bf16[160,1024]{1,0:T(8,128)(2,1)}, u32[]{:S(2)}, u32[]{:S(2)}) %collective-permute-start.11) | collective-permute-done | bytes 327712 | tf_op jit(solution)/shard_map/ppermute | solution.py:883
  195.9 21.7 %expert_fwd.3 = (bf16[2816,640]{1,0:T(8,128)(2,1)}, bf16[640,2816]{1,0:T(8,128)(2,1)}, bf16[640,2816]{1,0:T(8,128)(2,1)}, bf16[160,1024]{1,0:T(8,128)(2,1)}, bf1...) custom-call(bf16[1,1024,5632]{2,1,0:T(8,128)(2,1)} %wu_ref.7, ...), custom_call_target="tpu_custom_call" | custom-call | flops 18454937600 | bytes 30736384 | tf_op jit(solution)/shard_map/expert_fwd/pallas_call | solution.py:311
  219.9 9.6 %down_grad.2 = (bf16[4,1536,128]{2,1,0:T(8,128)(2,1)}, bf16[4,1536,128]{2,1,0:T(8,128)(2,1)}) custom-call(s32[1]{0:T(128)} %bitcast.13.ctx_ref, bf16[160,1024]{1,0:T(8,128)(2,1)} %convolution_convert_fusion.7.refs_0_, bf16[160,1024]{1,0:T(8,128)(2,1)} %copy-done.62, bf16[160,1024]{1,0:T(8,128)(2,1)} %collective-permute-done.1.refs_2_, ...), custom_call_target="tpu_custom_call" | custom-call | flops 8053063680 | bytes 9699328 | tf_op jit(solution)/shard_map/down_grad/pallas_call | solution.py:489
  230.4 8.6 %down_grad.3 = (bf16[4,1280,128]{2,1,0:T(8,128)(2,1)}, bf16[4,1280,128]{2,1,0:T(8,128)(2,1)}) custom-call(s32[1]{0:T(128)} %bitcast.13.ctx_ref, bf16[160,1024]{1,0:T(8,128)(2,1)} %convolution_convert_fusion.7.refs_0_, bf16[160,1024]{1,0:T(8,128)(2,1)} %copy-done.62, bf16[160,1024]{1,0:T(8,128)(2,1)} %collective-permute-done.1.refs_2_, ...), custom_call_target="tpu_custom_call" | custom-call | flops 6710886400 | bytes 8519680 | tf_op jit(solution)/shard_map/down_grad/pallas_call | solution.py:489
  239.0 25.5 %expert_bwd.2 = (bf16[2,640,2816]{2,1,0:T(8,128)(2,1)}, bf16[160,1024]{1,0:T(8,128)(2,1)}, bf16[160,1024]{1,0:T(8,128)(2,1)}, bf16[160,1024]{1,0:T(8,128)(2,1)}, bf16[160,1024]{1,0:T(8,128)(2,1)}) custom-call(bf16[640,2816]{1,0:T(8,128)(2,1)} %get-tuple-element.299.act_ref, bf16[640,2816]{1,0:T(8,128)(2,1)} %get-tuple-element.300.slope_ref, ...), custom_call_target="tpu_custom_call" | custom-call | flops 18454937600 | bytes 34340864 | tf_op jit(solution)/shard_map/expert_bwd/pallas_call | solution.py:366
  270.8 25.9 %expert_bwd.3 = (bf16[2,640,2816]{2,1,0:T(8,128)(2,1)}, bf16[160,1024]{1,0:T(8,128)(2,1)}, bf16[160,1024]{1,0:T(8,128)(2,1)}, bf16[160,1024]{1,0:T(8,128)(2,1)}, bf16[160,1024]{1,0:T(8,128)(2,1)}) custom-call(bf16[640,2816]{1,0:T(8,128)(2,1)} %get-tuple-element.319.act_ref, bf16[640,2816]{1,0:T(8,128)(2,1)} %get-tuple-element.320.slope_ref, ...), custom_call_target="tpu_custom_call" | custom-call | flops 18454937600 | bytes 34340864 | tf_op jit(solution)/shard_map/expert_bwd/pallas_call | solution.py:366
  302.0 5.3 turn.1.refs_0_.refs_1_.refs_2_.refs_3_
  310.0 5.8 in_grad.4
  316.5 5.5 in_grad.5
  322.0 10.7 %in_grad.6 = (bf16[512,2048]{1,0:T(8,128)(2,1)}, bf16[512,2048]{1,0:T(8,128)(2,1)}) custom-call(bf16[1024,1280]{1,0:T(8,128)(2,1)} %turn.1.refs_0_.refs_1_.refs_2_.refs_3_, bf16[1024,1280]{1,0:T(8,128)(2,1)} %turn.1.refs_0_.refs_1_.refs_2_.refs_3_, bf16[1024,1280]{1,0:T(8,128)(2,1)} %turn.1.refs_0_.refs_1_.refs_2_.refs_3_, ...), custom_call_target="tpu_custom_call" | custom-call | flops 10737418240 | bytes 12058624 | tf_op jit(solution)/shard_map/in_grad/pallas_call | solution.py:443
  336.8 15.5 %combine.1 = (bf16[512,1024]{1,0:T(8,128)(2,1)}, f32[512,1024]{1,0:T(8,128)}, bf16[8,64,512]{2,1,0:T(8,128)(2,1)}, bf16[8,64,512]{2,1,0:T(8,128)(2,1)}, bf16[256...) custom-call(s32[1]{0:T(128)} %bitcast.exp_ref, ...), custom_call_target="tpu_custom_call" | custom-call | flops 6174015488 | bytes 18874368 | tf_op jit(solution)/shard_map/combine/pallas_call | solution.py:698
  353.6 5.2 all-to-all-start.5
  358.8 10.7 %in_grad.7 = (bf16[512,2048]{1,0:T(8,128)(2,1)}, bf16[512,2048]{1,0:T(8,128)(2,1)}) custom-call(bf16[1024,1280]{1,0:T(8,128)(2,1)} %turn.1.refs_0_.refs_1_.refs_2_.refs_3_, bf16[1024,1280]{1,0:T(8,128)(2,1)} %turn.1.refs_0_.refs_1_.refs_2_.refs_3_, bf16[1024,1280]{1,0:T(8,128)(2,1)} %turn.1.refs_0_.refs_1_.refs_2_.refs_3_, ...), custom_call_target="tpu_custom_call" | custom-call | flops 10737418240 | bytes 12058624 | tf_op jit(solution)/shard_map/in_grad/pallas_call | solution.py:443
  377.5 47.4 %attention_bwd.2 = (bf16[8,3,64,512]{3,2,1,0:T(8,128)(2,1)}, f32[32,128]{1,0:T(8,128)}) custom-call(s32[8]{0:T(128)} %get-tuple-element.510.nch_ref, f32[32]{0:T(128)} %get-tuple-element.509.tab_ref, s32[8,8192]{1,0:T(8,128)} %broadcast_in_dim.58.buck_ref, bf16[64,4096]{1,0:T(8,128)(2,1)} %maximum_maximum_fusion.kmask_ref, ...), custom_call_target="tpu_custom_call" | custom-call | flops 41943040000 | bytes 4194304 | tf_op jit(solution)/shard_map/attention_bwd/pallas_call | solution.py:213
  440.9 9.1 %sequence_grad.2 = (bf16[256,256]{1,0:T(8,128)(2,1)}, bf16[256,256]{1,0:T(8,128)(2,1)}, bf16[256,256]{1,0:T(8,128)(2,1)}, bf16[256,256]{1,0:T(8,128)(2,1)}) custom-call(s32[1]{0:T(128)} %bitcast.14.dp_ref, bf16[8,3,64,512]{3,2,1,0:T(8,128)(2,1)} %get-tuple-element.426.out_ref, f32[32,128]{1,0:T(8,128)} %get-tuple-element.427.offsets_ref, ...), custom_call_target="tpu_custom_call" | custom-call | flops 1610612736 | bytes 9961472 | tf_op jit(solution)/shard_map/sequence_grad/pallas_call | solution.py:848
  453.5 4.5 add_convert_fusion
  459.4 47.2 %attention_bwd.3 = (bf16[8,3,64,512]{3,2,1,0:T(8,128)(2,1)}, f32[32,128]{1,0:T(8,128)}) custom-call(s32[8]{0:T(128)} %get-tuple-element.510.nch_ref, f32[32]{0:T(128)} %get-tuple-element.508.tab_ref, s32[8,8192]{1,0:T(8,128)} %broadcast_in_dim.58.buck_ref, bf16[64,4096]{1,0:T(8,128)(2,1)} %maximum_maximum_fusion.kmask_ref, ...), custom_call_target="tpu_custom_call" | custom-call | flops 41943040000 | bytes 4194304 | tf_op jit(solution)/shard_map/attention_bwd/pallas_call | solution.py:213
  510.5 5.3 all-to-all-start.7
  520.1 9.1 %sequence_grad.3 = (bf16[256,256]{1,0:T(8,128)(2,1)}, bf16[256,256]{1,0:T(8,128)(2,1)}, bf16[256,256]{1,0:T(8,128)(2,1)}, bf16[256,256]{1,0:T(8,128)(2,1)}) custom-call(s32[1]{0:T(128)} %bitcast.14.dp_ref, bf16[8,3,64,512]{3,2,1,0:T(8,128)(2,1)} %get-tuple-element.443.out_ref, f32[32,128]{1,0:T(8,128)} %get-tuple-element.444.offsets_ref, ...), custom_call_target="tpu_custom_call" | custom-call | flops 1610612736 | bytes 9961472 | tf_op jit(solution)/shard_map/sequence_grad/pallas_call | solution.py:848
  534.9 7.2 %collective-permute-done.36 = bf16[256,256]{1,0:T(8,128)(2,1)S(1)} collective-permute-done((bf16[256,256]{1,0:T(8,128)(2,1)}, bf16[256,256]{1,0:T(8,128)(2,1)S(1)}, u32[]{:S(2)}, u32[]{:S(2)}) %collective-permute-start.36) | collective-permute-done | bytes 131104 | tf_op jit(solution)/shard_map/ppermute | solution.py:883
  549.6 4.6 all-to-all-start.8
  554.3 11.2 %input_grad.1 = f32[512,1024]{1,0:T(8,128)} custom-call(bf16[512,1024]{1,0:T(8,128)(2,1)} %x_ref.5, f32[1,1024]{1,0:T(1,128)} %bitcast.63, f32[512,1024]{1,0:T(8,128)} %get-tuple-element.457.mid_ref, bf16[1024,3072]{1,0:T(8,128)(2,1)} %refs_3_.3, bf16[1024,3072]{1,0:T(8,128)(2,1)} %refs_3_.3, bf16[1024,3072]{1,0:T(8,128)(2,1)} %refs_3_.3, ...), custom_call_target="tpu_custom_call" | custom-call | flops 3221225472 | bytes 14680064 | tf_op jit(solution)/shard_map/input_grad/pallas_call | solution.py:579
  (330 shorter events, 133.0 us)
Async XLA Ops:
  21.6 196.1 %all-gather.3.cloned.1.call-start = ((), (), s32[]{:S(2)}) async-start(), calls=%async_computation.23 | async-start | bytes 9437184 | tf_op jit(solution)/shard_map/all_gather | solution.py:994
  42.9 37.4 %all-to-all-start.1 = ((bf16[8,3,64,512]{3,2,1,0:T(8,128)(2,1)}), bf16[8,3,64,512]{3,2,1,0:T(8,128)(2,1)S(1)}, u32[]{:S(2)}, u32[]{:S(2)}) async-start(bf16[8,3,64,512]{3,2,1,0:T(8,128)(2,1)} %get-tuple-element.250), calls=%async_computation.1 | async-start | bytes 3145728 | tf_op jit(solution)/shard_map/all_to_all | solution.py:877
  80.3 43.9 %all-to-all-start.2 = ((bf16[8,64,512]{2,1,0:T(8,128)(2,1)}), bf16[8,64,512]{2,1,0:T(8,128)(2,1)S(1)}, u32[]{:S(2)}, u32[]{:S(2)}) async-start(bf16[8,64,512]{2,1,0:T(8,128)(2,1)} %get-tuple-element.251.o_ref), calls=%async_computation.2 | async-start | bytes 1048576 | tf_op jit(solution)/shard_map/all_to_all | solution.py:877
  84.5 32.3 %collective-permute-start = (bf16[160,1024]{1,0:T(8,128)(2,1)S(1)}, bf16[160,1024]{1,0:T(8,128)(2,1)S(1)}, u32[]{:S(2)}, u32[]{:S(2)}) collective-permute-start(bf16[160,1024]{1,0:T(8,128)(2,1)S(1)} %copy-done.37), channel_id=1, source_target_pairs={{0,1},{1,0},{2,3},{3,2},{4,5},{5,4},{6,7},{7,6},{8,9},{9,8},{10,11... | collective-permute-start | bytes 983048 | tf_op jit(solution)/shard_map/ppermute | solution.py:883
  84.6 32.2 %collective-permute-start.1 = (bf16[160,1024]{1,0:T(8,128)(2,1)S(1)}, bf16[160,1024]{1,0:T(8,128)(2,1)}, u32[]{:S(2)}, u32[]{:S(2)}) collective-permute-start(bf16[160,1024]{1,0:T(8,128)(2,1)S(1)} %copy-done.36), channel_id=1, source_target_pairs={{0,2},{1,3},{2,0},{3,1},{4,6},{5,7},{6,4},{7,5},{8,10},{9,11},{10,... | collective-permute-start | bytes 983048 | tf_op jit(solution)/shard_map/ppermute | solution.py:883
  86.3 37.9 %collective-permute-start.2 = (bf16[160,1024]{1,0:T(8,128)(2,1)S(1)}, bf16[160,1024]{1,0:T(8,128)(2,1)}, u32[]{:S(2)}, u32[]{:S(2)}) collective-permute-start(bf16[160,1024]{1,0:T(8,128)(2,1)S(1)} %copy-done.35), channel_id=1, source_target_pairs={{0,3},{1,2},{2,1},{3,0},{4,7},{5,6},{6,5},{7,4},{8,11},{9,10},{10,... | collective-permute-start | bytes 983048 | tf_op jit(solution)/shard_map/ppermute | solution.py:883
  127.6 226.0 %reduce-scatter.8.cloned.1.call-start = ((), (), s32[]{:S(2)}) async-start(), calls=%async_computation.16 | async-start | bytes 1966080 | tf_op jit(solution)/shard_map/reduce_scatter | solution.py:1024
  147.2 40.6 %collective-permute-start.7 = (bf16[160,1152]{1,0:T(8,128)(2,1)}, bf16[160,1152]{1,0:T(8,128)(2,1)S(1)}, u32[]{:S(2)}, u32[]{:S(2)}) collective-permute-start(bf16[160,1152]{1,0:T(8,128)(2,1)} %get-tuple-element.284), channel_id=1, source_target_pairs={{0,2},{1,3},{2,0},{3,1},{4,6},{5,7},{6,4},{7,5},{8,10},{9,11},{10,... | collective-permute-start | bytes 1105928 | tf_op jit(solution)/shard_map/ppermute | solution.py:883
  147.6 40.2 %collective-permute-start.8 = (bf16[160,1152]{1,0:T(8,128)(2,1)}, bf16[160,1152]{1,0:T(8,128)(2,1)S(1)}, u32[]{:S(2)}, u32[]{:S(2)}) collective-permute-start(bf16[160,1152]{1,0:T(8,128)(2,1)} %get-tuple-element.285), channel_id=1, source_target_pairs={{0,3},{1,2},{2,1},{3,0},{4,7},{5,6},{6,5},{7,4},{8,11},{9,10},{10,... | collective-permute-start | bytes 1105928 | tf_op jit(solution)/shard_map/ppermute | solution.py:883
  217.7 46.8 %collective-permute-start.15 = (bf16[160,1024]{1,0:T(8,128)(2,1)}, bf16[160,1024]{1,0:T(8,128)(2,1)}, u32[]{:S(2)}, u32[]{:S(2)}) collective-permute-start(bf16[160,1024]{1,0:T(8,128)(2,1)} %get-tuple-element.315), channel_id=1, source_target_pairs={{0,1},{1,0},{2,3},{3,2},{4,5},{5,4},{6,7},{7,6},{8,9},{9,8},{10,11... | collective-permute-start | bytes 983048 | tf_op jit(solution)/shard_map/ppermute | solution.py:883
  217.7 46.8 %collective-permute-start.16 = (bf16[160,1024]{1,0:T(8,128)(2,1)}, bf16[160,1024]{1,0:T(8,128)(2,1)}, u32[]{:S(2)}, u32[]{:S(2)}) collective-permute-start(bf16[160,1024]{1,0:T(8,128)(2,1)} %get-tuple-element.316), channel_id=1, source_target_pairs={{0,2},{1,3},{2,0},{3,1},{4,6},{5,7},{6,4},{7,5},{8,10},{9,11},{10,... | collective-permute-start | bytes 983048 | tf_op jit(solution)/shard_map/ppermute | solution.py:883
  218.2 46.3 %collective-permute-start.17 = (bf16[160,1024]{1,0:T(8,128)(2,1)}, bf16[160,1024]{1,0:T(8,128)(2,1)}, u32[]{:S(2)}, u32[]{:S(2)}) collective-permute-start(bf16[160,1024]{1,0:T(8,128)(2,1)} %get-tuple-element.317), channel_id=1, source_target_pairs={{0,3},{1,2},{2,1},{3,0},{4,7},{5,6},{6,5},{7,4},{8,11},{9,10},{10,... | collective-permute-start | bytes 983048 | tf_op jit(solution)/shard_map/ppermute | solution.py:883
  229.5 36.4 %collective-permute-start.18 = (bf16[4,1536,128]{2,1,0:T(8,128)(2,1)}, bf16[4,1536,128]{2,1,0:T(8,128)(2,1)S(1)}, u32[]{:S(2)}, u32[]{:S(2)}) collective-permute-start(bf16[4,1536,128]{2,1,0:T(8,128)(2,1)} %get-tuple-element.330), channel_id=1, source_target_pairs={{0,4},{4,0},{1,5},{5,1},{2,6},{6,2},{3,7},{7,3},{8,12},{12,8},{9,1... | collective-permute-start | bytes 4718600 | tf_op jit(solution)/shard_map/ppermute | solution.py:1027
  267.6 157.4 %reduce-scatter.14.cloned.1.call-start = ((), (), s32[]{:S(2)}) async-start(), calls=%async_computation.19 | async-start | bytes 1638400 | tf_op jit(solution)/shard_map/reduce_scatter | solution.py:1024
  267.6 29.2 %collective-permute-start.19 = (bf16[160,1024]{1,0:T(8,128)(2,1)}, bf16[160,1024]{1,0:T(8,128)(2,1)S(1)}, u32[]{:S(2)}, u32[]{:S(2)}) collective-permute-start(bf16[160,1024]{1,0:T(8,128)(2,1)} %get-tuple-element.356), channel_id=1, source_target_pairs={{0,1},{1,0},{2,3},{3,2},{4,5},{5,4},{6,7},{7,6},{8,9},{9,8},{10,11... | collective-permute-start | bytes 983048 | tf_op jit(solution)/shard_map/ppermute | solution.py:883
  270.0 30.4 %collective-permute-start.22 = (bf16[4,1280,128]{2,1,0:T(8,128)(2,1)}, bf16[4,1280,128]{2,1,0:T(8,128)(2,1)S(1)}, u32[]{:S(2)}, u32[]{:S(2)}) collective-permute-start(bf16[4,1280,128]{2,1,0:T(8,128)(2,1)} %get-tuple-element.374), channel_id=1, source_target_pairs={{0,4},{4,0},{1,5},{5,1},{2,6},{6,2},{3,7},{7,3},{8,12},{12,8},{9,1... | collective-permute-start | bytes 3932168 | tf_op jit(solution)/shard_map/ppermute | solution.py:1027
  301.9 124.7 %reduce-scatter.10.cloned.1.call-start = ((), (), s32[]{:S(2)}) async-start(), calls=%async_computation.17 | async-start | bytes 2621440 | tf_op jit(solution)/shard_map/reduce_scatter | solution.py:1024
  335.1 91.5 %reduce-scatter.12.cloned.1.call-start = ((), (), s32[]{:S(2)}) async-start(), calls=%async_computation.18 | async-start | bytes 2621440 | tf_op jit(solution)/shard_map/reduce_scatter | solution.py:1024
  369.5 55.5 %all-to-all-start.4 = ((bf16[8,64,512]{2,1,0:T(8,128)(2,1)}), bf16[8,64,512]{2,1,0:T(8,128)(2,1)}, u32[]{:S(2)}, u32[]{:S(2)}) async-start(bf16[8,64,512]{2,1,0:T(8,128)(2,1)} %get-tuple-element.407), calls=%async_computation.5 | async-start | bytes 1048576 | tf_op jit(solution)/shard_map/all_to_all | solution.py:877
  373.7 132.9 %reduce-scatter.20.cloned.1.call-start = ((), (), s32[]{:S(2)}) async-start(), calls=%async_computation.22 | async-start | bytes 737280 | tf_op jit(solution)/shard_map/reduce_scatter | solution.py:1024
  373.9 51.0 %collective-permute-start.29 = (bf16[256,1152]{1,0:T(8,128)(2,1)}, bf16[256,1152]{1,0:T(8,128)(2,1)}, u32[]{:S(2)}, u32[]{:S(2)}) collective-permute-start(bf16[256,1152]{1,0:T(8,128)(2,1)} %get-tuple-element.421), channel_id=1, source_target_pairs={{0,1},{1,0},{2,3},{3,2},{4,5},{5,4},{6,7},{7,6},{8,9},{9,8},{10,11... | collective-permute-start | bytes 1769480 | tf_op jit(solution)/shard_map/ppermute | solution.py:883
  374.1 50.9 %collective-permute-start.30 = (bf16[256,1152]{1,0:T(8,128)(2,1)}, bf16[256,1152]{1,0:T(8,128)(2,1)}, u32[]{:S(2)}, u32[]{:S(2)}) collective-permute-start(bf16[256,1152]{1,0:T(8,128)(2,1)} %get-tuple-element.422), channel_id=1, source_target_pairs={{0,2},{1,3},{2,0},{3,1},{4,6},{5,7},{6,4},{7,5},{8,10},{9,11},{10,... | collective-permute-start | bytes 1769480 | tf_op jit(solution)/shard_map/ppermute | solution.py:883
  375.7 49.2 %collective-permute-start.31 = (bf16[256,1152]{1,0:T(8,128)(2,1)}, bf16[256,1152]{1,0:T(8,128)(2,1)}, u32[]{:S(2)}, u32[]{:S(2)}) collective-permute-start(bf16[256,1152]{1,0:T(8,128)(2,1)} %get-tuple-element.423), channel_id=1, source_target_pairs={{0,3},{1,2},{2,1},{3,0},{4,7},{5,6},{6,5},{7,4},{8,11},{9,10},{10,... | collective-permute-start | bytes 1769480 | tf_op jit(solution)/shard_map/ppermute | solution.py:883
  376.1 50.5 %collective-permute-start.28 = (bf16[512,2048]{1,0:T(8,128)(2,1)}, bf16[512,2048]{1,0:T(8,128)(2,1)S(1)}, u32[]{:S(2)}, u32[]{:S(2)}) collective-permute-start(bf16[512,2048]{1,0:T(8,128)(2,1)} %get-tuple-element.419), channel_id=1, source_target_pairs={{0,4},{4,0},{1,5},{5,1},{2,6},{6,2},{3,7},{7,3},{8,12},{12,8},{9,1... | collective-permute-start | bytes 6291464 | tf_op jit(solution)/shard_map/ppermute | solution.py:1027
  430.0 79.5 %reduce-scatter.16.cloned.1.call-start = ((), (), s32[]{:S(2)}) async-start(), calls=%async_computation.20 | async-start | bytes 1966080 | tf_op jit(solution)/shard_map/reduce_scatter | solution.py:1024
  436.2 73.3 %all-to-all-start.6 = ((bf16[8,3,64,512]{3,2,1,0:T(8,128)(2,1)}), bf16[8,3,64,512]{3,2,1,0:T(8,128)(2,1)S(1)}, u32[]{:S(2)}, u32[]{:S(2)}) async-start(bf16[8,3,64,512]{3,2,1,0:T(8,128)(2,1)} %get-tuple-element.426.out_ref), calls=%async_computation.10 | async-start | bytes 3145728 | tf_op jit(solution)/shard_map/all_to_all | solution.py:877
  440.6 124.9 %reduce-scatter.18.cloned.1.call-start = ((), (), s32[]{:S(2)}) async-start(), calls=%async_computation.21 | async-start | bytes 2621440 | tf_op jit(solution)/shard_map/reduce_scatter | solution.py:1024
  449.9 59.6 %collective-permute-start.33 = (bf16[256,256]{1,0:T(8,128)(2,1)}, bf16[256,256]{1,0:T(8,128)(2,1)S(1)}, u32[]{:S(2)}, u32[]{:S(2)}) collective-permute-start(bf16[256,256]{1,0:T(8,128)(2,1)} %get-tuple-element.436), channel_id=1, source_target_pairs={{0,8},{8,0},{16,24},{24,16},{1,9},{9,1},{17,25},{25,17},{2,10},{10... | collective-permute-start | bytes 393224 | tf_op jit(solution)/shard_map/ppermute | solution.py:883
  451.2 58.3 %collective-permute-start.34 = (bf16[256,256]{1,0:T(8,128)(2,1)}, bf16[256,256]{1,0:T(8,128)(2,1)S(1)}, u32[]{:S(2)}, u32[]{:S(2)}) collective-permute-start(bf16[256,256]{1,0:T(8,128)(2,1)} %get-tuple-element.437), channel_id=1, source_target_pairs={{0,16},{8,24},{16,0},{24,8},{1,17},{9,25},{17,1},{25,9},{2,18},{10... | collective-permute-start | bytes 393224 | tf_op jit(solution)/shard_map/ppermute | solution.py:883
  453.5 56.0 %collective-permute-start.35 = (bf16[256,256]{1,0:T(8,128)(2,1)}, bf16[256,256]{1,0:T(8,128)(2,1)S(1)}, u32[]{:S(2)}, u32[]{:S(2)}) collective-permute-start(bf16[256,256]{1,0:T(8,128)(2,1)} %get-tuple-element.438), channel_id=1, source_target_pairs={{0,24},{8,16},{16,8},{24,0},{1,25},{9,17},{17,9},{25,1},{2,26},{10... | collective-permute-start | bytes 393224 | tf_op jit(solution)/shard_map/ppermute | solution.py:883
  458.0 51.5 %collective-permute-start.32 = (bf16[128,2048]{1,0:T(8,128)(2,1)S(1)}, bf16[128,2048]{1,0:T(8,128)(2,1)S(1)}, u32[]{:S(2)}, u32[]{:S(2)}) collective-permute-start(bf16[128,2048]{1,0:T(8,128)(2,1)S(1)} %copy-done.58), channel_id=1, source_target_pairs={{0,4},{4,0},{1,5},{5,1},{2,6},{6,2},{3,7},{7,3},{8,12},{12,8},{9,1... | collective-permute-start | bytes 1572872 | tf_op jit(solution)/shard_map/ppermute | solution.py:1027
  510.5 36.7 %all-to-all-start.7 = ((bf16[8,3,64,512]{3,2,1,0:T(8,128)(2,1)}), bf16[8,3,64,512]{3,2,1,0:T(8,128)(2,1)S(1)}, u32[]{:S(2)}, u32[]{:S(2)}) async-start(bf16[8,3,64,512]{3,2,1,0:T(8,128)(2,1)} %get-tuple-element.443.out_ref), calls=%async_computation.12 | async-start | bytes 3145728 | tf_op jit(solution)/shard_map/all_to_all | solution.py:877
  (97 other events, 1471.5 us)
Sparse Core Ops, SparseCore 0:
  43.0 87.3 all-gather.2
  267.7 34.9 reduce-scatter.7
  305.5 30.1 reduce-scatter.13
  337.9 42.6 reduce-scatter.9
  382.9 43.1 reduce-scatter.11
  430.1 20.3 reduce-scatter.19
  452.8 36.5 reduce-scatter.15
  492.3 47.7 reduce-scatter.17

commit v3 on v2

--- a/solution.py
+++ b/solution.py
@@ -166,18 +166,25 @@
     doaug = jnp.concatenate([do_t, three_rows(-delta, 32), blank], axis=0).T
     base = (length - 128) // 8 + qi * (tok // 8)
 
+    half = tok // 2
+
     def step(j, dq):
         ks = pl.ds(pl.multiple_of(j * bk, bk), bk)
-        start = base - j * (bk // 8)
-        probs = jnp.exp2(mm(qaug, kaug[:, ks], NN) * SCALE + bias_tile(tb, start, tok, bk))
-        ds = probs * mm(doaug, vaug[:, ks], NN)
-        for c in range(bk // 128):
-            at = pl.ds(start - 16 * c, tok // 8)
-            gb[at] += ds[:, 128 * c : 128 * c + 128].reshape(tok // 8, 8, 128)
-        low = ds.astype(bf16)
-        dvacc[:, ks] += mm(do_t, probs.astype(bf16), NN)
-        dkacc[:, ks] += mm(q_t, low, NN)
-        return dq + mm(low, knat[ks, :], NN)
+        parts = []
+        for i in range(2):
+            rows = slice(i * half, (i + 1) * half)
+            start = base + i * (half // 8) - j * (bk // 8)
+            scores = mm(qaug[rows], kaug[:, ks], NN) * SCALE + bias_tile(tb, start, half, bk)
+            probs = jnp.exp2(scores)
+            ds = probs * mm(doaug[rows], vaug[:, ks], NN)
+            for c in range(bk // 128):
+                at = pl.ds(start - 16 * c, half // 8)
+                gb[at] += ds[:, 128 * c : 128 * c + 128].reshape(half // 8, 8, 128)
+            low = ds.astype(bf16)
+            dvacc[:, ks] += mm(do_t[:, rows], probs.astype(bf16), NN)
+            dkacc[:, ks] += mm(q_t[:, rows], low, NN)
+            parts.append(mm(low, knat[ks, :], NN))
+        return dq + jnp.concatenate(parts, axis=0)
 
     dq = lax.fori_loop(0, nch_ref[qi], step, jnp.zeros((tok, 64), f32))
     out_ref[order(qi), 0] = (dq * 0.125).T.astype(bf16)
@@ -940,7 +947,7 @@
     exp_index = lax.axis_index("expert")
     ctx_arg = ctx_index.astype(jnp.int32).reshape(1)
     pair = ("expert", "ctx")
-    step_k = 512
+    step_k = 1024
 
     def order(p):
         return (p % n_exp) * n_ctx + p // n_exp
@@ -957,7 +964,6 @@
         block_ids[0], bucket_ids, groups, tok
     )
     chunks = (seen + step_k - 1) // step_k
-    chunks_fwd = (seen + 2 * step_k - 1) // (2 * step_k)
 
     flat_ids = expert_ids.reshape(TOP * tok)
     fill_rank = fill_order.reshape(TOP * tok)
@@ -986,9 +992,16 @@
     forward, mixed = [], []
     cot_slots = to_slots(cotangent)
     slots_a, slots_b = cot_slots[:experts], cot_slots[experts:]
-    qkv[0], place, slots_a, slots_b, buck_rev, buck, kmask, qmask, hide = (
+    rows_dev = width // (n_dp * groups)
+    my_rows = ((lax.axis_index("dp") * n_ctx + ctx_index) * n_exp + exp_index) * rows_dev
+    weight_rows = lax.dynamic_slice_in_dim(qkv_weight, my_rows, rows_dev, 0)
+    gain_rows = lax.dynamic_slice_in_dim(attn_gain, my_rows, rows_dev, 0).reshape(rows_dev, 1)
+    qkv[0], place, slots_a, slots_b, buck_rev, buck, kmask, qmask, hide, weight_rows, gain_rows = (
         lax.optimization_barrier(
-            (qkv[0], place, slots_a, slots_b, buck_rev, buck, kmask, qmask, hide)
+            (
+                qkv[0], place, slots_a, slots_b, buck_rev, buck, kmask, qmask, hide, weight_rows,
+                gain_rows,
+            )
         )
     )
     normed_seq = lax.all_gather(after(normed_t, qkv[0]), pair)
@@ -997,7 +1010,7 @@
         if h == heads - 1:
             grad_a = exchange(after(slots_a, arg))
         out = attention_fwd(
-            order, chunks_fwd, table_dev[:, h], buck_rev, kmask, qmask, arg, 2 * step_k
+            order, chunks, table_dev[:, h], buck_rev, kmask, qmask, arg, step_k
         )
         out = after(out, qkv[h + 1] if h < heads - 1 else grad_a, mixed)
         forward.append(out)
@@ -1067,16 +1080,15 @@
     part_c = in_grad(after(xt, outs), grads_in, first, total - first)
     early = outs[heads:]
     mixed_grad = [swap_blocks(part, pair) for part in outs[:heads]]
-    rows_dev = width // (n_dp * groups)
 
     last_own, last_other = [sum_dp(half) for half in part_d]
     sum_a = sum_dp(half_a)
 
     lanes = -(-(3 * HEAD_DIM + 1) // 128) * 128
     dp_arg = lax.axis_index("dp").astype(jnp.int32).reshape(1)
-    backward, grads, late = [], [], []
+    backward, grads = [], []
     for h in range(heads):
-        arg = after(mixed_grad[h], backward if h else part_c)
+        arg = after(mixed_grad[h], backward if h else (part_c, half_a))
         beside = [grads[h - 1]] if h else []
         if h == 0:
             came_c = to_ctx(after(part_c[1], arg))
@@ -1086,7 +1098,7 @@
             arg = after(arg, half_c)
         if h == heads - 1:
             last_came = to_ctx(after(last_other, arg))
-            beside += [last_came, sum_a] + ([late] if h else [])
+            beside += [last_came, sum_a]
         out = attention_bwd(
             order, chunks, table_dev[:, h], buck, kmask, hide, qkv[h], forward[h][0],
             arg, forward[h][1], step_k,
@@ -1096,17 +1108,19 @@
             half_c = add_low((part_c[0], beside[0]))
             sum_c = sum_dp(half_c)
             early_half = sum_dp(add_low(beside[1]))
-        elif h == heads - 1:
-            late = beside[-1]
         backward.append(out)
         grads.append(swap_blocks(out[0], pair))
-        shares = sequence_grad(dp_arg, normed_seq, *out, n_dp, n_exp, copies, lanes)
-        late.append(exchange(shares, "dp"))
+    late = []
+    for out, offsets in reversed(backward):
+        shares = sequence_grad(
+            dp_arg, normed_seq, after(out, backward), offsets, n_dp, n_exp, copies, lanes
+        )
+        late.insert(0, exchange(shares, "dp"))
     in_sums = [sum_a, add_low((last_own, after(last_came, backward))), sum_c]
-    late, grads = lax.optimization_barrier((late, grads))
+    input_grad = input_gradient(layer_input, attn_gain, middle_grad, qkv_weight, grads)
+    late, input_grad = lax.optimization_barrier((late, input_grad))
     late = jnp.concatenate([add_low(parts) for parts in late], axis=1)
     rows_out = swap_blocks(in_swap_order(late.reshape(groups, rows_dev, -1)), pair)
-    input_grad = input_gradient(layer_input, attn_gain, middle_grad, qkv_weight, grads)
     early_half = early_half.reshape(n_ctx, rows_dev, width + 128)
     early_own, early_other = [
         lax.dynamic_index_in_dim(early_half, at, 0, False) for at in (ctx_index, 1 - ctx_index)
@@ -1115,18 +1129,17 @@
         early_other, "ctx", [(0, 1), (1, 0)]
     ).astype(f32)
     expert_in_grad = jnp.concatenate(in_sums, axis=1).astype(f32)
-    expert_down_grad = jnp.concatenate(down_sums, axis=1).astype(f32)
+    expert_down_grad = jnp.concatenate(after(down_sums, backward), axis=1).astype(f32)
     rows_out, input_grad, expert_in_grad, expert_down_grad, early_rows = (
         lax.optimization_barrier(
             (rows_out, input_grad, expert_in_grad, expert_down_grad, early_rows)
         )
     )
-    my_rows = ((lax.axis_index("dp") * n_ctx + ctx_index) * n_exp + exp_index) * rows_dev
     qkv_grad, attn_gain_grad, bias_rows = finish(
         exp_arg,
         rows_out,
-        lax.dynamic_slice_in_dim(qkv_weight, my_rows, rows_dev, 0),
-        lax.dynamic_slice_in_dim(attn_gain, my_rows, rows_dev, 0).reshape(rows_dev, 1),
+        weight_rows,
+        gain_rows,
         heads,
         lanes,
         n_ctx,

time: 594 us -> 594 us (level)
  the two profiles are of different devices: /device:TPU:1 before, /device:TPU:9 now
where the time goes in v3:
time: 594 us; the launch traced here: 582 us
  Pallas kernels  368 us (62%)
  starting transfers between devices  77 us (13%)
  waiting for transfers between devices  64 us (11%)
  other arithmetic  29.6 us (5%)
  local copies, waits for them, and re-layouts  19.1 us (3%)
  between operations  15.5 us (3%)
  matrix products  8.88 us (1%)
    pallas_call x2, Pallas kernels, attention_bwd(): pl.pallas_call(functools.partial(attention_bwd_kernel, bk, order), grid_s...  93.6 us
    pallas_call x2, Pallas kernels, attention_fwd(): pl.pallas_call(functools.partial(attention_fwd_kernel, bk, order), grid_s...  60.5 us
    pallas_call x2, Pallas kernels, expert_bwd(): pl.pallas_call(functools.partial(expert_bwd_kernel, steps, groups), grid=...  51.2 us
    pallas_call x2, Pallas kernels, expert_fwd(): pl.pallas_call(functools.partial(expert_fwd_kernel, steps, groups), grid=...  43.2 us
    all_to_all x9, starting transfers between devices, swap_blocks(): return lax.all_to_all(blocks, axes, split_axis=0, concat_axis=0, tiled=True)  40.7 us
    ppermute x33, waiting for transfers between devices, exchange(): lax.ppermute(parts[d], axis, [(i, i ^ d) for i in range(n)])  34.5 us
    pallas_call x4, Pallas kernels, in_grad(): pl.pallas_call(in_grad_kernel, grid=(count,), in_specs=[pl.BlockSpec((wid...  32.8 us
    ppermute x33, starting transfers between devices, exchange(): lax.ppermute(parts[d], axis, [(i, i ^ d) for i in range(n)])  28.1 us
  transfers between devices with their start and end apart: 57, of which 15 were waited for; matrix products, arithmetic and copies ran while one was open for 7% of the time, Pallas kernels for 61%

profile of v3, /device:TPU:9, one launch (start us, length us, event | category | flops | bytes accessed | tf_op | source)
XLA Modules:
  0.0 582.4 jit_solution(14132625552502812548)
XLA Ops:
  7.2 9.0 %project.1 = (bf16[1024,512]{1,0:T(8,128)(2,1)}, bf16[8,3,64,512]{3,2,1,0:T(8,128)(2,1)}, bf16[8,3,64,512]{3,2,1,0:T(8,128)(2,1)}) custom-call(bf16[512,1024]{1,0:T(8,128)(2,1)} %x_ref.5, f32[1,1024]{1,0:T(1,128)} %bitcast.62, bf16[1024,3072]{1,0:T(8,128)(2,1)} %refs_3_.3, bf16[1024,3072]{1,0:T(8,128)(2,1)} %refs_3_.3, bf16[1024,3072]{1,0:T(8,128)(2,1)} %refs_3_.3, ...), custom_call_target="tpu_custom_call" | custom-call | flops 3221225472 | bytes 11534336 | tf_op jit(solution)/shard_map/project/pallas_call | solution.py:537
  42.1 5.0 all-to-all-start.1
  49.7 30.3 %attention_fwd.2 = (bf16[8,64,512]{2,1,0:T(8,128)(2,1)}, f32[8,1,512]{2,1,0:T(1,128)}) custom-call(s32[8]{0:T(128)} %and_select_fusion.nch_ref, f32[32]{0:T(128)} %get-tuple-element.511.tab_ref, s32[8,8192]{1,0:T(8,128)} %broadcast_in_dim.57.buck_ref, bf16[64,4096]{1,0:T(8,128)(2,1)} %maximum_maximum_fusion.kmask_ref, ...), custom_call_target="tpu_custom_call" | custom-call | flops 16777216000 | bytes 2097152 | tf_op jit(solution)/shard_map/attention_fwd/pallas_call | solution.py:96
  86.4 30.2 %attention_fwd.3 = (bf16[8,64,512]{2,1,0:T(8,128)(2,1)}, f32[8,1,512]{2,1,0:T(1,128)}) custom-call(s32[8]{0:T(128)} %and_select_fusion.nch_ref, f32[32]{0:T(128)} %get-tuple-element.510.tab_ref, s32[8,8192]{1,0:T(8,128)} %broadcast_in_dim.57.buck_ref, bf16[64,4096]{1,0:T(8,128)(2,1)} %maximum_maximum_fusion.kmask_ref, ...), custom_call_target="tpu_custom_call" | custom-call | flops 16777216000 | bytes 2097152 | tf_op jit(solution)/shard_map/attention_fwd/pallas_call | solution.py:96
  117.3 6.5 %collective-permute-done.2.refs_3_ = bf16[160,1024]{1,0:T(8,128)(2,1)S(1)} collective-permute-done((bf16[160,1024]{1,0:T(8,128)(2,1)S(1)}, bf16[160,1024]{1,0:T(8,128)(2,1)S(1)}, u32[]{:S(2)}, u32[]{:S(2)}) %collective-permute-start.2) | collective-permute-done | bytes 327712 | tf_op jit(solution)/shard_map/ppermute | solution.py:890
  129.3 6.2 %all-to-all-done.3 = bf16[8,64,512]{2,1,0:T(8,128)(2,1)S(1)} async-done(((bf16[8,64,512]{2,1,0:T(8,128)(2,1)}), bf16[8,64,512]{2,1,0:T(8,128)(2,1)S(1)}, u32[]{:S(2)}, u32[]{:S(2)}) %all-to-all-start.3) | async-done | bytes 524320 | tf_op jit(solution)/shard_map/all_to_all | solution.py:884
  136.4 8.0 %route.1 = (f32[512,1024]{1,0:T(8,128)}, bf16[512,1024]{1,0:T(8,128)(2,1)}, f32[512,4]{1,0:T(8,128)}, bf16[160,1152]{1,0:T(8,128)(2,1)}, bf16[160,1152]{1,0:T(8,...) custom-call(bf16[512,1024]{1,0:T(8,128)(2,1)} %x_ref.5, ...), custom_call_target="tpu_custom_call" | custom-call | flops 2415919104 | bytes 8388608 | tf_op jit(solution)/shard_map/route/pallas_call | solution.py:804
  148.9 6.5 %collective-permute-done.4.refs_2_.refs_10_.refs_6_ = bf16[160,1152]{1,0:T(8,128)(2,1)S(1)} collective-permute-done((bf16[160,1152]{1,0:T(8,128)(2,1)}, bf16[160,1152]{1,0:T(8,128)(2,1)S(1)}, u32[]{:S(2)}, u32[]{:S(2)}) %collective-permute-start.4) | collective-permute-done | bytes 368672 | tf_op jit(solution)/shard_map/ppermute | solution.py:890
  155.4 8.5 %collective-permute-done.5.refs_3_.refs_11_.refs_7_ = bf16[160,1152]{1,0:T(8,128)(2,1)S(1)} collective-permute-done((bf16[160,1152]{1,0:T(8,128)(2,1)}, bf16[160,1152]{1,0:T(8,128)(2,1)S(1)}, u32[]{:S(2)}, u32[]{:S(2)}) %collective-permute-start.5) | collective-permute-done | bytes 368672 | tf_op jit(solution)/shard_map/ppermute | solution.py:890
  165.9 21.6 %expert_fwd.2 = (bf16[2816,640]{1,0:T(8,128)(2,1)}, bf16[640,2816]{1,0:T(8,128)(2,1)}, bf16[640,2816]{1,0:T(8,128)(2,1)}, bf16[160,1024]{1,0:T(8,128)(2,1)}, bf1...) custom-call(bf16[1,1024,5632]{2,1,0:T(8,128)(2,1)} %wu_ref.7, ...), custom_call_target="tpu_custom_call" | custom-call | flops 18454937600 | bytes 30736384 | tf_op jit(solution)/shard_map/expert_fwd/pallas_call | solution.py:318
  187.5 5.9 %collective-permute-done.11.refs_7_.refs_3_ = bf16[160,1024]{1,0:T(8,128)(2,1)} collective-permute-done((bf16[160,1024]{1,0:T(8,128)(2,1)S(1)}, bf16[160,1024]{1,0:T(8,128)(2,1)}, u32[]{:S(2)}, u32[]{:S(2)}) %collective-permute-start.11) | collective-permute-done | bytes 327712 | tf_op jit(solution)/shard_map/ppermute | solution.py:890
  195.6 21.6 %expert_fwd.3 = (bf16[2816,640]{1,0:T(8,128)(2,1)}, bf16[640,2816]{1,0:T(8,128)(2,1)}, bf16[640,2816]{1,0:T(8,128)(2,1)}, bf16[160,1024]{1,0:T(8,128)(2,1)}, bf1...) custom-call(bf16[1,1024,5632]{2,1,0:T(8,128)(2,1)} %wu_ref.7, ...), custom_call_target="tpu_custom_call" | custom-call | flops 18454937600 | bytes 30736384 | tf_op jit(solution)/shard_map/expert_fwd/pallas_call | solution.py:318
  219.5 9.6 %down_grad.2 = (bf16[4,1536,128]{2,1,0:T(8,128)(2,1)}, bf16[4,1536,128]{2,1,0:T(8,128)(2,1)}) custom-call(s32[1]{0:T(128)} %bitcast.14.ctx_ref, bf16[160,1024]{1,0:T(8,128)(2,1)} %convolution_convert_fusion.7.refs_0_, bf16[160,1024]{1,0:T(8,128)(2,1)} %copy-done.55, bf16[160,1024]{1,0:T(8,128)(2,1)} %copy-done.56, bf16[160,1024]{1,0:T(8,128)(2,1)} %copy-done.57, ...), custom_call_target="tpu_custom_call" | custom-call | flops 8053063680 | bytes 9699328 | tf_op jit(solution)/shard_map/down_grad/pallas_call | solution.py:496
  230.0 8.6 %down_grad.3 = (bf16[4,1280,128]{2,1,0:T(8,128)(2,1)}, bf16[4,1280,128]{2,1,0:T(8,128)(2,1)}) custom-call(s32[1]{0:T(128)} %bitcast.14.ctx_ref, bf16[160,1024]{1,0:T(8,128)(2,1)} %convolution_convert_fusion.7.refs_0_, bf16[160,1024]{1,0:T(8,128)(2,1)} %copy-done.55, bf16[160,1024]{1,0:T(8,128)(2,1)} %copy-done.56, bf16[160,1024]{1,0:T(8,128)(2,1)} %copy-done.57, ...), custom_call_target="tpu_custom_call" | custom-call | flops 6710886400 | bytes 8519680 | tf_op jit(solution)/shard_map/down_grad/pallas_call | solution.py:496
  238.6 25.4 %expert_bwd.2 = (bf16[2,640,2816]{2,1,0:T(8,128)(2,1)}, bf16[160,1024]{1,0:T(8,128)(2,1)}, bf16[160,1024]{1,0:T(8,128)(2,1)}, bf16[160,1024]{1,0:T(8,128)(2,1)}, bf16[160,1024]{1,0:T(8,128)(2,1)}) custom-call(bf16[640,2816]{1,0:T(8,128)(2,1)} %get-tuple-element.300.act_ref, bf16[640,2816]{1,0:T(8,128)(2,1)} %get-tuple-element.301.slope_ref, ...), custom_call_target="tpu_custom_call" | custom-call | flops 18454937600 | bytes 34340864 | tf_op jit(solution)/shard_map/expert_bwd/pallas_call | solution.py:373
  270.5 25.7 %expert_bwd.3 = (bf16[2,640,2816]{2,1,0:T(8,128)(2,1)}, bf16[160,1024]{1,0:T(8,128)(2,1)}, bf16[160,1024]{1,0:T(8,128)(2,1)}, bf16[160,1024]{1,0:T(8,128)(2,1)}, bf16[160,1024]{1,0:T(8,128)(2,1)}) custom-call(bf16[640,2816]{1,0:T(8,128)(2,1)} %get-tuple-element.320.act_ref, bf16[640,2816]{1,0:T(8,128)(2,1)} %get-tuple-element.321.slope_ref, ...), custom_call_target="tpu_custom_call" | custom-call | flops 18454937600 | bytes 34340864 | tf_op jit(solution)/shard_map/expert_bwd/pallas_call | solution.py:373
  301.8 5.3 turn.1.refs_0_.refs_1_.refs_2_.refs_3_
  309.7 5.8 in_grad.4
  316.2 5.5 in_grad.5
  321.7 10.7 %in_grad.6 = (bf16[512,2048]{1,0:T(8,128)(2,1)}, bf16[512,2048]{1,0:T(8,128)(2,1)}) custom-call(bf16[1024,1280]{1,0:T(8,128)(2,1)} %turn.1.refs_0_.refs_1_.refs_2_.refs_3_, bf16[1024,1280]{1,0:T(8,128)(2,1)} %turn.1.refs_0_.refs_1_.refs_2_.refs_3_, bf16[1024,1280]{1,0:T(8,128)(2,1)} %turn.1.refs_0_.refs_1_.refs_2_.refs_3_, ...), custom_call_target="tpu_custom_call" | custom-call | flops 10737418240 | bytes 12058624 | tf_op jit(solution)/shard_map/in_grad/pallas_call | solution.py:450
  336.6 15.5 %combine.1 = (bf16[512,1024]{1,0:T(8,128)(2,1)}, f32[512,1024]{1,0:T(8,128)}, bf16[8,64,512]{2,1,0:T(8,128)(2,1)}, bf16[8,64,512]{2,1,0:T(8,128)(2,1)}, bf16[256...) custom-call(s32[1]{0:T(128)} %bitcast.exp_ref, ...), custom_call_target="tpu_custom_call" | custom-call | flops 6174015488 | bytes 18874368 | tf_op jit(solution)/shard_map/combine/pallas_call | solution.py:705
  353.9 5.2 all-to-all-start.4
  359.1 10.7 %in_grad.7 = (bf16[512,2048]{1,0:T(8,128)(2,1)}, bf16[512,2048]{1,0:T(8,128)(2,1)}) custom-call(bf16[1024,1280]{1,0:T(8,128)(2,1)} %turn.1.refs_0_.refs_1_.refs_2_.refs_3_, bf16[1024,1280]{1,0:T(8,128)(2,1)} %turn.1.refs_0_.refs_1_.refs_2_.refs_3_, bf16[1024,1280]{1,0:T(8,128)(2,1)} %turn.1.refs_0_.refs_1_.refs_2_.refs_3_, ...), custom_call_target="tpu_custom_call" | custom-call | flops 10737418240 | bytes 12058624 | tf_op jit(solution)/shard_map/in_grad/pallas_call | solution.py:450
  379.5 46.8 %attention_bwd.2 = (bf16[8,3,64,512]{3,2,1,0:T(8,128)(2,1)}, f32[32,128]{1,0:T(8,128)}) custom-call(s32[8]{0:T(128)} %and_select_fusion.nch_ref, f32[32]{0:T(128)} %get-tuple-element.511.tab_ref, s32[8,8192]{1,0:T(8,128)} %broadcast_in_dim.58.buck_ref, bf16[64,4096]{1,0:T(8,128)(2,1)} %maximum_maximum_fusion.kmask_ref, ...), custom_call_target="tpu_custom_call" | custom-call | flops 41943040000 | bytes 4194304 | tf_op jit(solution)/shard_map/attention_bwd/pallas_call | solution.py:220
  437.9 4.6 add_convert_fusion
  443.8 6.9 %reduce-scatter.20.cloned.1.call-done = bf16[64,1152]{1,0:T(8,128)(2,1)} async-done(((bf16[256,1152]{1,0:T(8,128)(2,1)}), bf16[64,1152]{1,0:T(8,128)(2,1)}) %reduce-scatter.20.cloned.1.call-update) | async-done | bytes 147472 | tf_op jit(solution)/shard_map/reduce_scatter | solution.py:1037
  453.8 46.8 %attention_bwd.3 = (bf16[8,3,64,512]{3,2,1,0:T(8,128)(2,1)}, f32[32,128]{1,0:T(8,128)}) custom-call(s32[8]{0:T(128)} %and_select_fusion.nch_ref, f32[32]{0:T(128)} %get-tuple-element.510.tab_ref, s32[8,8192]{1,0:T(8,128)} %broadcast_in_dim.58.buck_ref, bf16[64,4096]{1,0:T(8,128)(2,1)} %maximum_maximum_fusion.kmask_ref, ...), custom_call_target="tpu_custom_call" | custom-call | flops 41943040000 | bytes 4194304 | tf_op jit(solution)/shard_map/attention_bwd/pallas_call | solution.py:220
  501.6 5.6 all-to-all-start.7
  509.1 9.0 %sequence_grad.3 = (bf16[256,256]{1,0:T(8,128)(2,1)}, bf16[256,256]{1,0:T(8,128)(2,1)}, bf16[256,256]{1,0:T(8,128)(2,1)}, bf16[256,256]{1,0:T(8,128)(2,1)}) custom-call(s32[1]{0:T(128)} %bitcast.15.dp_ref, bf16[8,3,64,512]{3,2,1,0:T(8,128)(2,1)} %get-tuple-element.443.out_ref, f32[32,128]{1,0:T(8,128)} %get-tuple-element.437.offsets_ref, ...), custom_call_target="tpu_custom_call" | custom-call | flops 1610612736 | bytes 9961472 | tf_op jit(solution)/shard_map/sequence_grad/pallas_call | solution.py:855
  522.4 9.0 %sequence_grad.2 = (bf16[256,256]{1,0:T(8,128)(2,1)}, bf16[256,256]{1,0:T(8,128)(2,1)}, bf16[256,256]{1,0:T(8,128)(2,1)}, bf16[256,256]{1,0:T(8,128)(2,1)}) custom-call(s32[1]{0:T(128)} %bitcast.15.dp_ref, bf16[8,3,64,512]{3,2,1,0:T(8,128)(2,1)} %get-tuple-element.438.out_ref, f32[32,128]{1,0:T(8,128)} %get-tuple-element.429.offsets_ref, ...), custom_call_target="tpu_custom_call" | custom-call | flops 1610612736 | bytes 9961472 | tf_op jit(solution)/shard_map/sequence_grad/pallas_call | solution.py:855
  538.3 11.2 %input_grad.1 = f32[512,1024]{1,0:T(8,128)} custom-call(bf16[512,1024]{1,0:T(8,128)(2,1)} %x_ref.5, f32[1,1024]{1,0:T(1,128)} %bitcast.63, f32[512,1024]{1,0:T(8,128)} %get-tuple-element.448.mid_ref, bf16[1024,3072]{1,0:T(8,128)(2,1)} %refs_3_.3, bf16[1024,3072]{1,0:T(8,128)(2,1)} %refs_3_.3, bf16[1024,3072]{1,0:T(8,128)(2,1)} %refs_3_.3, ...), custom_call_target="tpu_custom_call" | custom-call | flops 3221225472 | bytes 14680064 | tf_op jit(solution)/shard_map/input_grad/pallas_call | solution.py:586
  551.7 4.8 collective-permute-done.35
  (323 shorter events, 134.8 us)
Async XLA Ops:
  20.8 196.5 %all-gather.3.cloned.1.call-start = ((), (), s32[]{:S(2)}) async-start(), calls=%async_computation.23 | async-start | bytes 9437184 | tf_op jit(solution)/shard_map/all_gather | solution.py:1007
  42.1 38.0 %all-to-all-start.1 = ((bf16[8,3,64,512]{3,2,1,0:T(8,128)(2,1)}), bf16[8,3,64,512]{3,2,1,0:T(8,128)(2,1)}, u32[]{:S(2)}, u32[]{:S(2)}) async-start(bf16[8,3,64,512]{3,2,1,0:T(8,128)(2,1)} %get-tuple-element.251), calls=%async_computation.1 | async-start | bytes 3145728 | tf_op jit(solution)/shard_map/all_to_all | solution.py:884
  80.1 43.8 %all-to-all-start.2 = ((bf16[8,64,512]{2,1,0:T(8,128)(2,1)}), bf16[8,64,512]{2,1,0:T(8,128)(2,1)S(1)}, u32[]{:S(2)}, u32[]{:S(2)}) async-start(bf16[8,64,512]{2,1,0:T(8,128)(2,1)} %get-tuple-element.252.o_ref), calls=%async_computation.2 | async-start | bytes 1048576 | tf_op jit(solution)/shard_map/all_to_all | solution.py:884
  84.2 32.3 %collective-permute-start = (bf16[160,1024]{1,0:T(8,128)(2,1)S(1)}, bf16[160,1024]{1,0:T(8,128)(2,1)S(1)}, u32[]{:S(2)}, u32[]{:S(2)}) collective-permute-start(bf16[160,1024]{1,0:T(8,128)(2,1)S(1)} %copy-done.37), channel_id=1, source_target_pairs={{0,1},{1,0},{2,3},{3,2},{4,5},{5,4},{6,7},{7,6},{8,9},{9,8},{10,11... | collective-permute-start | bytes 983048 | tf_op jit(solution)/shard_map/ppermute | solution.py:890
  84.3 32.2 %collective-permute-start.1 = (bf16[160,1024]{1,0:T(8,128)(2,1)S(1)}, bf16[160,1024]{1,0:T(8,128)(2,1)S(1)}, u32[]{:S(2)}, u32[]{:S(2)}) collective-permute-start(bf16[160,1024]{1,0:T(8,128)(2,1)S(1)} %copy-done.36), channel_id=1, source_target_pairs={{0,2},{1,3},{2,0},{3,1},{4,6},{5,7},{6,4},{7,5},{8,10},{9,11},{10,... | collective-permute-start | bytes 983048 | tf_op jit(solution)/shard_map/ppermute | solution.py:890
  86.0 37.9 %collective-permute-start.2 = (bf16[160,1024]{1,0:T(8,128)(2,1)S(1)}, bf16[160,1024]{1,0:T(8,128)(2,1)S(1)}, u32[]{:S(2)}, u32[]{:S(2)}) collective-permute-start(bf16[160,1024]{1,0:T(8,128)(2,1)S(1)} %copy-done.35), channel_id=1, source_target_pairs={{0,3},{1,2},{2,1},{3,0},{4,7},{5,6},{6,5},{7,4},{8,11},{9,10},{10,... | collective-permute-start | bytes 983048 | tf_op jit(solution)/shard_map/ppermute | solution.py:890
  127.3 226.6 %reduce-scatter.8.cloned.1.call-start = ((), (), s32[]{:S(2)}) async-start(), calls=%async_computation.16 | async-start | bytes 1966080 | tf_op jit(solution)/shard_map/reduce_scatter | solution.py:1037
  146.9 40.5 %collective-permute-start.7 = (bf16[160,1152]{1,0:T(8,128)(2,1)}, bf16[160,1152]{1,0:T(8,128)(2,1)S(1)}, u32[]{:S(2)}, u32[]{:S(2)}) collective-permute-start(bf16[160,1152]{1,0:T(8,128)(2,1)} %get-tuple-element.285), channel_id=1, source_target_pairs={{0,2},{1,3},{2,0},{3,1},{4,6},{5,7},{6,4},{7,5},{8,10},{9,11},{10,... | collective-permute-start | bytes 1105928 | tf_op jit(solution)/shard_map/ppermute | solution.py:890
  147.5 40.0 %collective-permute-start.8 = (bf16[160,1152]{1,0:T(8,128)(2,1)}, bf16[160,1152]{1,0:T(8,128)(2,1)S(1)}, u32[]{:S(2)}, u32[]{:S(2)}) collective-permute-start(bf16[160,1152]{1,0:T(8,128)(2,1)} %get-tuple-element.286), channel_id=1, source_target_pairs={{0,3},{1,2},{2,1},{3,0},{4,7},{5,6},{6,5},{7,4},{8,11},{9,10},{10,... | collective-permute-start | bytes 1105928 | tf_op jit(solution)/shard_map/ppermute | solution.py:890
  164.6 28.8 %collective-permute-start.11 = (bf16[160,1024]{1,0:T(8,128)(2,1)S(1)}, bf16[160,1024]{1,0:T(8,128)(2,1)}, u32[]{:S(2)}, u32[]{:S(2)}) collective-permute-start(bf16[160,1024]{1,0:T(8,128)(2,1)S(1)} %copy-done.32), channel_id=1, source_target_pairs={{0,3},{1,2},{2,1},{3,0},{4,7},{5,6},{6,5},{7,4},{8,11},{9,10},{10,... | collective-permute-start | bytes 983048 | tf_op jit(solution)/shard_map/ppermute | solution.py:890
  217.3 46.8 %collective-permute-start.15 = (bf16[160,1024]{1,0:T(8,128)(2,1)}, bf16[160,1024]{1,0:T(8,128)(2,1)S(1)}, u32[]{:S(2)}, u32[]{:S(2)}) collective-permute-start(bf16[160,1024]{1,0:T(8,128)(2,1)} %get-tuple-element.316), channel_id=1, source_target_pairs={{0,1},{1,0},{2,3},{3,2},{4,5},{5,4},{6,7},{7,6},{8,9},{9,8},{10,11... | collective-permute-start | bytes 983048 | tf_op jit(solution)/shard_map/ppermute | solution.py:890
  217.4 46.7 %collective-permute-start.16 = (bf16[160,1024]{1,0:T(8,128)(2,1)}, bf16[160,1024]{1,0:T(8,128)(2,1)S(1)}, u32[]{:S(2)}, u32[]{:S(2)}) collective-permute-start(bf16[160,1024]{1,0:T(8,128)(2,1)} %get-tuple-element.317), channel_id=1, source_target_pairs={{0,2},{1,3},{2,0},{3,1},{4,6},{5,7},{6,4},{7,5},{8,10},{9,11},{10,... | collective-permute-start | bytes 983048 | tf_op jit(solution)/shard_map/ppermute | solution.py:890
  218.0 46.1 %collective-permute-start.17 = (bf16[160,1024]{1,0:T(8,128)(2,1)}, bf16[160,1024]{1,0:T(8,128)(2,1)}, u32[]{:S(2)}, u32[]{:S(2)}) collective-permute-start(bf16[160,1024]{1,0:T(8,128)(2,1)} %get-tuple-element.318), channel_id=1, source_target_pairs={{0,3},{1,2},{2,1},{3,0},{4,7},{5,6},{6,5},{7,4},{8,11},{9,10},{10,... | collective-permute-start | bytes 983048 | tf_op jit(solution)/shard_map/ppermute | solution.py:890
  229.1 36.4 %collective-permute-start.18 = (bf16[4,1536,128]{2,1,0:T(8,128)(2,1)}, bf16[4,1536,128]{2,1,0:T(8,128)(2,1)S(1)}, u32[]{:S(2)}, u32[]{:S(2)}) collective-permute-start(bf16[4,1536,128]{2,1,0:T(8,128)(2,1)} %get-tuple-element.331), channel_id=1, source_target_pairs={{0,4},{4,0},{1,5},{5,1},{2,6},{6,2},{3,7},{7,3},{8,12},{12,8},{9,1... | collective-permute-start | bytes 4718600 | tf_op jit(solution)/shard_map/ppermute | solution.py:1040
  267.2 159.1 %reduce-scatter.14.cloned.1.call-start = ((), (), s32[]{:S(2)}) async-start(), calls=%async_computation.19 | async-start | bytes 1638400 | tf_op jit(solution)/shard_map/reduce_scatter | solution.py:1037
  267.3 29.0 %collective-permute-start.19 = (bf16[160,1024]{1,0:T(8,128)(2,1)}, bf16[160,1024]{1,0:T(8,128)(2,1)S(1)}, u32[]{:S(2)}, u32[]{:S(2)}) collective-permute-start(bf16[160,1024]{1,0:T(8,128)(2,1)} %get-tuple-element.357), channel_id=1, source_target_pairs={{0,1},{1,0},{2,3},{3,2},{4,5},{5,4},{6,7},{7,6},{8,9},{9,8},{10,11... | collective-permute-start | bytes 983048 | tf_op jit(solution)/shard_map/ppermute | solution.py:890
  269.7 30.5 %collective-permute-start.22 = (bf16[4,1280,128]{2,1,0:T(8,128)(2,1)}, bf16[4,1280,128]{2,1,0:T(8,128)(2,1)S(1)}, u32[]{:S(2)}, u32[]{:S(2)}) collective-permute-start(bf16[4,1280,128]{2,1,0:T(8,128)(2,1)} %get-tuple-element.375), channel_id=1, source_target_pairs={{0,4},{4,0},{1,5},{5,1},{2,6},{6,2},{3,7},{7,3},{8,12},{12,8},{9,1... | collective-permute-start | bytes 3932168 | tf_op jit(solution)/shard_map/ppermute | solution.py:1040
  301.7 126.9 %reduce-scatter.10.cloned.1.call-start = ((), (), s32[]{:S(2)}) async-start(), calls=%async_computation.17 | async-start | bytes 2621440 | tf_op jit(solution)/shard_map/reduce_scatter | solution.py:1037
  334.7 93.9 %reduce-scatter.12.cloned.1.call-start = ((), (), s32[]{:S(2)}) async-start(), calls=%async_computation.18 | async-start | bytes 2621440 | tf_op jit(solution)/shard_map/reduce_scatter | solution.py:1037
  371.4 54.9 %all-to-all-start.5 = ((bf16[8,64,512]{2,1,0:T(8,128)(2,1)}), bf16[8,64,512]{2,1,0:T(8,128)(2,1)}, u32[]{:S(2)}, u32[]{:S(2)}) async-start(bf16[8,64,512]{2,1,0:T(8,128)(2,1)} %get-tuple-element.409), calls=%async_computation.9 | async-start | bytes 1048576 | tf_op jit(solution)/shard_map/all_to_all | solution.py:884
  375.7 75.0 %reduce-scatter.20.cloned.1.call-start = ((), (), s32[]{:S(2)}) async-start(), calls=%async_computation.22 | async-start | bytes 737280 | tf_op jit(solution)/shard_map/reduce_scatter | solution.py:1037
  375.9 50.5 %collective-permute-start.29 = (bf16[256,1152]{1,0:T(8,128)(2,1)}, bf16[256,1152]{1,0:T(8,128)(2,1)S(1)}, u32[]{:S(2)}, u32[]{:S(2)}) collective-permute-start(bf16[256,1152]{1,0:T(8,128)(2,1)} %get-tuple-element.423), channel_id=1, source_target_pairs={{0,1},{1,0},{2,3},{3,2},{4,5},{5,4},{6,7},{7,6},{8,9},{9,8},{10,11... | collective-permute-start | bytes 1769480 | tf_op jit(solution)/shard_map/ppermute | solution.py:890
  376.1 50.3 %collective-permute-start.30 = (bf16[256,1152]{1,0:T(8,128)(2,1)}, bf16[256,1152]{1,0:T(8,128)(2,1)}, u32[]{:S(2)}, u32[]{:S(2)}) collective-permute-start(bf16[256,1152]{1,0:T(8,128)(2,1)} %get-tuple-element.424), channel_id=1, source_target_pairs={{0,2},{1,3},{2,0},{3,1},{4,6},{5,7},{6,4},{7,5},{8,10},{9,11},{10,... | collective-permute-start | bytes 1769480 | tf_op jit(solution)/shard_map/ppermute | solution.py:890
  377.7 48.7 %collective-permute-start.31 = (bf16[256,1152]{1,0:T(8,128)(2,1)}, bf16[256,1152]{1,0:T(8,128)(2,1)}, u32[]{:S(2)}, u32[]{:S(2)}) collective-permute-start(bf16[256,1152]{1,0:T(8,128)(2,1)} %get-tuple-element.425), channel_id=1, source_target_pairs={{0,3},{1,2},{2,1},{3,0},{4,7},{5,6},{6,5},{7,4},{8,11},{9,10},{10,... | collective-permute-start | bytes 1769480 | tf_op jit(solution)/shard_map/ppermute | solution.py:890
  378.1 50.5 %collective-permute-start.28 = (bf16[512,2048]{1,0:T(8,128)(2,1)}, bf16[512,2048]{1,0:T(8,128)(2,1)S(1)}, u32[]{:S(2)}, u32[]{:S(2)}) collective-permute-start(bf16[512,2048]{1,0:T(8,128)(2,1)} %get-tuple-element.421), channel_id=1, source_target_pairs={{0,4},{4,0},{1,5},{5,1},{2,6},{6,2},{3,7},{7,3},{8,12},{12,8},{9,1... | collective-permute-start | bytes 6291464 | tf_op jit(solution)/shard_map/ppermute | solution.py:1040
  431.8 69.0 %reduce-scatter.16.cloned.1.call-start = ((), (), s32[]{:S(2)}) async-start(), calls=%async_computation.20 | async-start | bytes 1966080 | tf_op jit(solution)/shard_map/reduce_scatter | solution.py:1037
  433.3 67.6 %all-to-all-start.6 = ((bf16[8,3,64,512]{3,2,1,0:T(8,128)(2,1)}), bf16[8,3,64,512]{3,2,1,0:T(8,128)(2,1)S(1)}, u32[]{:S(2)}, u32[]{:S(2)}) async-start(bf16[8,3,64,512]{3,2,1,0:T(8,128)(2,1)} %get-tuple-element.438.out_ref), calls=%async_computation.10 | async-start | bytes 3145728 | tf_op jit(solution)/shard_map/all_to_all | solution.py:884
  437.6 124.9 %reduce-scatter.18.cloned.1.call-start = ((), (), s32[]{:S(2)}) async-start(), calls=%async_computation.21 | async-start | bytes 2621440 | tf_op jit(solution)/shard_map/reduce_scatter | solution.py:1037
  442.4 58.4 %collective-permute-start.32 = (bf16[128,2048]{1,0:T(8,128)(2,1)S(1)}, bf16[128,2048]{1,0:T(8,128)(2,1)S(1)}, u32[]{:S(2)}, u32[]{:S(2)}) collective-permute-start(bf16[128,2048]{1,0:T(8,128)(2,1)S(1)} %copy-done.52), channel_id=1, source_target_pairs={{0,4},{4,0},{1,5},{5,1},{2,6},{6,2},{3,7},{7,3},{8,12},{12,8},{9,1... | collective-permute-start | bytes 1572872 | tf_op jit(solution)/shard_map/ppermute | solution.py:1040
  452.6 54.6 %collective-permute-start.39 = (bf16[32,1152]{0,1:T(8,128)(2,1)}, bf16[32,1152]{0,1:T(8,128)(2,1)}, u32[]{:S(2)}, u32[]{:S(2)}) collective-permute-start(bf16[32,1152]{0,1:T(8,128)(2,1)} %bitcast.21), channel_id=1, source_target_pairs={{0,4},{4,0},{1,5},{5,1},{2,6},{6,2},{3,7},{7,3},{8,12},{12,8},{9,1... | collective-permute-start | bytes 221192 | tf_op jit(solution)/shard_map/ppermute | solution.py:1128
  501.6 35.5 %all-to-all-start.7 = ((bf16[8,3,64,512]{3,2,1,0:T(8,128)(2,1)}), bf16[8,3,64,512]{3,2,1,0:T(8,128)(2,1)S(1)}, u32[]{:S(2)}, u32[]{:S(2)}) async-start(bf16[8,3,64,512]{3,2,1,0:T(8,128)(2,1)} %get-tuple-element.443.out_ref), calls=%async_computation.12 | async-start | bytes 3145728 | tf_op jit(solution)/shard_map/all_to_all | solution.py:884
  521.1 28.4 %collective-permute-start.37 = (bf16[256,256]{1,0:T(8,128)(2,1)}, bf16[256,256]{1,0:T(8,128)(2,1)S(1)}, u32[]{:S(2)}, u32[]{:S(2)}) collective-permute-start(bf16[256,256]{1,0:T(8,128)(2,1)} %get-tuple-element.446), channel_id=1, source_target_pairs={{0,16},{8,24},{16,0},{24,8},{1,17},{9,25},{17,1},{25,9},{2,18},{10... | collective-permute-start | bytes 393224 | tf_op jit(solution)/shard_map/ppermute | solution.py:890
  (94 other events, 1448.5 us)
Sparse Core Ops, SparseCore 0:
  42.2 87.8 all-gather.2
  267.3 33.1 reduce-scatter.7
  303.4 30.0 reduce-scatter.13
  335.7 42.2 reduce-scatter.9
  380.2 43.1 reduce-scatter.11
  431.9 18.7 reduce-scatter.19
  453.0 35.3 reduce-scatter.15
  491.2 52.6 reduce-scatter.17

commit v4 on v3

--- a/solution.py
+++ b/solution.py
@@ -817,10 +817,11 @@
       weight, *mixed)
 
 
-def sequence_grad_kernel(n_exp, copies, dp_ref, out_ref, offsets_ref, *refs):
+def sequence_grad_kernel(heads, n_exp, copies, dp_ref, *refs):
+    outs, offsets, refs = refs[:heads], refs[heads : 2 * heads], refs[2 * heads :]
     normed_refs, (*shares, acc) = refs[:4], refs[4:]
     step = pl.program_id(0)
-    width, lanes = acc.shape
+    width, lanes = acc.shape[0], acc.shape[1] // heads
     own = 3 * HEAD_DIM
 
     @pl.when(step == 0)
@@ -828,52 +829,56 @@
         acc[...] = jnp.zeros_like(acc)
 
     normed = jnp.concatenate([ref[0] for ref in normed_refs], axis=0)
-    acc[:, 0:own] += mm(normed, out_ref[0].reshape(own, out_ref.shape[3]), NT)
+    for h, out_ref in enumerate(outs):
+        rows = out_ref[0].reshape(own, out_ref.shape[3])
+        acc[:, h * lanes : h * lanes + own] += mm(normed, rows, NT)
 
     @pl.when(step == pl.num_programs(0) - 1)
     def _():
-        count = offsets_ref.shape[0]
+        count = offsets[0].shape[0]
         buckets, rows_dev = count // copies, width // (copies * n_exp)
         row = lax.broadcasted_iota(jnp.int32, (width, count), 0)
         bucket = lax.broadcasted_iota(jnp.int32, (width, count), 1)
         place = row // (n_exp * rows_dev) * buckets + row % rows_dev
         here = ((place == bucket) & (row % rows_dev < buckets)).astype(f32).astype(bf16)
-        table = jnp.sum(offsets_ref[...], axis=1, keepdims=True)
-        column = jnp.sum(mm(here, wide_thirds(table), NN), axis=1, keepdims=True)
         base = own // 128 * 128
         lane = lax.broadcasted_iota(jnp.int32, (width, 128), 1) + base
-        acc[:, base : base + 128] += jnp.where(lane == own, column, 0.0)
+        for h, offsets_ref in enumerate(offsets):
+            table = jnp.sum(offsets_ref[...], axis=1, keepdims=True)
+            column = jnp.sum(mm(here, wide_thirds(table), NN), axis=1, keepdims=True)
+            at = h * lanes + base
+            acc[:, at : at + 128] += jnp.where(lane == own, column, 0.0)
         per = shares[0].shape[0]
         for d, share in enumerate(shares):
             start = pl.multiple_of(jnp.bitwise_xor(dp_ref[0], d) * per, per)
             share[...] = acc[pl.ds(start, per), :].astype(bf16)
 
 
-def sequence_grad(dp, normed, out, offsets, n_dp, n_exp, copies, lanes):
-    groups, _, dim, tok = out.shape
+def sequence_grad(dp, normed, outs, offsets, n_dp, n_exp, copies, lanes):
+    groups, _, dim, tok = outs[0].shape
     width = normed.shape[1]
+    heads = len(outs)
+    columns = heads * lanes
     return pl.pallas_call(
-        functools.partial(sequence_grad_kernel, n_exp, copies),
+        functools.partial(sequence_grad_kernel, heads, n_exp, copies),
         grid_spec=pltpu.PrefetchScalarGridSpec(
             num_scalar_prefetch=1,
             grid=(groups,),
-            in_specs=[
-                pl.BlockSpec((1, 3, dim, tok), lambda g, d: (g, 0, 0, 0)),
-                pl.BlockSpec(offsets.shape, lambda g, d: (0, 0)),
-            ]
+            in_specs=[pl.BlockSpec((1, 3, dim, tok), lambda g, d: (g, 0, 0, 0)) for _ in outs]
+            + [pl.BlockSpec(o.shape, lambda g, d: (0, 0)) for o in offsets]
             + [
                 pl.BlockSpec((1, width // 4, tok), lambda g, d, i=i: (g, i, 0)) for i in range(4)
             ],
-            out_specs=[pl.BlockSpec((width // n_dp, lanes), lambda g, d: (0, 0))] * n_dp,
-            scratch_shapes=[pltpu.VMEM((width, lanes), f32)],
+            out_specs=[pl.BlockSpec((width // n_dp, columns), lambda g, d: (0, 0))] * n_dp,
+            scratch_shapes=[pltpu.VMEM((width, columns), f32)],
         ),
-        out_shape=[jax.ShapeDtypeStruct((width // n_dp, lanes), bf16)] * n_dp,
+        out_shape=[jax.ShapeDtypeStruct((width // n_dp, columns), bf16)] * n_dp,
         compiler_params=pltpu.CompilerParams(vmem_limit_bytes=60 << 20),
         cost_estimate=cost(
-            6 * dim * groups * tok * width, 2 * groups * tok * (width + 3 * dim)
+            6 * heads * dim * groups * tok * width, 2 * groups * tok * (width + 3 * heads * dim)
         ),
         name="sequence_grad",
-    )(dp, out, offsets, *[normed] * 4)
+    )(dp, *outs, *offsets, *[normed] * 4)
 
 
 def dot_f32(left, right, left_dim, right_dim):
@@ -1107,21 +1112,20 @@
         if h == 0:
             half_c = add_low((part_c[0], beside[0]))
             sum_c = sum_dp(half_c)
-            early_half = sum_dp(add_low(beside[1]))
+            early_half = sum_dp(after(add_low(beside[1]), half_c))
         backward.append(out)
         grads.append(swap_blocks(out[0], pair))
-    late = []
-    for out, offsets in reversed(backward):
-        shares = sequence_grad(
-            dp_arg, normed_seq, after(out, backward), offsets, n_dp, n_exp, copies, lanes
-        )
-        late.insert(0, exchange(shares, "dp"))
+    shares = sequence_grad(
+        dp_arg, normed_seq, [out[0] for out in backward], [out[1] for out in backward], n_dp,
+        n_exp, copies, lanes,
+    )
+    late = exchange(shares, "dp")
     in_sums = [sum_a, add_low((last_own, after(last_came, backward))), sum_c]
     input_grad = input_gradient(layer_input, attn_gain, middle_grad, qkv_weight, grads)
     late, input_grad = lax.optimization_barrier((late, input_grad))
-    late = jnp.concatenate([add_low(parts) for parts in late], axis=1)
+    late = add_low(late)
     rows_out = swap_blocks(in_swap_order(late.reshape(groups, rows_dev, -1)), pair)
-    early_half = early_half.reshape(n_ctx, rows_dev, width + 128)
+    early_half = after(early_half, backward).reshape(n_ctx, rows_dev, width + 128)
     early_own, early_other = [
         lax.dynamic_index_in_dim(early_half, at, 0, False) for at in (ctx_index, 1 - ctx_index)
     ]

time: 594 us -> 590 us (level)
  waiting for transfers between devices: 64 us -> 73.8 us
  starting transfers between devices: 77 us -> 70.9 us
  Pallas kernels: 368 us -> 362 us
    ppermute x33 -> x30, waiting for transfers between devices: 34.5 us -> 47.3 us  [exchange(): lax.ppermute(parts[d], axis, [(i, i ^ d) for i in range(n)])]
    reduce_scatter x7, waiting for transfers between devices: 6.95 us -> 0.03 us  [sum_dp(): return lax.psum_scatter(half, 'dp', scatter_dimension=0, tiled=True)]
    pallas_call x2 -> x1, Pallas kernels: 18 us -> 11.2 us  [sequence_grad(): pl.pallas_call(functools.partial(sequence_grad_kernel, heads, n_exp, copi...]
    ppermute x33 -> x30, starting transfers between devices: 28.1 us -> 22.9 us  [exchange(): lax.ppermute(parts[d], axis, [(i, i ^ d) for i in range(n)])]
    convert_element_type x9 -> x8, other arithmetic: 13.1 us -> 12 us  [add_low(): return sum((part.astype(f32) for part in parts)).astype(bf16)]
  transfers between devices with their start and end apart: 57 -> 54, of which waited for: 15 -> 15; matrix products, arithmetic and copies ran while one was open for 7% -> 8% of each run, Pallas kernels for 61% -> 61%
where the time goes in v4:
time: 590 us; the launch traced here: 578 us
  Pallas kernels  362 us (61%)
  waiting for transfers between devices  73.8 us (13%)
  starting transfers between devices  70.9 us (12%)
  other arithmetic  29.2 us (5%)
  local copies, waits for them, and re-layouts  19 us (3%)
  between operations  15.4 us (3%)
  matrix products  8.13 us (1%)
    pallas_call x2, Pallas kernels, attention_bwd(): pl.pallas_call(functools.partial(attention_bwd_kernel, bk, order), grid_s...  93.7 us
    pallas_call x2, Pallas kernels, attention_fwd(): pl.pallas_call(functools.partial(attention_fwd_kernel, bk, order), grid_s...  60.5 us
    pallas_call x2, Pallas kernels, expert_bwd(): pl.pallas_call(functools.partial(expert_bwd_kernel, steps, groups), grid=...  51.2 us
    ppermute x30, waiting for transfers between devices, exchange(): lax.ppermute(parts[d], axis, [(i, i ^ d) for i in range(n)])  47.3 us
    pallas_call x2, Pallas kernels, expert_fwd(): pl.pallas_call(functools.partial(expert_fwd_kernel, steps, groups), grid=...  43.2 us
    all_to_all x9, starting transfers between devices, swap_blocks(): return lax.all_to_all(blocks, axes, split_axis=0, concat_axis=0, tiled=True)  39.6 us
    pallas_call x4, Pallas kernels, in_grad(): pl.pallas_call(in_grad_kernel, grid=(count,), in_specs=[pl.BlockSpec((wid...  32.8 us
    ppermute x30, starting transfers between devices, exchange(): lax.ppermute(parts[d], axis, [(i, i ^ d) for i in range(n)])  22.9 us
  transfers between devices with their start and end apart: 54, of which 15 were waited for; matrix products, arithmetic and copies ran while one was open for 8% of the time, Pallas kernels for 61%

profile of v4, /device:TPU:9, one launch (start us, length us, event | category | flops | bytes accessed | tf_op | source)
XLA Modules:
  0.0 578.2 jit_solution(1961156927717558208)
XLA Ops:
  7.2 9.0 %project.1 = (bf16[1024,512]{1,0:T(8,128)(2,1)}, bf16[8,3,64,512]{3,2,1,0:T(8,128)(2,1)}, bf16[8,3,64,512]{3,2,1,0:T(8,128)(2,1)}) custom-call(bf16[512,1024]{1,0:T(8,128)(2,1)} %x_ref.5, f32[1,1024]{1,0:T(1,128)} %bitcast.58, bf16[1024,3072]{1,0:T(8,128)(2,1)} %refs_3_.3, bf16[1024,3072]{1,0:T(8,128)(2,1)} %refs_3_.3, bf16[1024,3072]{1,0:T(8,128)(2,1)} %refs_3_.3, ...), custom_call_target="tpu_custom_call" | custom-call | flops 3221225472 | bytes 11534336 | tf_op jit(solution)/shard_map/project/pallas_call | solution.py:537
  16.2 4.6 all-to-all-start
  42.1 5.0 all-to-all-start.1
  49.7 30.3 %attention_fwd.2 = (bf16[8,64,512]{2,1,0:T(8,128)(2,1)}, f32[8,1,512]{2,1,0:T(1,128)}) custom-call(s32[8]{0:T(128)} %and_select_fusion.nch_ref, f32[32]{0:T(128)} %get-tuple-element.495.tab_ref, s32[8,8192]{1,0:T(8,128)} %broadcast_in_dim.57.buck_ref, bf16[64,4096]{1,0:T(8,128)(2,1)} %maximum_maximum_fusion.kmask_ref, ...), custom_call_target="tpu_custom_call" | custom-call | flops 16777216000 | bytes 2097152 | tf_op jit(solution)/shard_map/attention_fwd/pallas_call | solution.py:96
  86.4 30.2 %attention_fwd.3 = (bf16[8,64,512]{2,1,0:T(8,128)(2,1)}, f32[8,1,512]{2,1,0:T(1,128)}) custom-call(s32[8]{0:T(128)} %and_select_fusion.nch_ref, f32[32]{0:T(128)} %get-tuple-element.494.tab_ref, s32[8,8192]{1,0:T(8,128)} %broadcast_in_dim.57.buck_ref, bf16[64,4096]{1,0:T(8,128)(2,1)} %maximum_maximum_fusion.kmask_ref, ...), custom_call_target="tpu_custom_call" | custom-call | flops 16777216000 | bytes 2097152 | tf_op jit(solution)/shard_map/attention_fwd/pallas_call | solution.py:96
  116.6 7.3 %collective-permute-done.2.refs_3_ = bf16[160,1024]{1,0:T(8,128)(2,1)S(1)} collective-permute-done((bf16[160,1024]{1,0:T(8,128)(2,1)S(1)}, bf16[160,1024]{1,0:T(8,128)(2,1)S(1)}, u32[]{:S(2)}, u32[]{:S(2)}) %collective-permute-start.2) | collective-permute-done | bytes 327712 | tf_op jit(solution)/shard_map/ppermute | solution.py:895
  129.3 6.3 %all-to-all-done.3 = bf16[8,64,512]{2,1,0:T(8,128)(2,1)S(1)} async-done(((bf16[8,64,512]{2,1,0:T(8,128)(2,1)}), bf16[8,64,512]{2,1,0:T(8,128)(2,1)S(1)}, u32[]{:S(2)}, u32[]{:S(2)}) %all-to-all-start.3) | async-done | bytes 524320 | tf_op jit(solution)/shard_map/all_to_all | solution.py:889
  136.4 7.9 %route.1 = (f32[512,1024]{1,0:T(8,128)}, bf16[512,1024]{1,0:T(8,128)(2,1)}, f32[512,4]{1,0:T(8,128)}, bf16[160,1152]{1,0:T(8,128)(2,1)}, bf16[160,1152]{1,0:T(8,...) custom-call(bf16[512,1024]{1,0:T(8,128)(2,1)} %x_ref.5, ...), custom_call_target="tpu_custom_call" | custom-call | flops 2415919104 | bytes 8388608 | tf_op jit(solution)/shard_map/route/pallas_call | solution.py:804
  149.0 6.5 %collective-permute-done.4.refs_2_.refs_10_.refs_6_ = bf16[160,1152]{1,0:T(8,128)(2,1)S(1)} collective-permute-done((bf16[160,1152]{1,0:T(8,128)(2,1)}, bf16[160,1152]{1,0:T(8,128)(2,1)S(1)}, u32[]{:S(2)}, u32[]{:S(2)}) %collective-permute-start.4) | collective-permute-done | bytes 368672 | tf_op jit(solution)/shard_map/ppermute | solution.py:895
  155.5 8.5 %collective-permute-done.5.refs_3_.refs_11_.refs_7_ = bf16[160,1152]{1,0:T(8,128)(2,1)S(1)} collective-permute-done((bf16[160,1152]{1,0:T(8,128)(2,1)}, bf16[160,1152]{1,0:T(8,128)(2,1)S(1)}, u32[]{:S(2)}, u32[]{:S(2)}) %collective-permute-start.5) | collective-permute-done | bytes 368672 | tf_op jit(solution)/shard_map/ppermute | solution.py:895
  165.9 21.5 %expert_fwd.2 = (bf16[2816,640]{1,0:T(8,128)(2,1)}, bf16[640,2816]{1,0:T(8,128)(2,1)}, bf16[640,2816]{1,0:T(8,128)(2,1)}, bf16[160,1024]{1,0:T(8,128)(2,1)}, bf1...) custom-call(bf16[1,1024,5632]{2,1,0:T(8,128)(2,1)} %wu_ref.7, ...), custom_call_target="tpu_custom_call" | custom-call | flops 18454937600 | bytes 30736384 | tf_op jit(solution)/shard_map/expert_fwd/pallas_call | solution.py:318
  187.5 6.0 %collective-permute-done.11.refs_7_.refs_3_ = bf16[160,1024]{1,0:T(8,128)(2,1)} collective-permute-done((bf16[160,1024]{1,0:T(8,128)(2,1)S(1)}, bf16[160,1024]{1,0:T(8,128)(2,1)}, u32[]{:S(2)}, u32[]{:S(2)}) %collective-permute-start.11) | collective-permute-done | bytes 327712 | tf_op jit(solution)/shard_map/ppermute | solution.py:895
  195.6 21.7 %expert_fwd.3 = (bf16[2816,640]{1,0:T(8,128)(2,1)}, bf16[640,2816]{1,0:T(8,128)(2,1)}, bf16[640,2816]{1,0:T(8,128)(2,1)}, bf16[160,1024]{1,0:T(8,128)(2,1)}, bf1...) custom-call(bf16[1,1024,5632]{2,1,0:T(8,128)(2,1)} %wu_ref.7, ...), custom_call_target="tpu_custom_call" | custom-call | flops 18454937600 | bytes 30736384 | tf_op jit(solution)/shard_map/expert_fwd/pallas_call | solution.py:318
  219.6 9.6 %down_grad.2 = (bf16[4,1536,128]{2,1,0:T(8,128)(2,1)}, bf16[4,1536,128]{2,1,0:T(8,128)(2,1)}) custom-call(s32[1]{0:T(128)} %bitcast.14.ctx_ref, bf16[160,1024]{1,0:T(8,128)(2,1)} %convolution_convert_fusion.7.refs_0_, bf16[160,1024]{1,0:T(8,128)(2,1)} %copy-done.50, bf16[160,1024]{1,0:T(8,128)(2,1)} %copy-done.51, bf16[160,1024]{1,0:T(8,128)(2,1)} %copy-done.52, ...), custom_call_target="tpu_custom_call" | custom-call | flops 8053063680 | bytes 9699328 | tf_op jit(solution)/shard_map/down_grad/pallas_call | solution.py:496
  230.0 8.6 %down_grad.3 = (bf16[4,1280,128]{2,1,0:T(8,128)(2,1)}, bf16[4,1280,128]{2,1,0:T(8,128)(2,1)}) custom-call(s32[1]{0:T(128)} %bitcast.14.ctx_ref, bf16[160,1024]{1,0:T(8,128)(2,1)} %convolution_convert_fusion.7.refs_0_, bf16[160,1024]{1,0:T(8,128)(2,1)} %copy-done.50, bf16[160,1024]{1,0:T(8,128)(2,1)} %copy-done.51, bf16[160,1024]{1,0:T(8,128)(2,1)} %copy-done.52, ...), custom_call_target="tpu_custom_call" | custom-call | flops 6710886400 | bytes 8519680 | tf_op jit(solution)/shard_map/down_grad/pallas_call | solution.py:496
  238.7 25.5 %expert_bwd.2 = (bf16[2,640,2816]{2,1,0:T(8,128)(2,1)}, bf16[160,1024]{1,0:T(8,128)(2,1)}, bf16[160,1024]{1,0:T(8,128)(2,1)}, bf16[160,1024]{1,0:T(8,128)(2,1)}, bf16[160,1024]{1,0:T(8,128)(2,1)}) custom-call(bf16[640,2816]{1,0:T(8,128)(2,1)} %get-tuple-element.292.act_ref, bf16[640,2816]{1,0:T(8,128)(2,1)} %get-tuple-element.293.slope_ref, ...), custom_call_target="tpu_custom_call" | custom-call | flops 18454937600 | bytes 34340864 | tf_op jit(solution)/shard_map/expert_bwd/pallas_call | solution.py:373
  270.5 25.8 %expert_bwd.3 = (bf16[2,640,2816]{2,1,0:T(8,128)(2,1)}, bf16[160,1024]{1,0:T(8,128)(2,1)}, bf16[160,1024]{1,0:T(8,128)(2,1)}, bf16[160,1024]{1,0:T(8,128)(2,1)}, bf16[160,1024]{1,0:T(8,128)(2,1)}) custom-call(bf16[640,2816]{1,0:T(8,128)(2,1)} %get-tuple-element.312.act_ref, bf16[640,2816]{1,0:T(8,128)(2,1)} %get-tuple-element.313.slope_ref, ...), custom_call_target="tpu_custom_call" | custom-call | flops 18454937600 | bytes 34340864 | tf_op jit(solution)/shard_map/expert_bwd/pallas_call | solution.py:373
  301.8 5.3 turn.1.refs_0_.refs_1_.refs_2_.refs_3_
  309.7 5.8 %in_grad.4 = (bf16[512,768]{1,0:T(8,128)(2,1)}, bf16[512,768]{1,0:T(8,128)(2,1)}) custom-call(bf16[1024,1280]{1,0:T(8,128)(2,1)} %turn.1.refs_0_.refs_1_.refs_2_.refs_3_, bf16[1024,1280]{1,0:T(8,128)(2,1)} %turn.1.refs_0_.refs_1_.refs_2_.refs_3_, bf16[1024,1280]{1,0:T(8,128)(2,1)} %turn.1.refs_0_.refs_1_.refs_2_.refs_3_, ...), custom_call_target="tpu_custom_call" | custom-call | flops 4026531840 | bytes 6160384 | tf_op jit(solution)/shard_map/in_grad/pallas_call | solution.py:450
  316.3 5.6 in_grad.5
  321.8 10.7 %in_grad.6 = (bf16[512,2048]{1,0:T(8,128)(2,1)}, bf16[512,2048]{1,0:T(8,128)(2,1)}) custom-call(bf16[1024,1280]{1,0:T(8,128)(2,1)} %turn.1.refs_0_.refs_1_.refs_2_.refs_3_, bf16[1024,1280]{1,0:T(8,128)(2,1)} %turn.1.refs_0_.refs_1_.refs_2_.refs_3_, bf16[1024,1280]{1,0:T(8,128)(2,1)} %turn.1.refs_0_.refs_1_.refs_2_.refs_3_, ...), custom_call_target="tpu_custom_call" | custom-call | flops 10737418240 | bytes 12058624 | tf_op jit(solution)/shard_map/in_grad/pallas_call | solution.py:450
  337.0 15.5 %combine.1 = (bf16[512,1024]{1,0:T(8,128)(2,1)}, f32[512,1024]{1,0:T(8,128)}, bf16[8,64,512]{2,1,0:T(8,128)(2,1)}, bf16[8,64,512]{2,1,0:T(8,128)(2,1)}, bf16[256...) custom-call(s32[1]{0:T(128)} %bitcast.exp_ref, ...), custom_call_target="tpu_custom_call" | custom-call | flops 6174015488 | bytes 18874368 | tf_op jit(solution)/shard_map/combine/pallas_call | solution.py:705
  354.4 5.2 all-to-all-start.4
  359.6 10.7 %in_grad.7 = (bf16[512,2048]{1,0:T(8,128)(2,1)}, bf16[512,2048]{1,0:T(8,128)(2,1)}) custom-call(bf16[1024,1280]{1,0:T(8,128)(2,1)} %turn.1.refs_0_.refs_1_.refs_2_.refs_3_, bf16[1024,1280]{1,0:T(8,128)(2,1)} %turn.1.refs_0_.refs_1_.refs_2_.refs_3_, bf16[1024,1280]{1,0:T(8,128)(2,1)} %turn.1.refs_0_.refs_1_.refs_2_.refs_3_, ...), custom_call_target="tpu_custom_call" | custom-call | flops 10737418240 | bytes 12058624 | tf_op jit(solution)/shard_map/in_grad/pallas_call | solution.py:450
  371.8 4.3 all-to-all-start.5
  379.9 46.9 %attention_bwd.2 = (bf16[8,3,64,512]{3,2,1,0:T(8,128)(2,1)}, f32[32,128]{1,0:T(8,128)}) custom-call(s32[8]{0:T(128)} %and_select_fusion.nch_ref, f32[32]{0:T(128)} %get-tuple-element.495.tab_ref, s32[8,8192]{1,0:T(8,128)} %broadcast_in_dim.58.buck_ref, bf16[64,4096]{1,0:T(8,128)(2,1)} %maximum_maximum_fusion.kmask_ref, ...), custom_call_target="tpu_custom_call" | custom-call | flops 41943040000 | bytes 4194304 | tf_op jit(solution)/shard_map/attention_bwd/pallas_call | solution.py:220
  436.0 4.4 all-to-all-start.6
  442.1 46.8 %attention_bwd.3 = (bf16[8,3,64,512]{3,2,1,0:T(8,128)(2,1)}, f32[32,128]{1,0:T(8,128)}) custom-call(s32[8]{0:T(128)} %and_select_fusion.nch_ref, f32[32]{0:T(128)} %get-tuple-element.494.tab_ref, s32[8,8192]{1,0:T(8,128)} %broadcast_in_dim.58.buck_ref, bf16[64,4096]{1,0:T(8,128)(2,1)} %maximum_maximum_fusion.kmask_ref, ...), custom_call_target="tpu_custom_call" | custom-call | flops 41943040000 | bytes 4194304 | tf_op jit(solution)/shard_map/attention_bwd/pallas_call | solution.py:220
  497.7 11.2 %sequence_grad.1 = (bf16[256,512]{1,0:T(8,128)(2,1)}, bf16[256,512]{1,0:T(8,128)(2,1)}, bf16[256,512]{1,0:T(8,128)(2,1)}, bf16[256,512]{1,0:T(8,128)(2,1)}) custom-call(s32[1]{0:T(128)} %bitcast.15.dp_ref, bf16[8,3,64,512]{3,2,1,0:T(8,128)(2,1)} %get-tuple-element.420.refs_0_, bf16[8,3,64,512]{3,2,1,0:T(8,128)(2,1)} %get-tuple-element.428.refs_1_, ...), custom_call_target="tpu_custom_call" | custom-call | flops 3221225472 | bytes 11534336 | tf_op jit(solution)/shard_map/sequence_grad/pallas_call | solution.py:862
  521.7 11.2 %input_grad.1 = f32[512,1024]{1,0:T(8,128)} custom-call(bf16[512,1024]{1,0:T(8,128)(2,1)} %x_ref.5, f32[1,1024]{1,0:T(1,128)} %bitcast.59, f32[512,1024]{1,0:T(8,128)} %get-tuple-element.434.mid_ref, bf16[1024,3072]{1,0:T(8,128)(2,1)} %refs_3_.3, bf16[1024,3072]{1,0:T(8,128)(2,1)} %refs_3_.3, bf16[1024,3072]{1,0:T(8,128)(2,1)} %refs_3_.3, ...), custom_call_target="tpu_custom_call" | custom-call | flops 3221225472 | bytes 14680064 | tf_op jit(solution)/shard_map/input_grad/pallas_call | solution.py:586
  535.4 16.5 %collective-permute-done.35 = bf16[256,512]{1,0:T(8,128)(2,1)} collective-permute-done((bf16[256,512]{1,0:T(8,128)(2,1)}, bf16[256,512]{1,0:T(8,128)(2,1)}, u32[]{:S(2)}, u32[]{:S(2)}) %collective-permute-start.35) | collective-permute-done | bytes 262176 | tf_op jit(solution)/shard_map/ppermute | solution.py:895
  553.8 4.5 all-to-all-start.8
  (303 shorter events, 124.2 us)
Async XLA Ops:
  20.8 196.6 %all-gather.3.cloned.1.call-start = ((), (), s32[]{:S(2)}) async-start(), calls=%async_computation.23 | async-start | bytes 9437184 | tf_op jit(solution)/shard_map/all_gather | solution.py:1012
  42.1 38.0 %all-to-all-start.1 = ((bf16[8,3,64,512]{3,2,1,0:T(8,128)(2,1)}), bf16[8,3,64,512]{3,2,1,0:T(8,128)(2,1)}, u32[]{:S(2)}, u32[]{:S(2)}) async-start(bf16[8,3,64,512]{3,2,1,0:T(8,128)(2,1)} %get-tuple-element.243), calls=%async_computation.1 | async-start | bytes 3145728 | tf_op jit(solution)/shard_map/all_to_all | solution.py:889
  80.1 43.8 %all-to-all-start.2 = ((bf16[8,64,512]{2,1,0:T(8,128)(2,1)}), bf16[8,64,512]{2,1,0:T(8,128)(2,1)S(1)}, u32[]{:S(2)}, u32[]{:S(2)}) async-start(bf16[8,64,512]{2,1,0:T(8,128)(2,1)} %get-tuple-element.244.o_ref), calls=%async_computation.2 | async-start | bytes 1048576 | tf_op jit(solution)/shard_map/all_to_all | solution.py:889
  84.3 32.3 %collective-permute-start = (bf16[160,1024]{1,0:T(8,128)(2,1)S(1)}, bf16[160,1024]{1,0:T(8,128)(2,1)S(1)}, u32[]{:S(2)}, u32[]{:S(2)}) collective-permute-start(bf16[160,1024]{1,0:T(8,128)(2,1)S(1)} %copy-done.33), channel_id=1, source_target_pairs={{0,1},{1,0},{2,3},{3,2},{4,5},{5,4},{6,7},{7,6},{8,9},{9,8},{10,11... | collective-permute-start | bytes 983048 | tf_op jit(solution)/shard_map/ppermute | solution.py:895
  84.3 32.2 %collective-permute-start.1 = (bf16[160,1024]{1,0:T(8,128)(2,1)S(1)}, bf16[160,1024]{1,0:T(8,128)(2,1)S(1)}, u32[]{:S(2)}, u32[]{:S(2)}) collective-permute-start(bf16[160,1024]{1,0:T(8,128)(2,1)S(1)} %copy-done.32), channel_id=1, source_target_pairs={{0,2},{1,3},{2,0},{3,1},{4,6},{5,7},{6,4},{7,5},{8,10},{9,11},{10,... | collective-permute-start | bytes 983048 | tf_op jit(solution)/shard_map/ppermute | solution.py:895
  86.0 37.9 %collective-permute-start.2 = (bf16[160,1024]{1,0:T(8,128)(2,1)S(1)}, bf16[160,1024]{1,0:T(8,128)(2,1)S(1)}, u32[]{:S(2)}, u32[]{:S(2)}) collective-permute-start(bf16[160,1024]{1,0:T(8,128)(2,1)S(1)} %convolution_convert_fusion.4), channel_id=1, source_target_pairs={{0,3},{1,2},{2,1},{3,0},{4,7},{5,6},{6,5},{7,4},{8,11},{9,10},{10,... | collective-permute-start | bytes 983048 | tf_op jit(solution)/shard_map/ppermute | solution.py:895
  127.4 227.0 %reduce-scatter.8.cloned.1.call-start = ((), (), s32[]{:S(2)}) async-start(), calls=%async_computation.16 | async-start | bytes 1966080 | tf_op jit(solution)/shard_map/reduce_scatter | solution.py:1042
  147.0 40.5 %collective-permute-start.7 = (bf16[160,1152]{1,0:T(8,128)(2,1)}, bf16[160,1152]{1,0:T(8,128)(2,1)S(1)}, u32[]{:S(2)}, u32[]{:S(2)}) collective-permute-start(bf16[160,1152]{1,0:T(8,128)(2,1)} %get-tuple-element.277), channel_id=1, source_target_pairs={{0,2},{1,3},{2,0},{3,1},{4,6},{5,7},{6,4},{7,5},{8,10},{9,11},{10,... | collective-permute-start | bytes 1105928 | tf_op jit(solution)/shard_map/ppermute | solution.py:895
  147.5 40.0 %collective-permute-start.8 = (bf16[160,1152]{1,0:T(8,128)(2,1)}, bf16[160,1152]{1,0:T(8,128)(2,1)S(1)}, u32[]{:S(2)}, u32[]{:S(2)}) collective-permute-start(bf16[160,1152]{1,0:T(8,128)(2,1)} %get-tuple-element.278), channel_id=1, source_target_pairs={{0,3},{1,2},{2,1},{3,0},{4,7},{5,6},{6,5},{7,4},{8,11},{9,10},{10,... | collective-permute-start | bytes 1105928 | tf_op jit(solution)/shard_map/ppermute | solution.py:895
  164.7 28.8 %collective-permute-start.11 = (bf16[160,1024]{1,0:T(8,128)(2,1)S(1)}, bf16[160,1024]{1,0:T(8,128)(2,1)}, u32[]{:S(2)}, u32[]{:S(2)}) collective-permute-start(bf16[160,1024]{1,0:T(8,128)(2,1)S(1)} %copy-done.29), channel_id=1, source_target_pairs={{0,3},{1,2},{2,1},{3,0},{4,7},{5,6},{6,5},{7,4},{8,11},{9,10},{10,... | collective-permute-start | bytes 983048 | tf_op jit(solution)/shard_map/ppermute | solution.py:895
  217.4 46.8 %collective-permute-start.15 = (bf16[160,1024]{1,0:T(8,128)(2,1)}, bf16[160,1024]{1,0:T(8,128)(2,1)S(1)}, u32[]{:S(2)}, u32[]{:S(2)}) collective-permute-start(bf16[160,1024]{1,0:T(8,128)(2,1)} %get-tuple-element.308), channel_id=1, source_target_pairs={{0,1},{1,0},{2,3},{3,2},{4,5},{5,4},{6,7},{7,6},{8,9},{9,8},{10,11... | collective-permute-start | bytes 983048 | tf_op jit(solution)/shard_map/ppermute | solution.py:895
  217.5 46.7 %collective-permute-start.16 = (bf16[160,1024]{1,0:T(8,128)(2,1)}, bf16[160,1024]{1,0:T(8,128)(2,1)S(1)}, u32[]{:S(2)}, u32[]{:S(2)}) collective-permute-start(bf16[160,1024]{1,0:T(8,128)(2,1)} %get-tuple-element.309), channel_id=1, source_target_pairs={{0,2},{1,3},{2,0},{3,1},{4,6},{5,7},{6,4},{7,5},{8,10},{9,11},{10,... | collective-permute-start | bytes 983048 | tf_op jit(solution)/shard_map/ppermute | solution.py:895
  218.1 46.1 %collective-permute-start.17 = (bf16[160,1024]{1,0:T(8,128)(2,1)}, bf16[160,1024]{1,0:T(8,128)(2,1)}, u32[]{:S(2)}, u32[]{:S(2)}) collective-permute-start(bf16[160,1024]{1,0:T(8,128)(2,1)} %get-tuple-element.310), channel_id=1, source_target_pairs={{0,3},{1,2},{2,1},{3,0},{4,7},{5,6},{6,5},{7,4},{8,11},{9,10},{10,... | collective-permute-start | bytes 983048 | tf_op jit(solution)/shard_map/ppermute | solution.py:895
  229.2 36.4 %collective-permute-start.18 = (bf16[4,1536,128]{2,1,0:T(8,128)(2,1)}, bf16[4,1536,128]{2,1,0:T(8,128)(2,1)S(1)}, u32[]{:S(2)}, u32[]{:S(2)}) collective-permute-start(bf16[4,1536,128]{2,1,0:T(8,128)(2,1)} %get-tuple-element.323), channel_id=1, source_target_pairs={{0,4},{4,0},{1,5},{5,1},{2,6},{6,2},{3,7},{7,3},{8,12},{12,8},{9,1... | collective-permute-start | bytes 4718600 | tf_op jit(solution)/shard_map/ppermute | solution.py:1045
  267.3 159.5 %reduce-scatter.14.cloned.1.call-start = ((), (), s32[]{:S(2)}) async-start(), calls=%async_computation.19 | async-start | bytes 1638400 | tf_op jit(solution)/shard_map/reduce_scatter | solution.py:1042
  267.3 29.0 %collective-permute-start.19 = (bf16[160,1024]{1,0:T(8,128)(2,1)}, bf16[160,1024]{1,0:T(8,128)(2,1)S(1)}, u32[]{:S(2)}, u32[]{:S(2)}) collective-permute-start(bf16[160,1024]{1,0:T(8,128)(2,1)} %get-tuple-element.349), channel_id=1, source_target_pairs={{0,1},{1,0},{2,3},{3,2},{4,5},{5,4},{6,7},{7,6},{8,9},{9,8},{10,11... | collective-permute-start | bytes 983048 | tf_op jit(solution)/shard_map/ppermute | solution.py:895
  268.0 28.3 %collective-permute-start.20 = (bf16[160,1024]{1,0:T(8,128)(2,1)}, bf16[160,1024]{1,0:T(8,128)(2,1)S(1)}, u32[]{:S(2)}, u32[]{:S(2)}) collective-permute-start(bf16[160,1024]{1,0:T(8,128)(2,1)} %get-tuple-element.350), channel_id=1, source_target_pairs={{0,2},{1,3},{2,0},{3,1},{4,6},{5,7},{6,4},{7,5},{8,10},{9,11},{10,... | collective-permute-start | bytes 983048 | tf_op jit(solution)/shard_map/ppermute | solution.py:895
  269.8 30.5 %collective-permute-start.22 = (bf16[4,1280,128]{2,1,0:T(8,128)(2,1)}, bf16[4,1280,128]{2,1,0:T(8,128)(2,1)S(1)}, u32[]{:S(2)}, u32[]{:S(2)}) collective-permute-start(bf16[4,1280,128]{2,1,0:T(8,128)(2,1)} %get-tuple-element.367), channel_id=1, source_target_pairs={{0,4},{4,0},{1,5},{5,1},{2,6},{6,2},{3,7},{7,3},{8,12},{12,8},{9,1... | collective-permute-start | bytes 3932168 | tf_op jit(solution)/shard_map/ppermute | solution.py:1045
  301.8 127.3 %reduce-scatter.10.cloned.1.call-start = ((), (), s32[]{:S(2)}) async-start(), calls=%async_computation.17 | async-start | bytes 2621440 | tf_op jit(solution)/shard_map/reduce_scatter | solution.py:1042
  334.8 94.3 %reduce-scatter.12.cloned.1.call-start = ((), (), s32[]{:S(2)}) async-start(), calls=%async_computation.18 | async-start | bytes 2621440 | tf_op jit(solution)/shard_map/reduce_scatter | solution.py:1042
  359.6 129.3 %reduce-scatter.16.cloned.1.call-start = ((), (), s32[]{:S(2)}) async-start(), calls=%async_computation.20 | async-start | bytes 1966080 | tf_op jit(solution)/shard_map/reduce_scatter | solution.py:1042
  371.8 55.0 %all-to-all-start.5 = ((bf16[8,64,512]{2,1,0:T(8,128)(2,1)}), bf16[8,64,512]{2,1,0:T(8,128)(2,1)}, u32[]{:S(2)}, u32[]{:S(2)}) async-start(bf16[8,64,512]{2,1,0:T(8,128)(2,1)} %get-tuple-element.401), calls=%async_computation.9 | async-start | bytes 1048576 | tf_op jit(solution)/shard_map/all_to_all | solution.py:889
  376.1 117.7 %reduce-scatter.20.cloned.1.call-start = ((), (), s32[]{:S(2)}) async-start(), calls=%async_computation.22 | async-start | bytes 737280 | tf_op jit(solution)/shard_map/reduce_scatter | solution.py:1042
  376.3 50.5 %collective-permute-start.29 = (bf16[256,1152]{1,0:T(8,128)(2,1)}, bf16[256,1152]{1,0:T(8,128)(2,1)S(1)}, u32[]{:S(2)}, u32[]{:S(2)}) collective-permute-start(bf16[256,1152]{1,0:T(8,128)(2,1)} %get-tuple-element.415), channel_id=1, source_target_pairs={{0,1},{1,0},{2,3},{3,2},{4,5},{5,4},{6,7},{7,6},{8,9},{9,8},{10,11... | collective-permute-start | bytes 1769480 | tf_op jit(solution)/shard_map/ppermute | solution.py:895
  376.6 50.3 %collective-permute-start.30 = (bf16[256,1152]{1,0:T(8,128)(2,1)}, bf16[256,1152]{1,0:T(8,128)(2,1)}, u32[]{:S(2)}, u32[]{:S(2)}) collective-permute-start(bf16[256,1152]{1,0:T(8,128)(2,1)} %get-tuple-element.416), channel_id=1, source_target_pairs={{0,2},{1,3},{2,0},{3,1},{4,6},{5,7},{6,4},{7,5},{8,10},{9,11},{10,... | collective-permute-start | bytes 1769480 | tf_op jit(solution)/shard_map/ppermute | solution.py:895
  378.1 48.7 %collective-permute-start.31 = (bf16[256,1152]{1,0:T(8,128)(2,1)}, bf16[256,1152]{1,0:T(8,128)(2,1)}, u32[]{:S(2)}, u32[]{:S(2)}) collective-permute-start(bf16[256,1152]{1,0:T(8,128)(2,1)} %get-tuple-element.417), channel_id=1, source_target_pairs={{0,3},{1,2},{2,1},{3,0},{4,7},{5,6},{6,5},{7,4},{8,11},{9,10},{10,... | collective-permute-start | bytes 1769480 | tf_op jit(solution)/shard_map/ppermute | solution.py:895
  378.5 50.6 %collective-permute-start.28 = (bf16[512,2048]{1,0:T(8,128)(2,1)}, bf16[512,2048]{1,0:T(8,128)(2,1)}, u32[]{:S(2)}, u32[]{:S(2)}) collective-permute-start(bf16[512,2048]{1,0:T(8,128)(2,1)} %get-tuple-element.413), channel_id=1, source_target_pairs={{0,4},{4,0},{1,5},{5,1},{2,6},{6,2},{3,7},{7,3},{8,12},{12,8},{9,1... | collective-permute-start | bytes 6291464 | tf_op jit(solution)/shard_map/ppermute | solution.py:1045
  436.0 52.9 %all-to-all-start.6 = ((bf16[8,3,64,512]{3,2,1,0:T(8,128)(2,1)}), bf16[8,3,64,512]{3,2,1,0:T(8,128)(2,1)S(1)}, u32[]{:S(2)}, u32[]{:S(2)}) async-start(bf16[8,3,64,512]{3,2,1,0:T(8,128)(2,1)} %get-tuple-element.420.refs_0_), calls=%async_computation.10 | async-start | bytes 3145728 | tf_op jit(solution)/shard_map/all_to_all | solution.py:889
  440.3 118.0 %reduce-scatter.18.cloned.1.call-start = ((), (), s32[]{:S(2)}) async-start(), calls=%async_computation.21 | async-start | bytes 2621440 | tf_op jit(solution)/shard_map/reduce_scatter | solution.py:1042
  440.6 48.3 %collective-permute-start.32 = (bf16[128,2048]{1,0:T(8,128)(2,1)S(1)}, bf16[128,2048]{1,0:T(8,128)(2,1)S(1)}, u32[]{:S(2)}, u32[]{:S(2)}) collective-permute-start(bf16[128,2048]{1,0:T(8,128)(2,1)S(1)} %copy-done.47), channel_id=1, source_target_pairs={{0,4},{4,0},{1,5},{5,1},{2,6},{6,2},{3,7},{7,3},{8,12},{12,8},{9,1... | collective-permute-start | bytes 1572872 | tf_op jit(solution)/shard_map/ppermute | solution.py:1045
  489.7 30.9 %all-to-all-start.7 = ((bf16[8,3,64,512]{3,2,1,0:T(8,128)(2,1)}), bf16[8,3,64,512]{3,2,1,0:T(8,128)(2,1)S(1)}, u32[]{:S(2)}, u32[]{:S(2)}) async-start(bf16[8,3,64,512]{3,2,1,0:T(8,128)(2,1)} %get-tuple-element.428.refs_1_), calls=%async_computation.12 | async-start | bytes 3145728 | tf_op jit(solution)/shard_map/all_to_all | solution.py:889
  511.5 40.3 %collective-permute-start.35 = (bf16[256,512]{1,0:T(8,128)(2,1)}, bf16[256,512]{1,0:T(8,128)(2,1)}, u32[]{:S(2)}, u32[]{:S(2)}) collective-permute-start(bf16[256,512]{1,0:T(8,128)(2,1)} %get-tuple-element.433), channel_id=1, source_target_pairs={{0,24},{8,16},{16,8},{24,0},{1,25},{9,17},{17,9},{25,1},{2,26},{10... | collective-permute-start | bytes 786440 | tf_op jit(solution)/shard_map/ppermute | solution.py:895
  (85 other events, 1348.0 us)
Sparse Core Ops, SparseCore 0:
  42.2 87.8 all-gather.2
  267.4 33.0 reduce-scatter.7
  303.4 30.0 reduce-scatter.13
  335.7 42.2 reduce-scatter.9
  380.2 43.1 reduce-scatter.11
  425.6 35.0 reduce-scatter.15
  463.6 19.2 reduce-scatter.19
  485.7 63.3 reduce-scatter.17

commit v5 on v4

--- a/solution.py
+++ b/solution.py
@@ -896,6 +896,19 @@
     ]
 
 
+def scatter_dp(rows):
+    n = lax.axis_size("dp")
+    shares = rows.reshape((n, rows.shape[0] // n) + rows.shape[1:])
+    mine = lax.axis_index("dp")
+    return exchange(
+        [
+            lax.dynamic_index_in_dim(shares, jnp.bitwise_xor(mine, d), 0, False)
+            for d in range(n)
+        ],
+        "dp",
+    )
+
+
 def add_low(parts):
     return sum(part.astype(f32) for part in parts).astype(bf16)
 
@@ -1103,7 +1116,7 @@
             arg = after(arg, half_c)
         if h == heads - 1:
             last_came = to_ctx(after(last_other, arg))
-            beside += [last_came, sum_a]
+            beside += [last_came, sum_a] + ([early_sums] if h else [])
         out = attention_bwd(
             order, chunks, table_dev[:, h], buck, kmask, hide, qkv[h], forward[h][0],
             arg, forward[h][1], step_k,
@@ -1112,7 +1125,9 @@
         if h == 0:
             half_c = add_low((part_c[0], beside[0]))
             sum_c = sum_dp(half_c)
-            early_half = sum_dp(after(add_low(beside[1]), half_c))
+            early_sums = scatter_dp(add_low(beside[1]))
+        elif h == heads - 1:
+            early_sums = beside[-1]
         backward.append(out)
         grads.append(swap_blocks(out[0], pair))
     shares = sequence_grad(
@@ -1125,7 +1140,7 @@
     late, input_grad = lax.optimization_barrier((late, input_grad))
     late = add_low(late)
     rows_out = swap_blocks(in_swap_order(late.reshape(groups, rows_dev, -1)), pair)
-    early_half = after(early_half, backward).reshape(n_ctx, rows_dev, width + 128)
+    early_half = add_low(after(early_sums, backward)).reshape(n_ctx, rows_dev, width + 128)
     early_own, early_other = [
         lax.dynamic_index_in_dim(early_half, at, 0, False) for at in (ctx_index, 1 - ctx_index)
     ]

time: 590 us -> 578 us (0.980)
  waiting for transfers between devices: 73.8 us -> 58.8 us
    ppermute x30 -> x33, waiting for transfers between devices: 47.3 us -> 35.5 us  [exchange(): lax.ppermute(parts[d], axis, [(i, i ^ d) for i in range(n)])]
    ppermute x30 -> x33, starting transfers between devices: 22.9 us -> 26.5 us  [exchange(): lax.ppermute(parts[d], axis, [(i, i ^ d) for i in range(n)])]
    convert_element_type x8 -> x9, other arithmetic: 12 us -> 13.9 us  [add_low(): return sum((part.astype(f32) for part in parts)).astype(bf16)]
  transfers between devices with their start and end apart: 54 -> 56, of which waited for: 15 -> 14; matrix products, arithmetic and copies ran while one was open for 8% -> 8% of each run, Pallas kernels for 61% -> 62%
where the time goes in v5:
time: 578 us; the launch traced here: 567 us
  Pallas kernels  362 us (63%)
  starting transfers between devices  75.3 us (13%)
  waiting for transfers between devices  58.8 us (10%)
  other arithmetic  28.7 us (5%)
  local copies, waits for them, and re-layouts  17.9 us (3%)
  between operations  15.5 us (3%)
  matrix products  8.86 us (2%)
    pallas_call x2, Pallas kernels, attention_bwd(): pl.pallas_call(functools.partial(attention_bwd_kernel, bk, order), grid_s...  93.6 us
    pallas_call x2, Pallas kernels, attention_fwd(): pl.pallas_call(functools.partial(attention_fwd_kernel, bk, order), grid_s...  60.5 us
    pallas_call x2, Pallas kernels, expert_bwd(): pl.pallas_call(functools.partial(expert_bwd_kernel, steps, groups), grid=...  51.3 us
    pallas_call x2, Pallas kernels, expert_fwd(): pl.pallas_call(functools.partial(expert_fwd_kernel, steps, groups), grid=...  43.1 us
    all_to_all x9, starting transfers between devices, swap_blocks(): return lax.all_to_all(blocks, axes, split_axis=0, concat_axis=0, tiled=True)  40.6 us
    ppermute x33, waiting for transfers between devices, exchange(): lax.ppermute(parts[d], axis, [(i, i ^ d) for i in range(n)])  35.5 us
    pallas_call x4, Pallas kernels, in_grad(): pl.pallas_call(in_grad_kernel, grid=(count,), in_specs=[pl.BlockSpec((wid...  32.8 us
    ppermute x33, starting transfers between devices, exchange(): lax.ppermute(parts[d], axis, [(i, i ^ d) for i in range(n)])  26.5 us
  transfers between devices with their start and end apart: 56, of which 14 were waited for; matrix products, arithmetic and copies ran while one was open for 8% of the time, Pallas kernels for 62%

profile of v5, /device:TPU:9, one launch (start us, length us, event | category | flops | bytes accessed | tf_op | source)
XLA Modules:
  0.0 566.7 jit_solution(3108853527847011411)
XLA Ops:
  7.2 9.0 %project.1 = (bf16[1024,512]{1,0:T(8,128)(2,1)}, bf16[8,3,64,512]{3,2,1,0:T(8,128)(2,1)}, bf16[8,3,64,512]{3,2,1,0:T(8,128)(2,1)}) custom-call(bf16[512,1024]{1,0:T(8,128)(2,1)} %x_ref.5, f32[1,1024]{1,0:T(1,128)} %bitcast.68, bf16[1024,3072]{1,0:T(8,128)(2,1)} %refs_3_.3, bf16[1024,3072]{1,0:T(8,128)(2,1)} %refs_3_.3, bf16[1024,3072]{1,0:T(8,128)(2,1)} %refs_3_.3, ...), custom_call_target="tpu_custom_call" | custom-call | flops 3221225472 | bytes 11534336 | tf_op jit(solution)/shard_map/project/pallas_call | solution.py:537
  16.2 4.6 all-to-all-start
  42.1 5.0 all-to-all-start.1
  49.7 30.4 %attention_fwd.2 = (bf16[8,64,512]{2,1,0:T(8,128)(2,1)}, f32[8,1,512]{2,1,0:T(1,128)}) custom-call(s32[8]{0:T(128)} %and_select_fusion.nch_ref, f32[32]{0:T(128)} %get-tuple-element.519.tab_ref, s32[8,8192]{1,0:T(8,128)} %broadcast_in_dim.57.buck_ref, bf16[64,4096]{1,0:T(8,128)(2,1)} %maximum_maximum_fusion.kmask_ref, ...), custom_call_target="tpu_custom_call" | custom-call | flops 16777216000 | bytes 2097152 | tf_op jit(solution)/shard_map/attention_fwd/pallas_call | solution.py:96
  86.4 30.1 %attention_fwd.3 = (bf16[8,64,512]{2,1,0:T(8,128)(2,1)}, f32[8,1,512]{2,1,0:T(1,128)}) custom-call(s32[8]{0:T(128)} %and_select_fusion.nch_ref, f32[32]{0:T(128)} %get-tuple-element.518.tab_ref, s32[8,8192]{1,0:T(8,128)} %broadcast_in_dim.57.buck_ref, bf16[64,4096]{1,0:T(8,128)(2,1)} %maximum_maximum_fusion.kmask_ref, ...), custom_call_target="tpu_custom_call" | custom-call | flops 16777216000 | bytes 2097152 | tf_op jit(solution)/shard_map/attention_fwd/pallas_call | solution.py:96
  117.3 6.5 %collective-permute-done.2.refs_3_ = bf16[160,1024]{1,0:T(8,128)(2,1)S(1)} collective-permute-done((bf16[160,1024]{1,0:T(8,128)(2,1)S(1)}, bf16[160,1024]{1,0:T(8,128)(2,1)S(1)}, u32[]{:S(2)}, u32[]{:S(2)}) %collective-permute-start.2) | collective-permute-done | bytes 327712 | tf_op jit(solution)/shard_map/ppermute | solution.py:895
  129.3 6.2 %all-to-all-done.3 = bf16[8,64,512]{2,1,0:T(8,128)(2,1)S(1)} async-done(((bf16[8,64,512]{2,1,0:T(8,128)(2,1)}), bf16[8,64,512]{2,1,0:T(8,128)(2,1)S(1)}, u32[]{:S(2)}, u32[]{:S(2)}) %all-to-all-start.3) | async-done | bytes 524320 | tf_op jit(solution)/shard_map/all_to_all | solution.py:889
  136.4 7.9 %route.1 = (f32[512,1024]{1,0:T(8,128)}, bf16[512,1024]{1,0:T(8,128)(2,1)}, f32[512,4]{1,0:T(8,128)}, bf16[160,1152]{1,0:T(8,128)(2,1)}, bf16[160,1152]{1,0:T(8,...) custom-call(bf16[512,1024]{1,0:T(8,128)(2,1)} %x_ref.5, ...), custom_call_target="tpu_custom_call" | custom-call | flops 2415919104 | bytes 8388608 | tf_op jit(solution)/shard_map/route/pallas_call | solution.py:804
  149.0 6.5 %collective-permute-done.4.refs_2_.refs_10_.refs_6_ = bf16[160,1152]{1,0:T(8,128)(2,1)S(1)} collective-permute-done((bf16[160,1152]{1,0:T(8,128)(2,1)}, bf16[160,1152]{1,0:T(8,128)(2,1)S(1)}, u32[]{:S(2)}, u32[]{:S(2)}) %collective-permute-start.4) | collective-permute-done | bytes 368672 | tf_op jit(solution)/shard_map/ppermute | solution.py:895
  155.5 8.5 %collective-permute-done.5.refs_3_.refs_11_.refs_7_ = bf16[160,1152]{1,0:T(8,128)(2,1)S(1)} collective-permute-done((bf16[160,1152]{1,0:T(8,128)(2,1)}, bf16[160,1152]{1,0:T(8,128)(2,1)S(1)}, u32[]{:S(2)}, u32[]{:S(2)}) %collective-permute-start.5) | collective-permute-done | bytes 368672 | tf_op jit(solution)/shard_map/ppermute | solution.py:895
  165.9 21.5 %expert_fwd.2 = (bf16[2816,640]{1,0:T(8,128)(2,1)}, bf16[640,2816]{1,0:T(8,128)(2,1)}, bf16[640,2816]{1,0:T(8,128)(2,1)}, bf16[160,1024]{1,0:T(8,128)(2,1)}, bf1...) custom-call(bf16[1,1024,5632]{2,1,0:T(8,128)(2,1)} %wu_ref.7, ...), custom_call_target="tpu_custom_call" | custom-call | flops 18454937600 | bytes 30736384 | tf_op jit(solution)/shard_map/expert_fwd/pallas_call | solution.py:318
  187.5 5.9 %collective-permute-done.11.refs_7_.refs_3_ = bf16[160,1024]{1,0:T(8,128)(2,1)} collective-permute-done((bf16[160,1024]{1,0:T(8,128)(2,1)S(1)}, bf16[160,1024]{1,0:T(8,128)(2,1)}, u32[]{:S(2)}, u32[]{:S(2)}) %collective-permute-start.11) | collective-permute-done | bytes 327712 | tf_op jit(solution)/shard_map/ppermute | solution.py:895
  195.6 21.6 %expert_fwd.3 = (bf16[2816,640]{1,0:T(8,128)(2,1)}, bf16[640,2816]{1,0:T(8,128)(2,1)}, bf16[640,2816]{1,0:T(8,128)(2,1)}, bf16[160,1024]{1,0:T(8,128)(2,1)}, bf1...) custom-call(bf16[1,1024,5632]{2,1,0:T(8,128)(2,1)} %wu_ref.7, ...), custom_call_target="tpu_custom_call" | custom-call | flops 18454937600 | bytes 30736384 | tf_op jit(solution)/shard_map/expert_fwd/pallas_call | solution.py:318
  219.5 9.6 %down_grad.2 = (bf16[4,1536,128]{2,1,0:T(8,128)(2,1)}, bf16[4,1536,128]{2,1,0:T(8,128)(2,1)}) custom-call(s32[1]{0:T(128)} %bitcast.14.ctx_ref, bf16[160,1024]{1,0:T(8,128)(2,1)} %convolution_convert_fusion.7.refs_0_, bf16[160,1024]{1,0:T(8,128)(2,1)} %copy-done.51, bf16[160,1024]{1,0:T(8,128)(2,1)} %copy-done.52, bf16[160,1024]{1,0:T(8,128)(2,1)} %copy-done.53, ...), custom_call_target="tpu_custom_call" | custom-call | flops 8053063680 | bytes 9699328 | tf_op jit(solution)/shard_map/down_grad/pallas_call | solution.py:496
  229.9 8.6 %down_grad.3 = (bf16[4,1280,128]{2,1,0:T(8,128)(2,1)}, bf16[4,1280,128]{2,1,0:T(8,128)(2,1)}) custom-call(s32[1]{0:T(128)} %bitcast.14.ctx_ref, bf16[160,1024]{1,0:T(8,128)(2,1)} %convolution_convert_fusion.7.refs_0_, bf16[160,1024]{1,0:T(8,128)(2,1)} %copy-done.51, bf16[160,1024]{1,0:T(8,128)(2,1)} %copy-done.52, bf16[160,1024]{1,0:T(8,128)(2,1)} %copy-done.53, ...), custom_call_target="tpu_custom_call" | custom-call | flops 6710886400 | bytes 8519680 | tf_op jit(solution)/shard_map/down_grad/pallas_call | solution.py:496
  238.6 25.5 %expert_bwd.2 = (bf16[2,640,2816]{2,1,0:T(8,128)(2,1)}, bf16[160,1024]{1,0:T(8,128)(2,1)}, bf16[160,1024]{1,0:T(8,128)(2,1)}, bf16[160,1024]{1,0:T(8,128)(2,1)}, bf16[160,1024]{1,0:T(8,128)(2,1)}) custom-call(bf16[640,2816]{1,0:T(8,128)(2,1)} %get-tuple-element.298.act_ref, bf16[640,2816]{1,0:T(8,128)(2,1)} %get-tuple-element.299.slope_ref, ...), custom_call_target="tpu_custom_call" | custom-call | flops 18454937600 | bytes 34340864 | tf_op jit(solution)/shard_map/expert_bwd/pallas_call | solution.py:373
  270.4 25.9 %expert_bwd.3 = (bf16[2,640,2816]{2,1,0:T(8,128)(2,1)}, bf16[160,1024]{1,0:T(8,128)(2,1)}, bf16[160,1024]{1,0:T(8,128)(2,1)}, bf16[160,1024]{1,0:T(8,128)(2,1)}, bf16[160,1024]{1,0:T(8,128)(2,1)}) custom-call(bf16[640,2816]{1,0:T(8,128)(2,1)} %get-tuple-element.318.act_ref, bf16[640,2816]{1,0:T(8,128)(2,1)} %get-tuple-element.319.slope_ref, ...), custom_call_target="tpu_custom_call" | custom-call | flops 18454937600 | bytes 34340864 | tf_op jit(solution)/shard_map/expert_bwd/pallas_call | solution.py:373
  301.7 5.3 turn.1.refs_0_.refs_1_.refs_2_.refs_3_
  309.6 5.7 %in_grad.4 = (bf16[512,768]{1,0:T(8,128)(2,1)}, bf16[512,768]{1,0:T(8,128)(2,1)}) custom-call(bf16[1024,1280]{1,0:T(8,128)(2,1)} %turn.1.refs_0_.refs_1_.refs_2_.refs_3_, bf16[1024,1280]{1,0:T(8,128)(2,1)} %turn.1.refs_0_.refs_1_.refs_2_.refs_3_, bf16[1024,1280]{1,0:T(8,128)(2,1)} %turn.1.refs_0_.refs_1_.refs_2_.refs_3_, ...), custom_call_target="tpu_custom_call" | custom-call | flops 4026531840 | bytes 6160384 | tf_op jit(solution)/shard_map/in_grad/pallas_call | solution.py:450
  316.1 5.6 in_grad.5
  321.6 10.7 %in_grad.6 = (bf16[512,2048]{1,0:T(8,128)(2,1)}, bf16[512,2048]{1,0:T(8,128)(2,1)}) custom-call(bf16[1024,1280]{1,0:T(8,128)(2,1)} %turn.1.refs_0_.refs_1_.refs_2_.refs_3_, bf16[1024,1280]{1,0:T(8,128)(2,1)} %turn.1.refs_0_.refs_1_.refs_2_.refs_3_, bf16[1024,1280]{1,0:T(8,128)(2,1)} %turn.1.refs_0_.refs_1_.refs_2_.refs_3_, ...), custom_call_target="tpu_custom_call" | custom-call | flops 10737418240 | bytes 12058624 | tf_op jit(solution)/shard_map/in_grad/pallas_call | solution.py:450
  337.5 15.4 %combine.1 = (bf16[512,1024]{1,0:T(8,128)(2,1)}, f32[512,1024]{1,0:T(8,128)}, bf16[8,64,512]{2,1,0:T(8,128)(2,1)}, bf16[8,64,512]{2,1,0:T(8,128)(2,1)}, bf16[256...) custom-call(s32[1]{0:T(128)} %bitcast.exp_ref, ...), custom_call_target="tpu_custom_call" | custom-call | flops 6174015488 | bytes 18874368 | tf_op jit(solution)/shard_map/combine/pallas_call | solution.py:705
  354.9 5.2 all-to-all-start.4
  360.1 10.8 %in_grad.7 = (bf16[512,2048]{1,0:T(8,128)(2,1)}, bf16[512,2048]{1,0:T(8,128)(2,1)}) custom-call(bf16[1024,1280]{1,0:T(8,128)(2,1)} %turn.1.refs_0_.refs_1_.refs_2_.refs_3_, bf16[1024,1280]{1,0:T(8,128)(2,1)} %turn.1.refs_0_.refs_1_.refs_2_.refs_3_, bf16[1024,1280]{1,0:T(8,128)(2,1)} %turn.1.refs_0_.refs_1_.refs_2_.refs_3_, ...), custom_call_target="tpu_custom_call" | custom-call | flops 10737418240 | bytes 12058624 | tf_op jit(solution)/shard_map/in_grad/pallas_call | solution.py:450
  380.6 46.8 %attention_bwd.2 = (bf16[8,3,64,512]{3,2,1,0:T(8,128)(2,1)}, f32[32,128]{1,0:T(8,128)}) custom-call(s32[8]{0:T(128)} %and_select_fusion.nch_ref, f32[32]{0:T(128)} %get-tuple-element.519.tab_ref, s32[8,8192]{1,0:T(8,128)} %broadcast_in_dim.58.buck_ref, bf16[64,4096]{1,0:T(8,128)(2,1)} %maximum_maximum_fusion.kmask_ref, ...), custom_call_target="tpu_custom_call" | custom-call | flops 41943040000 | bytes 4194304 | tf_op jit(solution)/shard_map/attention_bwd/pallas_call | solution.py:220
  434.9 5.2 all-to-all-start.6
  440.4 4.5 add_convert_fusion
  446.3 46.8 %attention_bwd.3 = (bf16[8,3,64,512]{3,2,1,0:T(8,128)(2,1)}, f32[32,128]{1,0:T(8,128)}) custom-call(s32[8]{0:T(128)} %and_select_fusion.nch_ref, f32[32]{0:T(128)} %get-tuple-element.518.tab_ref, s32[8,8192]{1,0:T(8,128)} %broadcast_in_dim.58.buck_ref, bf16[64,4096]{1,0:T(8,128)(2,1)} %maximum_maximum_fusion.kmask_ref, ...), custom_call_target="tpu_custom_call" | custom-call | flops 41943040000 | bytes 4194304 | tf_op jit(solution)/shard_map/attention_bwd/pallas_call | solution.py:220
  500.7 11.3 %sequence_grad.1 = (bf16[256,512]{1,0:T(8,128)(2,1)}, bf16[256,512]{1,0:T(8,128)(2,1)}, bf16[256,512]{1,0:T(8,128)(2,1)}, bf16[256,512]{1,0:T(8,128)(2,1)}) custom-call(s32[1]{0:T(128)} %bitcast.15.dp_ref, bf16[8,3,64,512]{3,2,1,0:T(8,128)(2,1)} %get-tuple-element.426.refs_0_, bf16[8,3,64,512]{3,2,1,0:T(8,128)(2,1)} %get-tuple-element.438.refs_1_, ...), custom_call_target="tpu_custom_call" | custom-call | flops 3221225472 | bytes 11534336 | tf_op jit(solution)/shard_map/sequence_grad/pallas_call | solution.py:862
  521.1 11.1 %input_grad.1 = f32[512,1024]{1,0:T(8,128)} custom-call(bf16[512,1024]{1,0:T(8,128)(2,1)} %x_ref.5, f32[1,1024]{1,0:T(1,128)} %bitcast.69, f32[512,1024]{1,0:T(8,128)} %get-tuple-element.444.mid_ref, bf16[1024,3072]{1,0:T(8,128)(2,1)} %refs_3_.3, bf16[1024,3072]{1,0:T(8,128)(2,1)} %refs_3_.3, bf16[1024,3072]{1,0:T(8,128)(2,1)} %refs_3_.3, ...), custom_call_target="tpu_custom_call" | custom-call | flops 3221225472 | bytes 14680064 | tf_op jit(solution)/shard_map/input_grad/pallas_call | solution.py:586
  532.3 7.9 %collective-permute-done.38 = bf16[256,512]{1,0:T(8,128)(2,1)} collective-permute-done((bf16[256,512]{1,0:T(8,128)(2,1)}, bf16[256,512]{1,0:T(8,128)(2,1)}, u32[]{:S(2)}, u32[]{:S(2)}) %collective-permute-start.38) | collective-permute-done | bytes 262176 | tf_op jit(solution)/shard_map/ppermute | solution.py:895
  542.2 4.5 all-to-all-start.8
  (308 shorter events, 121.0 us)
Async XLA Ops:
  20.8 196.5 %all-gather.3.cloned.1.call-start = ((), (), s32[]{:S(2)}) async-start(), calls=%async_computation.21 | async-start | bytes 9437184 | tf_op jit(solution)/shard_map/all_gather | solution.py:1025
  42.1 38.0 %all-to-all-start.1 = ((bf16[8,3,64,512]{3,2,1,0:T(8,128)(2,1)}), bf16[8,3,64,512]{3,2,1,0:T(8,128)(2,1)}, u32[]{:S(2)}, u32[]{:S(2)}) async-start(bf16[8,3,64,512]{3,2,1,0:T(8,128)(2,1)} %get-tuple-element.249), calls=%async_computation.1 | async-start | bytes 3145728 | tf_op jit(solution)/shard_map/all_to_all | solution.py:889
  80.1 43.8 %all-to-all-start.2 = ((bf16[8,64,512]{2,1,0:T(8,128)(2,1)}), bf16[8,64,512]{2,1,0:T(8,128)(2,1)S(1)}, u32[]{:S(2)}, u32[]{:S(2)}) async-start(bf16[8,64,512]{2,1,0:T(8,128)(2,1)} %get-tuple-element.250.o_ref), calls=%async_computation.2 | async-start | bytes 1048576 | tf_op jit(solution)/shard_map/all_to_all | solution.py:889
  84.3 32.3 %collective-permute-start = (bf16[160,1024]{1,0:T(8,128)(2,1)S(1)}, bf16[160,1024]{1,0:T(8,128)(2,1)S(1)}, u32[]{:S(2)}, u32[]{:S(2)}) collective-permute-start(bf16[160,1024]{1,0:T(8,128)(2,1)S(1)} %copy-done.33), channel_id=1, source_target_pairs={{0,1},{1,0},{2,3},{3,2},{4,5},{5,4},{6,7},{7,6},{8,9},{9,8},{10,11... | collective-permute-start | bytes 983048 | tf_op jit(solution)/shard_map/ppermute | solution.py:895
  84.3 32.2 %collective-permute-start.1 = (bf16[160,1024]{1,0:T(8,128)(2,1)S(1)}, bf16[160,1024]{1,0:T(8,128)(2,1)S(1)}, u32[]{:S(2)}, u32[]{:S(2)}) collective-permute-start(bf16[160,1024]{1,0:T(8,128)(2,1)S(1)} %copy-done.32), channel_id=1, source_target_pairs={{0,2},{1,3},{2,0},{3,1},{4,6},{5,7},{6,4},{7,5},{8,10},{9,11},{10,... | collective-permute-start | bytes 983048 | tf_op jit(solution)/shard_map/ppermute | solution.py:895
  86.0 37.9 %collective-permute-start.2 = (bf16[160,1024]{1,0:T(8,128)(2,1)S(1)}, bf16[160,1024]{1,0:T(8,128)(2,1)S(1)}, u32[]{:S(2)}, u32[]{:S(2)}) collective-permute-start(bf16[160,1024]{1,0:T(8,128)(2,1)S(1)} %copy-done.31), channel_id=1, source_target_pairs={{0,3},{1,2},{2,1},{3,0},{4,7},{5,6},{6,5},{7,4},{8,11},{9,10},{10,... | collective-permute-start | bytes 983048 | tf_op jit(solution)/shard_map/ppermute | solution.py:895
  127.4 227.6 %reduce-scatter.7.cloned.1.call-start = ((), (), s32[]{:S(2)}) async-start(), calls=%async_computation.15 | async-start | bytes 1966080 | tf_op jit(solution)/shard_map/reduce_scatter | solution.py:1055
  147.0 40.5 %collective-permute-start.7 = (bf16[160,1152]{1,0:T(8,128)(2,1)}, bf16[160,1152]{1,0:T(8,128)(2,1)S(1)}, u32[]{:S(2)}, u32[]{:S(2)}) collective-permute-start(bf16[160,1152]{1,0:T(8,128)(2,1)} %get-tuple-element.283), channel_id=1, source_target_pairs={{0,2},{1,3},{2,0},{3,1},{4,6},{5,7},{6,4},{7,5},{8,10},{9,11},{10,... | collective-permute-start | bytes 1105928 | tf_op jit(solution)/shard_map/ppermute | solution.py:895
  147.6 39.9 %collective-permute-start.8 = (bf16[160,1152]{1,0:T(8,128)(2,1)}, bf16[160,1152]{1,0:T(8,128)(2,1)S(1)}, u32[]{:S(2)}, u32[]{:S(2)}) collective-permute-start(bf16[160,1152]{1,0:T(8,128)(2,1)} %get-tuple-element.284), channel_id=1, source_target_pairs={{0,3},{1,2},{2,1},{3,0},{4,7},{5,6},{6,5},{7,4},{8,11},{9,10},{10,... | collective-permute-start | bytes 1105928 | tf_op jit(solution)/shard_map/ppermute | solution.py:895
  164.6 28.9 %collective-permute-start.11 = (bf16[160,1024]{1,0:T(8,128)(2,1)S(1)}, bf16[160,1024]{1,0:T(8,128)(2,1)}, u32[]{:S(2)}, u32[]{:S(2)}) collective-permute-start(bf16[160,1024]{1,0:T(8,128)(2,1)S(1)} %copy-done.28), channel_id=1, source_target_pairs={{0,3},{1,2},{2,1},{3,0},{4,7},{5,6},{6,5},{7,4},{8,11},{9,10},{10,... | collective-permute-start | bytes 983048 | tf_op jit(solution)/shard_map/ppermute | solution.py:895
  217.3 46.8 %collective-permute-start.15 = (bf16[160,1024]{1,0:T(8,128)(2,1)}, bf16[160,1024]{1,0:T(8,128)(2,1)S(1)}, u32[]{:S(2)}, u32[]{:S(2)}) collective-permute-start(bf16[160,1024]{1,0:T(8,128)(2,1)} %get-tuple-element.314), channel_id=1, source_target_pairs={{0,1},{1,0},{2,3},{3,2},{4,5},{5,4},{6,7},{7,6},{8,9},{9,8},{10,11... | collective-permute-start | bytes 983048 | tf_op jit(solution)/shard_map/ppermute | solution.py:895
  217.4 46.7 %collective-permute-start.16 = (bf16[160,1024]{1,0:T(8,128)(2,1)}, bf16[160,1024]{1,0:T(8,128)(2,1)S(1)}, u32[]{:S(2)}, u32[]{:S(2)}) collective-permute-start(bf16[160,1024]{1,0:T(8,128)(2,1)} %get-tuple-element.315), channel_id=1, source_target_pairs={{0,2},{1,3},{2,0},{3,1},{4,6},{5,7},{6,4},{7,5},{8,10},{9,11},{10,... | collective-permute-start | bytes 983048 | tf_op jit(solution)/shard_map/ppermute | solution.py:895
  218.0 46.1 %collective-permute-start.17 = (bf16[160,1024]{1,0:T(8,128)(2,1)}, bf16[160,1024]{1,0:T(8,128)(2,1)}, u32[]{:S(2)}, u32[]{:S(2)}) collective-permute-start(bf16[160,1024]{1,0:T(8,128)(2,1)} %get-tuple-element.316), channel_id=1, source_target_pairs={{0,3},{1,2},{2,1},{3,0},{4,7},{5,6},{6,5},{7,4},{8,11},{9,10},{10,... | collective-permute-start | bytes 983048 | tf_op jit(solution)/shard_map/ppermute | solution.py:895
  229.1 36.4 %collective-permute-start.18 = (bf16[4,1536,128]{2,1,0:T(8,128)(2,1)}, bf16[4,1536,128]{2,1,0:T(8,128)(2,1)S(1)}, u32[]{:S(2)}, u32[]{:S(2)}) collective-permute-start(bf16[4,1536,128]{2,1,0:T(8,128)(2,1)} %get-tuple-element.329), channel_id=1, source_target_pairs={{0,4},{4,0},{1,5},{5,1},{2,6},{6,2},{3,7},{7,3},{8,12},{12,8},{9,1... | collective-permute-start | bytes 4718600 | tf_op jit(solution)/shard_map/ppermute | solution.py:1058
  267.2 160.3 %reduce-scatter.13.cloned.1.call-start = ((), (), s32[]{:S(2)}) async-start(), calls=%async_computation.18 | async-start | bytes 1638400 | tf_op jit(solution)/shard_map/reduce_scatter | solution.py:1055
  267.2 29.1 %collective-permute-start.19 = (bf16[160,1024]{1,0:T(8,128)(2,1)}, bf16[160,1024]{1,0:T(8,128)(2,1)S(1)}, u32[]{:S(2)}, u32[]{:S(2)}) collective-permute-start(bf16[160,1024]{1,0:T(8,128)(2,1)} %get-tuple-element.355), channel_id=1, source_target_pairs={{0,1},{1,0},{2,3},{3,2},{4,5},{5,4},{6,7},{7,6},{8,9},{9,8},{10,11... | collective-permute-start | bytes 983048 | tf_op jit(solution)/shard_map/ppermute | solution.py:895
  267.9 28.4 %collective-permute-start.20 = (bf16[160,1024]{1,0:T(8,128)(2,1)}, bf16[160,1024]{1,0:T(8,128)(2,1)S(1)}, u32[]{:S(2)}, u32[]{:S(2)}) collective-permute-start(bf16[160,1024]{1,0:T(8,128)(2,1)} %get-tuple-element.356), channel_id=1, source_target_pairs={{0,2},{1,3},{2,0},{3,1},{4,6},{5,7},{6,4},{7,5},{8,10},{9,11},{10,... | collective-permute-start | bytes 983048 | tf_op jit(solution)/shard_map/ppermute | solution.py:895
  269.6 30.5 %collective-permute-start.22 = (bf16[4,1280,128]{2,1,0:T(8,128)(2,1)}, bf16[4,1280,128]{2,1,0:T(8,128)(2,1)S(1)}, u32[]{:S(2)}, u32[]{:S(2)}) collective-permute-start(bf16[4,1280,128]{2,1,0:T(8,128)(2,1)} %get-tuple-element.373), channel_id=1, source_target_pairs={{0,4},{4,0},{1,5},{5,1},{2,6},{6,2},{3,7},{7,3},{8,12},{12,8},{9,1... | collective-permute-start | bytes 3932168 | tf_op jit(solution)/shard_map/ppermute | solution.py:1058
  301.7 128.1 %reduce-scatter.11.cloned.1.call-start = ((), (), s32[]{:S(2)}) async-start(), calls=%async_computation.17 | async-start | bytes 2621440 | tf_op jit(solution)/shard_map/reduce_scatter | solution.py:1055
  334.6 95.2 %reduce-scatter.9.cloned.1.call-start = ((), (), s32[]{:S(2)}) async-start(), calls=%async_computation.16 | async-start | bytes 2621440 | tf_op jit(solution)/shard_map/reduce_scatter | solution.py:1055
  360.1 133.0 %reduce-scatter.15.cloned.1.call-start = ((), (), s32[]{:S(2)}) async-start(), calls=%async_computation.19 | async-start | bytes 1966080 | tf_op jit(solution)/shard_map/reduce_scatter | solution.py:1055
  372.5 54.9 %all-to-all-start.5 = ((bf16[8,64,512]{2,1,0:T(8,128)(2,1)}), bf16[8,64,512]{2,1,0:T(8,128)(2,1)}, u32[]{:S(2)}, u32[]{:S(2)}) async-start(bf16[8,64,512]{2,1,0:T(8,128)(2,1)} %get-tuple-element.407), calls=%async_computation.9 | async-start | bytes 1048576 | tf_op jit(solution)/shard_map/all_to_all | solution.py:889
  377.0 50.5 %collective-permute-start.29 = (bf16[256,1152]{1,0:T(8,128)(2,1)}, bf16[256,1152]{1,0:T(8,128)(2,1)S(1)}, u32[]{:S(2)}, u32[]{:S(2)}) collective-permute-start(bf16[256,1152]{1,0:T(8,128)(2,1)} %get-tuple-element.421), channel_id=1, source_target_pairs={{0,1},{1,0},{2,3},{3,2},{4,5},{5,4},{6,7},{7,6},{8,9},{9,8},{10,11... | collective-permute-start | bytes 1769480 | tf_op jit(solution)/shard_map/ppermute | solution.py:895
  377.1 50.4 %collective-permute-start.30 = (bf16[256,1152]{1,0:T(8,128)(2,1)}, bf16[256,1152]{1,0:T(8,128)(2,1)}, u32[]{:S(2)}, u32[]{:S(2)}) collective-permute-start(bf16[256,1152]{1,0:T(8,128)(2,1)} %get-tuple-element.422), channel_id=1, source_target_pairs={{0,2},{1,3},{2,0},{3,1},{4,6},{5,7},{6,4},{7,5},{8,10},{9,11},{10,... | collective-permute-start | bytes 1769480 | tf_op jit(solution)/shard_map/ppermute | solution.py:895
  378.8 48.7 %collective-permute-start.31 = (bf16[256,1152]{1,0:T(8,128)(2,1)}, bf16[256,1152]{1,0:T(8,128)(2,1)}, u32[]{:S(2)}, u32[]{:S(2)}) collective-permute-start(bf16[256,1152]{1,0:T(8,128)(2,1)} %get-tuple-element.423), channel_id=1, source_target_pairs={{0,3},{1,2},{2,1},{3,0},{4,7},{5,6},{6,5},{7,4},{8,11},{9,10},{10,... | collective-permute-start | bytes 1769480 | tf_op jit(solution)/shard_map/ppermute | solution.py:895
  379.2 50.6 %collective-permute-start.28 = (bf16[512,2048]{1,0:T(8,128)(2,1)}, bf16[512,2048]{1,0:T(8,128)(2,1)S(1)}, u32[]{:S(2)}, u32[]{:S(2)}) collective-permute-start(bf16[512,2048]{1,0:T(8,128)(2,1)} %get-tuple-element.419), channel_id=1, source_target_pairs={{0,4},{4,0},{1,5},{5,1},{2,6},{6,2},{3,7},{7,3},{8,12},{12,8},{9,1... | collective-permute-start | bytes 6291464 | tf_op jit(solution)/shard_map/ppermute | solution.py:1058
  432.2 60.8 %collective-permute-start.33 = (bf16[64,1152]{1,0:T(8,128)(2,1)S(1)}, bf16[64,1152]{1,0:T(8,128)(2,1)S(1)}, u32[]{:S(2)}, u32[]{:S(2)}) collective-permute-start(bf16[64,1152]{1,0:T(8,128)(2,1)S(1)} %get-tuple-element.516), channel_id=1, source_target_pairs={{0,8},{8,0},{16,24},{24,16},{1,9},{9,1},{17,25},{25,17},{2,10},{10... | collective-permute-start | bytes 442376 | tf_op jit(solution)/shard_map/ppermute | solution.py:895
  432.6 60.5 %collective-permute-start.34 = (bf16[64,1152]{1,0:T(8,128)(2,1)S(1)}, bf16[64,1152]{1,0:T(8,128)(2,1)S(1)}, u32[]{:S(2)}, u32[]{:S(2)}) collective-permute-start(bf16[64,1152]{1,0:T(8,128)(2,1)S(1)} %get-tuple-element.515), channel_id=1, source_target_pairs={{0,16},{8,24},{16,0},{24,8},{1,17},{9,25},{17,1},{25,9},{2,18},{10... | collective-permute-start | bytes 442376 | tf_op jit(solution)/shard_map/ppermute | solution.py:895
  434.7 58.4 %collective-permute-start.35 = (bf16[64,1152]{1,0:T(8,128)(2,1)S(1)}, bf16[64,1152]{1,0:T(8,128)(2,1)S(1)}, u32[]{:S(2)}, u32[]{:S(2)}) collective-permute-start(bf16[64,1152]{1,0:T(8,128)(2,1)S(1)} %get-tuple-element.514), channel_id=1, source_target_pairs={{0,24},{8,16},{16,8},{24,0},{1,25},{9,17},{17,9},{25,1},{2,26},{10... | collective-permute-start | bytes 442376 | tf_op jit(solution)/shard_map/ppermute | solution.py:895
  434.9 58.2 %all-to-all-start.6 = ((bf16[8,3,64,512]{3,2,1,0:T(8,128)(2,1)}), bf16[8,3,64,512]{3,2,1,0:T(8,128)(2,1)S(1)}, u32[]{:S(2)}, u32[]{:S(2)}) async-start(bf16[8,3,64,512]{3,2,1,0:T(8,128)(2,1)} %get-tuple-element.426.refs_0_), calls=%async_computation.10 | async-start | bytes 3145728 | tf_op jit(solution)/shard_map/all_to_all | solution.py:889
  440.1 106.5 %reduce-scatter.17.cloned.1.call-start = ((), (), s32[]{:S(2)}) async-start(), calls=%async_computation.20 | async-start | bytes 2621440 | tf_op jit(solution)/shard_map/reduce_scatter | solution.py:1055
  444.9 48.3 %collective-permute-start.32 = (bf16[128,2048]{1,0:T(8,128)(2,1)}, bf16[128,2048]{1,0:T(8,128)(2,1)S(1)}, u32[]{:S(2)}, u32[]{:S(2)}) collective-permute-start(bf16[128,2048]{1,0:T(8,128)(2,1)} %reduce-scatter.11.cloned.1.call-done), channel_id=1, source_target_pairs={{0,4},{4,0},{1,5},{5,1},{2,6},{6,2},{3,7},{7,3},{8,12},{12,8},{9,1... | collective-permute-start | bytes 1572872 | tf_op jit(solution)/shard_map/ppermute | solution.py:1058
  (88 other events, 1374.8 us)
Sparse Core Ops, SparseCore 0:
  42.2 87.8 all-gather.2
  267.3 33.1 reduce-scatter.6
  303.3 30.0 reduce-scatter.12
  335.6 42.2 reduce-scatter.10
  380.1 43.2 reduce-scatter.8
  425.5 48.6 reduce-scatter.14
  477.1 40.4 reduce-scatter.16
